TPU v7x, 256 devices: a whole 4x4x8 slice. The times are simulated.
256 devices in a mesh: stn: 64 (over z, y_hi, x), chan: 4 (over y_lo, core).
Axes of the slice: x: 4, y: 4 (y_hi: 2, y_lo: 2; y = y_hi * 2 + y_lo), z: 8, core: 2. Of those that a mesh axis runs over, the one named last changes fastest.
Arguments:
- samples: bfloat16 [512, 17, 2, 8192], P(('stn', 'chan')), may hold values from -6 to 6
- keeper: int32 [64, 64], replicated, may hold values from 0 to 1, as said below
Outputs:
- visibilities: bfloat16 [512, 2, 4096, 264], P('stn', None, 'chan')
Inputs may be any that keep to these rules, and one draw needn't show every extreme that they name: keeper[g, g] is 1; for g != h with d = (g - h) mod 64: keeper[g, h] is 1 where 0 < d < 32, 0 where d > 32, and at d = 32 exactly one of keeper[g, h] and keeper[h, g] is 1, which one drawn for each such pair; half of the rows hold 33 ones, the others 33 - 1.
All inputs are finite; a program needn't handle non-finite values.
Results may differ from a plain program's by a relative error of at most 0.0077.
Values may be sent and summed in bfloat16 or wider, within the bound.
No kernel may reach another device: no remote copies, remote signals or barrier semaphores. Data moves between devices by JAX's collectives and lax.ppermute only.
A program may use at most 192 MiB of HBM per device.

v0:
```python
import math

import jax
import jax.numpy as jnp
from jax import lax
from jax.sharding import PartitionSpec as P

NFFT = 8192
TAPS = 16
CH_WIN = 1024
DFT_BLOCK = 256


def taps_table():
    pos = jnp.arange(TAPS * NFFT).astype(jnp.float32)
    shifted = (pos + 0.5) / NFFT - TAPS / 2.0
    window = 0.5 - 0.5 * jnp.cos(2.0 * math.pi * (pos + 0.5) / (TAPS * NFFT))
    return (jnp.sinc(shifted) * window).reshape(TAPS, NFFT)


def twiddles(width):
    index_n = jnp.arange(NFFT, dtype=jnp.int32)[:, None]
    index_k = jnp.arange(width, dtype=jnp.int32)[None, :]
    phase = (index_n * index_k % NFFT).astype(jnp.float32) * (2.0 * math.pi / NFFT)
    cosines = jnp.cos(phase).astype(jnp.bfloat16)
    sines = jnp.sin(phase).astype(jnp.bfloat16)
    upper = jnp.concatenate([cosines, -sines], axis=1)
    lower = jnp.concatenate([sines, cosines], axis=1)
    return jnp.concatenate([upper, lower], axis=0)


def rotations(ch_tot, width):
    blocks = ch_tot // width
    index_n = jnp.arange(NFFT, dtype=jnp.int32)[None, :]
    index_b = jnp.arange(blocks, dtype=jnp.int32)[:, None]
    phase = (index_n * index_b * width % NFFT).astype(jnp.float32) * (2.0 * math.pi / NFFT)
    return (jnp.cos(phase), jnp.sin(phase))


def channelise(block, taps, table, cos_rot, sin_rot, ch_tot):
    frames = block.shape[1] - TAPS + 1
    count = block.shape[0]
    width = table.shape[1] // 2
    blocks = ch_tot // width
    total = taps[0] * block[:, 0:frames].astype(jnp.float32)
    for tap in range(1, TAPS):
        total = total + taps[tap] * block[:, tap : tap + frames].astype(jnp.float32)
    real_part = total[:, :, 0][None]
    imag_part = total[:, :, 1][None]
    cosine = cos_rot[:, None, None, :]
    sine = sin_rot[:, None, None, :]
    rot_real = real_part * cosine + imag_part * sine
    rot_imag = imag_part * cosine - real_part * sine
    lhs = jnp.stack([rot_real, rot_imag], axis=3).astype(jnp.bfloat16)
    lhs = lhs.reshape(blocks * count * frames, 2 * NFFT)
    spectrum = jnp.dot(lhs, table, preferred_element_type=jnp.float32) * (1.0 / math.sqrt(NFFT))
    spectrum = spectrum.astype(jnp.bfloat16).reshape(blocks, count, frames, 2, width)
    spectrum = jnp.transpose(spectrum, (1, 0, 4, 3, 2))
    return spectrum.reshape(count, ch_tot, 2, frames)


def correlate(own, others, frames):
    half = others.shape[2] // 2
    turned = jnp.concatenate([-others[:, :, half:], others[:, :, :half]], axis=2)
    rhs = jnp.concatenate([others, turned], axis=0)
    product = lax.dot_general(
        own, rhs, (((2,), (2,)), ((1,), (1,))), preferred_element_type=jnp.float32
    )
    rows = others.shape[0]
    product = product.reshape(product.shape[0], product.shape[1], 2, rows)
    return jnp.transpose(product, (1, 2, 0, 3)) / frames


def slot_table(keep_rows, keep_slots):
    ranking = jnp.cumsum(keep_rows, axis=1) - 1
    slot_index = jnp.arange(keep_slots, dtype=jnp.int32)
    matched = (keep_rows[:, :, None] == 1) & (ranking[:, :, None] == slot_index[None, None, :])
    column_ids = jnp.arange(keep_rows.shape[1], dtype=jnp.int32)
    slot_column = jnp.sum(jnp.where(matched, column_ids[None, :, None], 0), axis=1)
    filled = jnp.any(matched, axis=1)
    return (slot_column, filled)


def per_device(samples, keeper):
    n_chan = lax.axis_size("chan")
    n_stn = lax.axis_size("stn")
    ch_tot = CH_WIN * n_chan
    frames = samples.shape[1] - TAPS + 1
    cos_rot, sin_rot = rotations(ch_tot, DFT_BLOCK)
    spectrum = channelise(samples, taps_table(), twiddles(DFT_BLOCK), cos_rot, sin_rot, ch_tot)
    local = lax.all_to_all(spectrum, "chan", split_axis=1, concat_axis=0, tiled=True)
    group_in = local.shape[0]
    own = local.reshape(group_in, CH_WIN, 2 * frames)
    keep_slots = n_stn // 2 + 1
    group_index = lax.axis_index("stn")
    row_keep = jnp.take(keeper, group_index, axis=0)
    slot_column, filled = slot_table(row_keep[None], keep_slots)
    slot_column = slot_column[0]
    filled = filled[0]
    nothing = jnp.zeros((), jnp.bfloat16)
    col_mask = jnp.repeat(row_keep, group_in).astype(jnp.float32)
    tile = correlate(own, lax.all_gather(own, "stn", axis=0, tiled=True), frames)
    whole = (tile * col_mask[None, None, None, :]).astype(jnp.bfloat16)
    whole = whole.reshape(group_in, 2, CH_WIN, n_stn, group_in)
    picked = jnp.take(whole, slot_column, axis=3)
    picked = jnp.where(filled[None, None, None, :, None], picked, nothing)
    return picked.reshape(group_in, 2, CH_WIN, keep_slots * group_in)


def solution(mesh):
    placed = (P(("stn", "chan"), None, None, None), P())
    return jax.shard_map(
        per_device,
        mesh=mesh,
        in_specs=placed,
        out_specs=P("stn", None, "chan", None),
        check_vma=False,
    )
```

profile of v0, /device:TPU:16, one launch (start us, length us, event | category | flops | bytes accessed | tf_op | source)
XLA Modules:
  0.0 383.9 jit_solution(5526646558050877336)
XLA Ops:
  6.5 2.4 fusion.33
  8.9 2.1 fusion.45
  11.0 35.0 %sine_convert_fusion = (bf16[8192,256]{1,0:T(8,128)(2,1)}, bf16[8192,256]{1,0:T(8,128)(2,1)}) fusion(), kind=kLoop, calls=%fused_computation.25 | loop fusion | flops 33554432 | bytes 8388608 | tf_op jit(solution)/shard_map/convert_element_type | solution.py:26
  46.0 32.4 %fusion.22 = bf16[8192,256]{1,0:T(8,128)(2,1)} fusion(), kind=kLoop, calls=%fused_computation.34 | loop fusion | flops 37748736 | bytes 4194304 | tf_op jit(solution)/shard_map/neg | solution.py:27
  78.4 2.1 multiply_add_fusion.1
  80.6 0.2 fusion.52
  80.8 0.2 copy_bitcast_fusion
  81.0 4.4 %add_convert_fusion = (bf16[16,2,2,1,8192]{4,3,2,1,0:T(2,128)(2,1)S(1)}, bf16[16,2,2,1,8192]{4,3,2,1,0:T(2,128)(2,1)S(1)}) fusion(f32[16,8192]{1,0:T(8,128)S(1)} %get-tuple-element.42, f32[2,2,8192]{2,1,0:T(2,128)S(1)} %get-tuple-element.40, f32[16,8192]{1,0:T(8,128)S(1)} %get-tuple-element.43, f32[2,2,8192]{2,1,0:T(2,128)S(1)} %get-tuple-element.41), kind=kLoop, calls=%fused_computation.33 | loop fusion | flops 4194304 | bytes 3407872 | tf_op jit(solution)/shard_map/convert
  85.4 4.8 %pad_maximum_fusion = bf16[16,2,2,2,8192]{4,3,2,1,0:T(2,128)(2,1)S(1)} fusion(bf16[16,2,2,1,8192]{4,3,2,1,0:T(2,128)(2,1)S(1)} %get-tuple-element.21, bf16[16,2,2,1,8192]{4,3,2,1,0:T(2,128)(2,1)S(1)} %get-tuple-element.20), kind=kLoop, calls=%fused_computation.31 | loop fusion | flops 4194304 | bytes 4194304 | tf_op jit(solution)/shard_map/stack | solution.py:54
  90.2 1.2 copy.51
  91.4 13.7 %fusion.26 = bf16[64,512]{1,0:T(8,128)(2,1)S(1)} fusion(bf16[64,16384]{1,0:T(8,128)(2,1)S(1)} %bitcast.44, bf16[8192,256]{1,0:T(8,128)(2,1)} %get-tuple-element.45, bf16[8192,256]{1,0:T(8,128)(2,1)} %get-tuple-element.44, bf16[8192,256]{1,0:T(8,128)(2,1)} %fusion.22), kind=kOutput, calls=%fused_computation.36 | convolution fusion | flops 1140916224 | bytes 14745600 | tf_op jit(solution)/shard_map/dot_general | solution.py:56
  105.2 4.8 %copy.46 = bf16[2,16,256,2,2]{4,3,0,2,1:T(2,128)(2,1)} copy(bf16[2,16,256,2,2]{2,1,4,3,0:T(8,128)(2,1)S(1)} %bitcast.45) | data formatting | bytes 131072 | tf_op jit(solution)/shard_map/reshape | solution.py:59
  110.0 7.2 %reshape.361 = bf16[4,2,4096]{2,1,0:T(2,128)(2,1)S(1)} reshape(bf16[4096,2,2,2]{3,2,1,0:T(2,128)(2,1)} %bitcast.41) | data formatting | bytes 131072
  117.2 6.5 %all_to_all.15 = bf16[4,2,4096]{2,1,0:T(2,128)(2,1)S(1)} all-to-all(bf16[4,2,4096]{2,1,0:T(2,128)(2,1)S(1)} %reshape.361), channel_id=1, replica_groups=mesh['stn'=64,'chan'=4] {'chan'}, dimensions={0} | all-to-all | bytes 131072 | tf_op jit(solution)/shard_map/all_to_all | solution.py:91
  123.6 10.0 %reshape.362 = bf16[4096,2,2,2]{3,2,1,0:T(2,128)(2,1)} reshape(bf16[4,2,4096]{2,1,0:T(2,128)(2,1)S(1)} %all_to_all.15) | data formatting | bytes 131072
  133.7 9.7 %copy.47 = bf16[2,4,1024,2,2]{2,1,4,3,0:T(4,128)(2,1)S(1)} copy(bf16[2,4,1024,2,2]{4,3,0,2,1:T(2,128)(2,1)} %bitcast.42) | data formatting | bytes 131072 | tf_op jit(solution)/shard_map/all_to_all | solution.py:91
  143.5 0.7 copy.38
  144.2 0.7 compare_bitcast_fusion
  145.4 0.7 select_reduce_fusion
  146.2 0.6 broadcast_in_dim.82
  146.8 0.7 fusion.47
  147.6 0.7 broadcast_in_dim.77
  148.3 0.7 copy.42
  149.0 123.4 %all-gather.2.cloned.1.call-done = bf16[512,1024,4]{1,2,0:T(4,128)(2,1)} async-done(((bf16[8,1024,4]{1,2,0:T(4,128)(2,1)}), bf16[512,1024,4]{1,2,0:T(4,128)(2,1)}) %all-gather.2.cloned.1.call-update) | async-done | bytes 4194320 | tf_op jit(solution)/shard_map/all_gather | solution.py:102
  272.4 10.1 %copy.41 = bf16[512,1024,4]{0,2,1:T(4,128)(2,1)} copy(bf16[512,1024,4]{1,2,0:T(4,128)(2,1)} %all-gather.2.cloned.1.call-done) | data formatting | bytes 8388608 | tf_op jit(solution)/shard_map/all_gather | solution.py:102
  282.6 7.7 %slice_negate_fusion = (bf16[512,1024,2]{0,2,1:T(2,128)(2,1)S(1)}, bf16[512,1024,2]{0,2,1:T(2,128)(2,1)S(1)}) fusion(bf16[512,1024,4]{0,2,1:T(4,128)(2,1)} %copy.41), kind=kLoop, calls=%fused_computation.30 | loop fusion | flops 1048576 | bytes 8388608 | tf_op jit(solution)/shard_map/neg | solution.py:64
  290.3 13.0 %fusion.13 = f32[1024,8,1024]{2,1,0:T(8,128)} fusion(bf16[8,1024,4]{0,2,1:T(4,128)(2,1)S(1)} %copy.42, bf16[512,1024,2]{0,2,1:T(2,128)(2,1)S(1)} %get-tuple-element.19, bf16[512,1024,2]{0,2,1:T(2,128)(2,1)S(1)} %get-tuple-element.18, bf16[512,1024,4]{0,2,1:T(4,128)(2,1)S(1)} %copy-done), kind=kOutput, calls=%fused_computation.19 | convolution fusion | flops 92274688 | bytes 42008576 | tf_op jit(solution)/shard_map/dot_general | solution.py:66
  303.3 32.2 %copy.43 = f32[1024,8,2,512]{0,3,2,1:T(8,128)} copy(f32[1024,8,2,512]{3,1,2,0:T(8,128)} %bitcast.40) | data formatting | bytes 67108864 | tf_op jit(solution)/shard_map/reshape | solution.py:70
  335.5 13.4 %fusion = bf16[8,2,1024,64,8]{2,4,3,1,0:T(8,128)(2,1)S(1)} fusion(f32[1024,8,2,512]{0,3,2,1:T(8,128)} %copy.43, f32[512]{0:T(512)S(1)} %mul.838), kind=kLoop, calls=%fused_computation.2 | loop fusion | flops 16777216 | bytes 50333696 | tf_op jit(solution)/shard_map/reshape | solution.py:104
  348.9 7.0 %copy.44 = bf16[8,2,1024,64,8]{2,4,1,0,3:T(8,128)(2,1)} copy(bf16[8,2,1024,64,8]{2,4,3,1,0:T(8,128)(2,1)S(1)} %fusion) | data formatting | bytes 33554432 | tf_op jit(solution)/shard_map/reshape | solution.py:104
  355.9 10.9 %gather_fusion = bf16[33,8,2,1024,8]{3,4,2,1,0:T(8,128)(2,1)} fusion(bf16[8,2,1024,64,8]{2,4,1,0,3:T(8,128)(2,1)} %copy.44, s32[1024]{0:T(1024)S(1)} %pad_clamp_fusion), kind=kCustom, calls=%fused_computation | custom fusion | bytes 17301636 | tf_op jit(solution)/shard_map/jit(_take)/gather | solution.py:105
  366.8 10.3 %fusion.9 = bf16[8,2,1024,264]{2,3,1,0:T(8,128)(2,1)} fusion(pred[264]{0:T(512)(128)(4,1)S(1)} %copy-done.2, pred[264]{0:T(512)(128)(4,1)S(1)} %copy-done.3, bf16[33,8,2,1024,8]{3,4,2,1,0:T(8,128)(2,1)} %gather_fusion), kind=kLoop, calls=%fused_computation.15 | loop fusion | flops 8650752 | bytes 17302032 | tf_op jit(solution)/shard_map/jit(_where)/select_n | solution.py:106
  (26 shorter events, 0.9 us)
Async XLA Ops:
  6.5 71.9 %copy-start.1 = (bf16[2,17,2,8192]{3,2,1,0:T(2,128)(2,1)S(1)}, bf16[2,17,2,8192]{3,2,1,0:T(2,128)(2,1)}, u32[]{:S(2)}) copy-start(bf16[2,17,2,8192]{3,2,1,0:T(2,128)(2,1)} %param.2) | copy-start | bytes 3342340
  6.5 265.9 %all-gather.2.cloned.1.call-start = ((), (), s32[]{:S(2)}) async-start(), calls=%async_computation.1 | async-start | bytes 4259840 | tf_op jit(solution)/shard_map/all_gather | solution.py:102
  282.5 7.8 %copy-start = (bf16[512,1024,4]{0,2,1:T(4,128)(2,1)S(1)}, bf16[512,1024,4]{0,2,1:T(4,128)(2,1)}, u32[]{:S(2)}) copy-start(bf16[512,1024,4]{0,2,1:T(4,128)(2,1)} %copy.41) | copy-start | bytes 12582916
  355.9 10.9 %copy-start.2 = (pred[264]{0:T(512)(128)(4,1)S(1)}, pred[264]{0:T(512)(128)(4,1)}, u32[]{:S(2)}) copy-start(pred[264]{0:T(512)(128)(4,1)} %broadcast_in_dim.82) | copy-start | bytes 796
  355.9 10.9 %copy-start.3 = (pred[264]{0:T(512)(128)(4,1)S(1)}, pred[264]{0:T(512)(128)(4,1)}, u32[]{:S(2)}) copy-start(pred[264]{0:T(512)(128)(4,1)} %broadcast_in_dim.77) | copy-start | bytes 796
Sparse Core Ops, SparseCore 0:
  144.3 128.0 all-gather.1
where the time goes:
time: 388 us; the launch traced here: 384 us
  waiting for transfers between devices  123 us (32%)
  other arithmetic  117 us (30%)
  local copies, waits for them, and re-layouts  96.8 us (25%)
  matrix products  26.7 us (7%)
  between operations  13.6 us (4%)
  blocking collectives  6.49 us (2%)
    all_gather x1, waiting for transfers between devices, per_device(): lax.all_gather(own, 'stn', axis=0, tiled=True)  123 us
    convert_element_type x1, other arithmetic, twiddles(): sines = jnp.sin(phase).astype(jnp.bfloat16)  35 us
    neg x1, other arithmetic, twiddles(): upper = jnp.concatenate([cosines, -sines], axis=1)  32.4 us
    reshape x1, local copies, waits for them, and re-layouts, correlate(): product = product.reshape(product.shape[0], product.shape[1], 2, rows)  32.2 us
    unnamed x12, local copies, waits for them, and re-layouts  18.6 us
    dot_general x1, matrix products, channelise(): jnp.dot(lhs, table, preferred_element_type=jnp.float32)  13.7 us
    reshape x1, other arithmetic, per_device(): whole = whole.reshape(group_in, 2, CH_WIN, n_stn, group_in)  13.4 us
    dot_general x1, matrix products, correlate(): lax.dot_general(own, rhs, (((2,), (2,)), ((1,), (1,))), preferred_element...  13 us
  transfers between devices with their start and end apart: 1, of which 1 were waited for; matrix products, arithmetic and copies ran while one was open for 1% of the time, Pallas kernels for 0%

commit v1 on v0

v1 whole, which is shorter than its diff:
```python
import functools
import math

import jax
import jax.numpy as jnp
import numpy as np
from jax import lax
from jax.experimental import pallas as pl
from jax.experimental.pallas import tpu as pltpu
from jax.sharding import PartitionSpec as P

NFFT = 8192
TAPS = 16
CH_WIN = 1024
N_Z, N_Y, N_X = 8, 2, 4
MIB = 1 << 20
SMEM = pltpu.MemorySpace.SMEM
VMEM = pltpu.MemorySpace.VMEM


def filter_taps():
    pos = np.arange(TAPS * NFFT, dtype=np.float64)
    shifted = (pos + 0.5) / NFFT - TAPS / 2.0
    window = 0.5 - 0.5 * np.cos(2.0 * math.pi * (pos + 0.5) / (TAPS * NFFT))
    taps = (np.sinc(shifted) * window).reshape(TAPS, 64, 1, 128)
    return np.broadcast_to(taps, (TAPS, 64, 2, 128)).reshape(TAPS, 128, 128).astype(np.float32)


def transform_tables():
    k1 = np.arange(64)
    angle = 2.0 * math.pi * (np.outer(k1, k1) % 64) / 64
    cos, sin = np.cos(angle), np.sin(angle)
    first = np.zeros((2, 64, 64, 2))
    first[0, :, :, 0], first[0, :, :, 1] = cos, sin
    first[1, :, :, 0], first[1, :, :, 1] = -sin, cos
    n2 = np.arange(128)
    turn = 2.0 * math.pi * np.outer(k1, n2) / NFFT
    k2 = np.arange(64)
    angle = 2.0 * math.pi * (np.outer(k2, n2) % 128) / 128
    cos = (np.cos(angle) / math.sqrt(NFFT)).reshape(32, 2, 128).transpose(1, 0, 2)
    sin = (np.sin(angle) / math.sqrt(NFFT)).reshape(32, 2, 128).transpose(1, 0, 2)
    second = np.zeros((2, 2, 32, 2, 128))
    second[:, 0, :, 0], second[:, 0, :, 1] = cos, sin
    second[:, 1, :, 0], second[:, 1, :, 1] = -sin, cos
    return (
        first.reshape(128, 128).astype(np.float32),
        np.stack([np.cos(turn), np.sin(turn)]).astype(np.float32),
        second.reshape(128, 256).astype(np.float32),
    )


def spectra_kernel(x_ref, taps_ref, first_ref, turn_ref, second_ref, out_ref, rows_ref):
    turned = []
    for i in range(2):
        for f in range(2):
            total = taps_ref[0] * x_ref[i, f].astype(jnp.float32)
            for tap in range(1, TAPS):
                total = total + taps_ref[tap] * x_ref[i, f + tap].astype(jnp.float32)
            y = jnp.dot(
                first_ref[...], total, precision=lax.Precision.HIGHEST, preferred_element_type=jnp.float32
            )
            re, im = y[:64], y[64:]
            cos, sin = turn_ref[0], turn_ref[1]
            turned.append(jnp.concatenate([re * cos + im * sin, im * cos - re * sin], axis=1))
    z = jnp.concatenate(turned, axis=0)
    o = lax.dot_general(
        second_ref[...], z, (((1,), (1,)), ((), ())),
        precision=lax.Precision.HIGHEST, preferred_element_type=jnp.float32,
    )
    for p in range(2):
        for i in range(2):
            for f in range(2):
                at = (i * 2 + f) * 64
                even = o[p * 32 : p * 32 + 32, at : at + 64]
                odd = o[64 + p * 32 : 64 + p * 32 + 32, at : at + 64]
                s = jnp.concatenate([even, odd], axis=1)
                row = (p * 2 + f) * 2 + i
                for k in range(32):
                    lane = (k % 8) * 128
                    rows_ref[k // 8, row : row + 1, lane : lane + 128] = s[k : k + 1]
    out_ref[...] = rows_ref[...].astype(jnp.bfloat16)


def spectra(samples):
    x = samples.reshape(2, 17, 2, 64, 128).transpose(0, 1, 3, 2, 4).reshape(2, 17, 128, 128)
    first, turn, second = transform_tables()
    return pl.pallas_call(
        spectra_kernel,
        out_shape=jax.ShapeDtypeStruct((4, 8, CH_WIN), jnp.bfloat16),
        in_specs=[pl.BlockSpec(memory_space=VMEM)] * 5,
        out_specs=pl.BlockSpec(memory_space=VMEM),
        scratch_shapes=[pltpu.VMEM((4, 8, CH_WIN), jnp.float32)],
        compiler_params=pltpu.CompilerParams(vmem_limit_bytes=24 * MIB),
        name="spectra",
    )(x, jnp.asarray(filter_taps()), jnp.asarray(first), jnp.asarray(turn), jnp.asarray(second))


def group_kernel(chan_ref, *refs):
    pieces, out_ref, wide_ref, rows_ref = refs[:4], refs[4], refs[5], refs[6]
    for d in range(4):
        wide_ref[d] = pieces[d][...].astype(jnp.float32)
    for source in range(4):
        piece = wide_ref[lax.rem(chan_ref[0] + 4 - source, 4)]
        for t in range(4):
            rows_ref[t, source * 2 : source * 2 + 2, :] = piece[t * 2 : t * 2 + 2]
    out_ref[...] = rows_ref[...].reshape(32, CH_WIN).astype(jnp.bfloat16)


def group_spectra(pieces):
    chan = lax.axis_index("chan").astype(jnp.int32).reshape(1)
    return pl.pallas_call(
        group_kernel,
        out_shape=jax.ShapeDtypeStruct((32, CH_WIN), jnp.bfloat16),
        in_specs=[pl.BlockSpec(memory_space=SMEM)] + [pl.BlockSpec(memory_space=VMEM)] * 4,
        out_specs=pl.BlockSpec(memory_space=VMEM),
        scratch_shapes=[pltpu.VMEM((4, 8, CH_WIN), jnp.float32)] * 2,
        compiler_params=pltpu.CompilerParams(vmem_limit_bytes=8 * MIB),
        name="group_spectra",
    )(chan, *pieces)


def tiles_kernel(base, picks, n_blocks, aliased, *refs):
    slots_ref, own_ref = refs[:2]
    blocks = refs[2 : 2 + n_blocks]
    out_ref, wide_ref, tile_ref, sems = refs[2 + n_blocks + (1 if aliased else 0) :]
    own = own_ref[...].astype(jnp.float32) * 0.5
    for t in range(4):
        for i in range(8):
            wide_ref[i, t] = jnp.broadcast_to(own[t * 8 + i : t * 8 + i + 1], (8, CH_WIN))
    copies = []
    for n, (which, index) in enumerate(picks):
        keep = slots_ref[1, base + n].astype(jnp.float32)

        @pl.loop(0, CH_WIN // 128)
        def _(step):
            lanes = pl.ds(pl.multiple_of(step * 128, 128), 128)
            other = blocks[which][index, :, lanes].astype(jnp.float32) * keep
            r0, r1, i0, i1 = (other[t * 8 : t * 8 + 8] for t in range(4))
            for i in range(8):
                a0, a1, b0, b1 = (wide_ref[i, t, :, lanes] for t in range(4))
                tile_ref[n, i, 0, :, lanes] = ((a0 * r0 + a1 * r1) + (b0 * i0 + b1 * i1)).astype(jnp.bfloat16)
                tile_ref[n, i, 1, :, lanes] = ((b0 * r0 + b1 * r1) - (a0 * i0 + a1 * i1)).astype(jnp.bfloat16)

        copy = pltpu.make_async_copy(tile_ref.at[n], out_ref.at[:, :, slots_ref[0, base + n]], sems.at[n])
        copy.start()
        copies.append(copy)
    for copy in copies:
        copy.wait()


def tiles(slots, base, own, blocks, picks, result, n_slots):
    n = len(picks)
    aliased = result is not None
    operands = [slots, own, *blocks] + ([result] if aliased else [])
    specs = [pl.BlockSpec(memory_space=SMEM)] + [pl.BlockSpec(memory_space=VMEM)] * (1 + len(blocks))
    specs += [pl.BlockSpec(memory_space=pl.ANY)] if aliased else []
    return pl.pallas_call(
        functools.partial(tiles_kernel, base, picks, len(blocks), aliased),
        out_shape=jax.ShapeDtypeStruct((8, 2, n_slots, 8, CH_WIN), jnp.bfloat16),
        in_specs=specs,
        out_specs=pl.BlockSpec(memory_space=pl.ANY),
        input_output_aliases={len(operands) - 1: 0} if aliased else {},
        scratch_shapes=[
            pltpu.VMEM((8, 4, 8, CH_WIN), jnp.float32),
            pltpu.VMEM((n, 8, 2, 8, CH_WIN), jnp.bfloat16),
            pltpu.SemaphoreType.DMA((n,)),
        ],
        compiler_params=pltpu.CompilerParams(vmem_limit_bytes=16 * MIB),
        cost_estimate=pl.CostEstimate(flops=n * 5 * 10**7, bytes_accessed=n * 300_000, transcendentals=0),
        name="tiles",
    )(*operands)


def shift(array, dz, dy, dx):
    def place(z, y, x):
        return ((z % N_Z) * N_Y + y % N_Y) * N_X + x % N_X

    pairs = [
        (place(z, y, x), place(z + dz, y + dy, x + dx)) for z in range(N_Z) for y in range(N_Y) for x in range(N_X)
    ]
    return lax.ppermute(array, "stn", pairs)


def per_device(samples, keeper):
    group = lax.axis_index("stn")
    chan = lax.axis_index("chan")
    z, y, x = group // (N_Y * N_X), group // N_X % N_Y, group % N_X
    n_slots = 33

    parts = spectra(samples)
    pieces = []
    for d in range(4):
        part = lax.dynamic_index_in_dim(parts, (chan + d) % 4, 0, keepdims=False)
        pieces.append(part if d == 0 else lax.ppermute(part, "chan", [(c, (c + d) % 4) for c in range(4)]))
    own = group_spectra(pieces)

    z1, z2, z3, z4 = (shift(own, d, 0, 0) for d in (1, 2, 3, 4))
    y1, y2, y3 = (shift(a, 0, 1, 0) for a in (z1, z2, z3))
    ys = shift(jnp.where(y == 0, own, z4), 0, 1, 0)
    ahead, behind, across = jnp.where(x < 3, own, z4), jnp.where(x > 0, z4, own), jnp.where(x < 2, own, z4)
    b1 = jnp.stack([z1, y1, z2, y2])
    f1, m1 = shift(b1, 0, 0, 1), shift(b1, 0, 0, -1)
    ff1, mm1 = shift(f1[:2], 0, 0, 1), shift(m1[2:], 0, 0, -1)
    f2 = shift(jnp.stack([z3, across, y3, ys, ahead]), 0, 0, 1)
    m2 = shift(jnp.stack([y3, ys, z3, behind]), 0, 0, -1)
    ff2, mm2 = shift(f2[:2], 0, 0, 1), shift(m2[:2], 0, 0, -1)

    def where_from(dz, other, dx):
        ry = 1 - y if other else y
        rx = (x - dx) % N_X
        if dz == "near":
            before = ry * N_X + rx < y * N_X + x
            back = jnp.where(before, 0, 4)
        else:
            back = dz
        return ((z - back) % N_Z) * (N_Y * N_X) + ry * N_X + rx

    local = [own[None], z4[None], ys[None], z1[None], y1[None], z2[None], y2[None], z3[None], y3[None]]
    local_from = [(0, 0, 0), (4, 0, 0), ("near", 1, 0), (1, 0, 0), (1, 1, 0), (2, 0, 0), (2, 1, 0), (3, 0, 0), (3, 1, 0)]
    calls = [
        (local, [(n, 0) for n in range(9)], local_from),
        (
            [f1, m1, ff1, mm1],
            [(w, n) for w in (0, 1) for n in range(4)] + [(2, 0), (2, 1), (3, 0), (3, 1)],
            [(1 + n // 2, n % 2, d) for d in (1, -1) for n in range(4)] + [(1, 0, 2), (1, 1, 2), (2, 0, 2), (2, 1, 2)],
        ),
        (
            [f2, m2, ff2, mm2],
            [(0, 0), (0, 2), (0, 3), (0, 4), (1, 0), (1, 1), (1, 2), (1, 3), (2, 0), (2, 1), (3, 0), (3, 1)],
            [(3, 0, 1), (3, 1, 1), ("near", 1, 1), ("near", 0, 1)]
            + [(3, 1, -1), ("near", 1, -1), (3, 0, -1), ("near", 0, -1)]
            + [(3, 0, 2), ("near", 0, 2), (3, 1, 2), ("near", 1, 2)],
        ),
    ]
    origin = jnp.stack([where_from(*o) for call in calls for o in call[2]]).astype(jnp.int32)
    keep_row = lax.dynamic_index_in_dim(keeper, group, 0, keepdims=False)
    columns = jnp.arange(keeper.shape[1], dtype=jnp.int32)[None, :]
    rank = jnp.sum(jnp.where(columns < origin[:, None], keep_row[None, :], 0), axis=1)
    kept = jnp.sum(jnp.where(columns == origin[:, None], keep_row[None, :], 0), axis=1)
    slots = jnp.stack([jnp.where(kept == 1, rank, n_slots - 1), kept]).astype(jnp.int32)

    result, base = None, 0
    for blocks, picks, _ in calls:
        result = tiles(slots, base, own, blocks, picks, result, n_slots)
        base += len(picks)
    return result.reshape(8, 2, n_slots * 8, CH_WIN).swapaxes(2, 3)


def solution(mesh):
    return jax.shard_map(
        per_device,
        mesh=mesh,
        in_specs=(P(("stn", "chan"), None, None, None), P()),
        out_specs=P("stn", None, "chan", None),
        check_vma=False,
    )
```

time: 388 us -> 70 us (0.18)
  the two profiles are of different devices: /device:TPU:16 before, /device:TPU:6 now
where the time goes in v1:
time: 70 us; the launch traced here: 69.7 us
  starting transfers between devices  33.4 us (48%)
  waiting for transfers between devices  18 us (26%)
  Pallas kernels  12.3 us (18%)
  local copies, waits for them, and re-layouts  5.25 us (8%)
    ppermute x16, starting transfers between devices, shift(): return lax.ppermute(array, 'stn', pairs)  30.3 us
    ppermute x16, waiting for transfers between devices, shift(): return lax.ppermute(array, 'stn', pairs)  16.7 us
    pallas_call x3, Pallas kernels, tiles(): pl.pallas_call(functools.partial(tiles_kernel, base, picks, len(blocks),...  11.1 us
    unnamed x15, local copies, waits for them, and re-layouts  5.08 us
    ppermute x3, starting transfers between devices, per_device(): lax.ppermute(part, 'chan', [(c, (c + d) % 4) for c in range(4)])  3.11 us
  transfers between devices with their start and end apart: 19, of which 9 were waited for; matrix products, arithmetic and copies ran while one was open for 1% of the time, Pallas kernels for 10%

profile of v1, /device:TPU:6, one launch (start us, length us, event | category | flops | bytes accessed | tf_op | source)
XLA Modules:
  0.0 69.7 jit_solution(2505503139322186106)
XLA Ops:
  0.0 1.3 %copy-done.1 = bf16[2,17,2,8192]{3,2,1,0:T(2,128)(2,1)S(1)} copy-done((bf16[2,17,2,8192]{3,2,1,0:T(2,128)(2,1)S(1)}, bf16[2,17,2,8192]{3,2,1,0:T(2,128)(2,1)}, u32[]{:S(2)}) %copy-start.1) | copy-done | bytes 1114136
  1.3 1.2 %copy-done.2 = f32[16,128,128]{2,1,0:T(8,128)S(1)} copy-done((f32[16,128,128]{2,1,0:T(8,128)S(1)}, f32[16,128,128]{2,1,0:T(8,128)}, u32[]{:S(2)}) %copy-start.2) | copy-done | bytes 1048600
  2.5 0.9 %copy-done.3 = f32[128,256]{1,0:T(8,128)S(1)} copy-done((f32[128,256]{1,0:T(8,128)S(1)}, f32[128,256]{1,0:T(8,128)}, u32[]{:S(2)}) %copy-start.3) | copy-done | bytes 131096
  3.4 0.8 %copy-done.4 = f32[128,128]{1,0:T(8,128)S(1)} copy-done((f32[128,128]{1,0:T(8,128)S(1)}, f32[128,128]{1,0:T(8,128)}, u32[]{:S(2)}) %copy-start.4) | copy-done | bytes 65560
  4.2 0.8 %copy-done.5 = f32[2,64,128]{2,1,0:T(8,128)S(1)} copy-done((f32[2,64,128]{2,1,0:T(8,128)S(1)}, f32[2,64,128]{2,1,0:T(8,128)}, u32[]{:S(2)}) %copy-start.5) | copy-done | bytes 65560
  5.1 1.2 %spectra.1 = bf16[4,8,1024]{2,1,0:T(8,128)(2,1)S(1)} custom-call(bf16[2,17,128,128]{3,2,1,0:T(8,128)(2,1)S(1)} %bitcast.75, f32[16,128,128]{2,1,0:T(8,128)S(1)} %copy-done.2, f32[128,128]{1,0:T(8,128)S(1)} %copy-done.4, f32[2,64,128]{2,1,0:T(8,128)S(1)} %copy-done.5, f32[128,256]{1,0:T(8,128)S(1)} %copy-done.3), custom_call_target="tpu_custom_call" | custom-call | tf_op jit(solution)/shard_map/spectra/pallas_call | solution.py:87
  6.4 1.7 %collective-permute-start.1 = (bf16[8,1024]{1,0:T(8,128)(2,1)S(1)}, bf16[8,1024]{1,0:T(8,128)(2,1)S(1)}, u32[]{:S(2)}, u32[]{:S(2)}) collective-permute-start(bf16[8,1024]{1,0:T(8,128)(2,1)S(1)} %get-tuple-element.10), channel_id=1, source_target_pairs={{0,2},{1,3},{2,0},{3,1},{4,6},{5,7},{6,4},{7,5},{8,10},{9,11},{10,... | collective-permute-start | bytes 49160 | tf_op jit(solution)/shard_map/ppermute | solution.py:194
  8.0 1.4 %collective-permute-start.2 = (bf16[8,1024]{1,0:T(8,128)(2,1)S(1)}, bf16[8,1024]{1,0:T(8,128)(2,1)S(1)}, u32[]{:S(2)}, u32[]{:S(2)}) collective-permute-start(bf16[8,1024]{1,0:T(8,128)(2,1)S(1)} %get-tuple-element.9), channel_id=1, source_target_pairs={{0,3},{1,0},{2,1},{3,2},{4,7},{5,4},{6,5},{7,6},{8,11},{9,8},{10,9... | collective-permute-start | bytes 49160 | tf_op jit(solution)/shard_map/ppermute | solution.py:194
  9.5 0.7 collective-permute-done.1.refs_2_
  10.2 0.6 collective-permute-done.2.refs_3_
  10.9 7.3 %collective-permute-start.4 = (bf16[32,1024]{1,0:T(8,128)(2,1)S(1)}, bf16[32,1024]{1,0:T(8,128)(2,1)S(1)}, u32[]{:S(2)}, u32[]{:S(2)}) collective-permute-start(bf16[32,1024]{1,0:T(8,128)(2,1)S(1)} %group_spectra.1.refs_1_), channel_id=1, source_target_pairs={{0,128},{4,132},{8,136},{12,140},{16,144},{20,148},{24,152},{28,15... | collective-permute-start | bytes 196616 | tf_op jit(solution)/shard_map/ppermute | solution.py:181
  18.2 2.0 %collective-permute-start.3 = (bf16[32,1024]{1,0:T(8,128)(2,1)S(1)}, bf16[32,1024]{1,0:T(8,128)(2,1)S(1)}, u32[]{:S(2)}, u32[]{:S(2)}) collective-permute-start(bf16[32,1024]{1,0:T(8,128)(2,1)S(1)} %group_spectra.1.refs_1_), channel_id=1, source_target_pairs={{0,96},{4,100},{8,104},{12,108},{16,112},{20,116},{24,120},{28,124... | collective-permute-start | bytes 196616 | tf_op jit(solution)/shard_map/ppermute | solution.py:181
  20.2 0.7 collective-permute-start.13
  21.1 3.3 %collective-permute-start.6 = (bf16[32,1024]{1,0:T(8,128)(2,1)S(1)}, bf16[32,1024]{1,0:T(8,128)(2,1)S(1)}, u32[]{:S(2)}, u32[]{:S(2)}) collective-permute-start(bf16[32,1024]{1,0:T(8,128)(2,1)S(1)} %get-tuple-element.8), channel_id=1, source_target_pairs={{0,16},{4,20},{8,24},{12,28},{16,0},{20,4},{24,8},{28,12},{32,48},... | collective-permute-start | bytes 196616 | tf_op jit(solution)/shard_map/ppermute | solution.py:181
  24.4 3.8 %collective-permute-done.3 = bf16[32,1024]{1,0:T(8,128)(2,1)S(1)} collective-permute-done((bf16[32,1024]{1,0:T(8,128)(2,1)S(1)}, bf16[32,1024]{1,0:T(8,128)(2,1)S(1)}, u32[]{:S(2)}, u32[]{:S(2)}) %collective-permute-start.3) | collective-permute-done | bytes 65568 | tf_op jit(solution)/shard_map/ppermute | solution.py:181
  28.2 3.3 %collective-permute-start.5 = (bf16[32,1024]{1,0:T(8,128)(2,1)S(1)}, bf16[32,1024]{1,0:T(8,128)(2,1)S(1)}, u32[]{:S(2)}, u32[]{:S(2)}) collective-permute-start(bf16[32,1024]{1,0:T(8,128)(2,1)S(1)} %collective-permute-done.3), channel_id=1, source_target_pairs={{0,16},{4,20},{8,24},{12,28},{16,0},{20,4},{24,8},{28,12},{32,48},... | collective-permute-start | bytes 196616 | tf_op jit(solution)/shard_map/ppermute | solution.py:181
  31.5 2.3 %collective-permute-start.12 = (bf16[32,1024]{1,0:T(8,128)(2,1)S(1)}, bf16[32,1024]{1,0:T(8,128)(2,1)S(1)}, u32[]{:S(2)}, u32[]{:S(2)}) collective-permute-start(bf16[32,1024]{1,0:T(8,128)(2,1)S(1)} %collective-permute-done.11), channel_id=1, source_target_pairs={{0,16},{4,20},{8,24},{12,28},{16,0},{20,4},{24,8},{28,12},{32,48},... | collective-permute-start | bytes 196616 | tf_op jit(solution)/shard_map/ppermute | solution.py:181
  33.8 1.4 %collective-permute-start.14 = (bf16[32,1024]{1,0:T(8,128)(2,1)S(1)}, bf16[32,1024]{1,0:T(8,128)(2,1)S(1)}, u32[]{:S(2)}, u32[]{:S(2)}) collective-permute-start(bf16[32,1024]{1,0:T(8,128)(2,1)S(1)} %collective-permute-done.13), channel_id=1, source_target_pairs={{0,16},{4,20},{8,24},{12,28},{16,0},{20,4},{24,8},{28,12},{32,48},... | collective-permute-start | bytes 196616 | tf_op jit(solution)/shard_map/ppermute | solution.py:181
  35.2 2.6 %collective-permute-done.12 = bf16[32,1024]{1,0:T(8,128)(2,1)S(1)} collective-permute-done((bf16[32,1024]{1,0:T(8,128)(2,1)S(1)}, bf16[32,1024]{1,0:T(8,128)(2,1)S(1)}, u32[]{:S(2)}, u32[]{:S(2)}) %collective-permute-start.12) | collective-permute-done | bytes 65568 | tf_op jit(solution)/shard_map/ppermute | solution.py:181
  37.8 1.8 %collective-permute-done.14 = bf16[32,1024]{1,0:T(8,128)(2,1)S(1)} collective-permute-done((bf16[32,1024]{1,0:T(8,128)(2,1)S(1)}, bf16[32,1024]{1,0:T(8,128)(2,1)S(1)}, u32[]{:S(2)}, u32[]{:S(2)}) %collective-permute-start.14) | collective-permute-done | bytes 65568 | tf_op jit(solution)/shard_map/ppermute | solution.py:181
  40.2 1.5 %collective-permute-start.16 = (bf16[4,32,1024]{2,1,0:T(8,128)(2,1)S(1)}, bf16[4,32,1024]{2,1,0:T(8,128)(2,1)S(1)}, u32[]{:S(2)}, u32[]{:S(2)}) collective-permute-start(bf16[4,32,1024]{2,1,0:T(8,128)(2,1)S(1)} %pad_maximum_fusion.1), channel_id=1, source_target_pairs={{0,12},{4,0},{8,4},{12,8},{16,28},{20,16},{24,20},{28,24},{32,44},... | collective-permute-start | bytes 786440 | tf_op jit(solution)/shard_map/ppermute | solution.py:181
  41.7 0.9 %collective-permute-start.8 = (bf16[4,32,1024]{2,1,0:T(8,128)(2,1)S(1)}, bf16[4,32,1024]{2,1,0:T(8,128)(2,1)S(1)}, u32[]{:S(2)}, u32[]{:S(2)}) collective-permute-start(bf16[4,32,1024]{2,1,0:T(8,128)(2,1)S(1)} %pad_maximum_fusion), channel_id=1, source_target_pairs={{0,12},{4,0},{8,4},{12,8},{16,28},{20,16},{24,20},{28,24},{32,44},... | collective-permute-start | bytes 786440 | tf_op jit(solution)/shard_map/ppermute | solution.py:181
  42.7 2.5 %collective-permute-start.7 = (bf16[5,32,1024]{2,1,0:T(8,128)(2,1)S(1)}, bf16[5,32,1024]{2,1,0:T(8,128)(2,1)S(1)}, u32[]{:S(2)}, u32[]{:S(2)}) collective-permute-start(bf16[5,32,1024]{2,1,0:T(8,128)(2,1)S(1)} %bitcast_dynamic-update-slice_fusion), channel_id=1, source_target_pairs={{0,4},{4,8},{8,12},{12,0},{16,20},{20,24},{24,28},{28,16},{32,36},... | collective-permute-start | bytes 983048 | tf_op jit(solution)/shard_map/ppermute | solution.py:181
  45.4 3.6 %collective-permute-done.15.refs_2_ = bf16[4,32,1024]{2,1,0:T(8,128)(2,1)S(1)} collective-permute-done((bf16[4,32,1024]{2,1,0:T(8,128)(2,1)S(1)}, bf16[4,32,1024]{2,1,0:T(8,128)(2,1)S(1)}, u32[]{:S(2)}, u32[]{:S(2)}) %collective-permute-start.15) | collective-permute-done | bytes 262176 | tf_op jit(solution)/shard_map/ppermute | solution.py:181
  49.5 1.1 %collective-permute-done.16.refs_3_ = bf16[4,32,1024]{2,1,0:T(8,128)(2,1)S(1)} collective-permute-done((bf16[4,32,1024]{2,1,0:T(8,128)(2,1)S(1)}, bf16[4,32,1024]{2,1,0:T(8,128)(2,1)S(1)}, u32[]{:S(2)}, u32[]{:S(2)}) %collective-permute-start.16) | collective-permute-done | bytes 262176 | tf_op jit(solution)/shard_map/ppermute | solution.py:181
  50.6 0.7 collective-permute-start.18
  51.3 3.7 %collective-permute-done.8.refs_3_ = bf16[4,32,1024]{2,1,0:T(8,128)(2,1)S(1)} collective-permute-done((bf16[4,32,1024]{2,1,0:T(8,128)(2,1)S(1)}, bf16[4,32,1024]{2,1,0:T(8,128)(2,1)S(1)}, u32[]{:S(2)}, u32[]{:S(2)}) %collective-permute-start.8) | collective-permute-done | bytes 262176 | tf_op jit(solution)/shard_map/ppermute | solution.py:181
  55.0 1.5 %collective-permute-start.10 = (bf16[2,32,1024]{2,1,0:T(8,128)(2,1)S(1)}, bf16[2,32,1024]{2,1,0:T(8,128)(2,1)S(1)}, u32[]{:S(2)}, u32[]{:S(2)}) collective-permute-start(bf16[2,32,1024]{2,1,0:T(8,128)(2,1)S(1)} %slice.17), channel_id=1, source_target_pairs={{0,12},{4,0},{8,4},{12,8},{16,28},{20,16},{24,20},{28,24},{32,44},... | collective-permute-start | bytes 393224 | tf_op jit(solution)/shard_map/ppermute | solution.py:181
  56.5 1.9 %collective-permute-start.9 = (bf16[2,32,1024]{2,1,0:T(8,128)(2,1)S(1)}, bf16[2,32,1024]{2,1,0:T(8,128)(2,1)S(1)}, u32[]{:S(2)}, u32[]{:S(2)}) collective-permute-start(bf16[2,32,1024]{2,1,0:T(8,128)(2,1)S(1)} %slice.16), channel_id=1, source_target_pairs={{0,4},{4,8},{8,12},{12,0},{16,20},{20,24},{24,28},{28,16},{32,36},... | collective-permute-start | bytes 393224 | tf_op jit(solution)/shard_map/ppermute | solution.py:181
  58.4 3.3 %tiles.3.refs_6_ = bf16[8,2,33,8,1024]{4,3,2,1,0:T(8,128)(2,1)} custom-call(s32[2,33]{1,0:T(2,128)S(1)} %pad_add_fusion.refs_0_, bf16[32,1024]{1,0:T(8,128)(2,1)S(1)} %group_spectra.1.refs_1_, bf16[1,32,1024]{2,1,0:T(8,128)(2,1)S(1)} %bitcast.74, bf16[1,32,1024]{2,1,0:T(8,128)(2,1)S(1)} %bitcast.76, bf16[1,32,1024]{2,1,0:T(8,128)(2,1)S(1)} %bitcast.80, ...), custom_call_target="tpu_custom_call" | custom-call | flops 450000000 | bytes 2700000 | tf_op jit(solution)/shard_map/tiles/pallas_call | solution.py:157
  61.7 3.9 %tiles.4.refs_6_ = bf16[8,2,33,8,1024]{4,3,2,1,0:T(8,128)(2,1)} custom-call(s32[2,33]{1,0:T(2,128)S(1)} %pad_add_fusion.refs_0_, bf16[32,1024]{1,0:T(8,128)(2,1)S(1)} %group_spectra.1.refs_1_, bf16[4,32,1024]{2,1,0:T(8,128)(2,1)S(1)} %collective-permute-done.15.refs_2_, ...), custom_call_target="tpu_custom_call", output_to_operand_aliasing={{}: (6, {})} | custom-call | flops 600000000 | bytes 3600000 | tf_op jit(solution)/shard_map/tiles/pallas_call | solution.py:157
  65.6 3.9 %tiles.5 = bf16[8,2,33,8,1024]{4,3,2,1,0:T(8,128)(2,1)} custom-call(s32[2,33]{1,0:T(2,128)S(1)} %pad_add_fusion.refs_0_, bf16[32,1024]{1,0:T(8,128)(2,1)S(1)} %group_spectra.1.refs_1_, bf16[5,32,1024]{2,1,0:T(8,128)(2,1)S(1)} %collective-permute-done.7.refs_2_, ...), custom_call_target="tpu_custom_call", output_to_operand_aliasing={{}: (6, {})} | custom-call | flops 600000000 | bytes 3600000 | tf_op jit(solution)/shard_map/tiles/pallas_call | solution.py:157
  (41 shorter events, 2.1 us)
Async XLA Ops:
  0.0 18.2 %copy-start = (s32[64,64]{1,0:T(8,128)S(1)}, s32[64,64]{1,0:T(8,128)}, u32[]{:S(2)}) copy-start(s32[64,64]{1,0:T(8,128)} %param.7) | copy-start | bytes 49156
  0.0 1.3 %copy-start.1 = (bf16[2,17,2,8192]{3,2,1,0:T(2,128)(2,1)S(1)}, bf16[2,17,2,8192]{3,2,1,0:T(2,128)(2,1)}, u32[]{:S(2)}) copy-start(bf16[2,17,2,8192]{3,2,1,0:T(2,128)(2,1)} %param.6) | copy-start | bytes 3342340
  1.3 1.2 %copy-start.2 = (f32[16,128,128]{2,1,0:T(8,128)S(1)}, f32[16,128,128]{2,1,0:T(8,128)}, u32[]{:S(2)}) copy-start(f32[16,128,128]{2,1,0:T(8,128)} %constant.277.clone.taps_ref) | copy-start | bytes 3145732
  2.5 0.9 %copy-start.3 = (f32[128,256]{1,0:T(8,128)S(1)}, f32[128,256]{1,0:T(8,128)}, u32[]{:S(2)}) copy-start(f32[128,256]{1,0:T(8,128)} %constant.280.clone.second_ref) | copy-start | bytes 393220
  3.4 0.8 %copy-start.4 = (f32[128,128]{1,0:T(8,128)S(1)}, f32[128,128]{1,0:T(8,128)}, u32[]{:S(2)}) copy-start(f32[128,128]{1,0:T(8,128)} %constant.278.clone.first_ref) | copy-start | bytes 196612
  4.2 0.8 %copy-start.5 = (f32[2,64,128]{2,1,0:T(8,128)S(1)}, f32[2,64,128]{2,1,0:T(8,128)}, u32[]{:S(2)}) copy-start(f32[2,64,128]{2,1,0:T(8,128)} %constant.279.clone.turn_ref) | copy-start | bytes 196612
  6.3 3.2 %collective-permute-start = (bf16[8,1024]{1,0:T(8,128)(2,1)S(1)}, bf16[8,1024]{1,0:T(8,128)(2,1)S(1)}, u32[]{:S(2)}, u32[]{:S(2)}) collective-permute-start(bf16[8,1024]{1,0:T(8,128)(2,1)S(1)} %get-tuple-element.11), channel_id=1, source_target_pairs={{0,1},{1,2},{2,3},{3,0},{4,5},{5,6},{6,7},{7,4},{8,9},{9,10},{10,1... | collective-permute-start | bytes 49160 | tf_op jit(solution)/shard_map/ppermute | solution.py:194
  6.4 3.8 %collective-permute-start.1 = (bf16[8,1024]{1,0:T(8,128)(2,1)S(1)}, bf16[8,1024]{1,0:T(8,128)(2,1)S(1)}, u32[]{:S(2)}, u32[]{:S(2)}) collective-permute-start(bf16[8,1024]{1,0:T(8,128)(2,1)S(1)} %get-tuple-element.10), channel_id=1, source_target_pairs={{0,2},{1,3},{2,0},{3,1},{4,6},{5,7},{6,4},{7,5},{8,10},{9,11},{10,... | collective-permute-start | bytes 49160 | tf_op jit(solution)/shard_map/ppermute | solution.py:194
  8.0 2.8 %collective-permute-start.2 = (bf16[8,1024]{1,0:T(8,128)(2,1)S(1)}, bf16[8,1024]{1,0:T(8,128)(2,1)S(1)}, u32[]{:S(2)}, u32[]{:S(2)}) collective-permute-start(bf16[8,1024]{1,0:T(8,128)(2,1)S(1)} %get-tuple-element.9), channel_id=1, source_target_pairs={{0,3},{1,0},{2,1},{3,2},{4,7},{5,4},{6,5},{7,6},{8,11},{9,8},{10,9... | collective-permute-start | bytes 49160 | tf_op jit(solution)/shard_map/ppermute | solution.py:194
  10.9 10.2 %collective-permute-start.4 = (bf16[32,1024]{1,0:T(8,128)(2,1)S(1)}, bf16[32,1024]{1,0:T(8,128)(2,1)S(1)}, u32[]{:S(2)}, u32[]{:S(2)}) collective-permute-start(bf16[32,1024]{1,0:T(8,128)(2,1)S(1)} %group_spectra.1.refs_1_), channel_id=1, source_target_pairs={{0,128},{4,132},{8,136},{12,140},{16,144},{20,148},{24,152},{28,15... | collective-permute-start | bytes 196616 | tf_op jit(solution)/shard_map/ppermute | solution.py:181
  18.2 10.0 %collective-permute-start.3 = (bf16[32,1024]{1,0:T(8,128)(2,1)S(1)}, bf16[32,1024]{1,0:T(8,128)(2,1)S(1)}, u32[]{:S(2)}, u32[]{:S(2)}) collective-permute-start(bf16[32,1024]{1,0:T(8,128)(2,1)S(1)} %group_spectra.1.refs_1_), channel_id=1, source_target_pairs={{0,96},{4,100},{8,104},{12,108},{16,112},{20,116},{24,120},{28,124... | collective-permute-start | bytes 196616 | tf_op jit(solution)/shard_map/ppermute | solution.py:181
  20.2 11.3 %collective-permute-start.11 = (bf16[32,1024]{1,0:T(8,128)(2,1)S(1)}, bf16[32,1024]{1,0:T(8,128)(2,1)S(1)}, u32[]{:S(2)}, u32[]{:S(2)}) collective-permute-start(bf16[32,1024]{1,0:T(8,128)(2,1)S(1)} %group_spectra.1.refs_1_), channel_id=1, source_target_pairs={{0,32},{4,36},{8,40},{12,44},{16,48},{20,52},{24,56},{28,60},{32,6... | collective-permute-start | bytes 196616 | tf_op jit(solution)/shard_map/ppermute | solution.py:181
  20.2 13.6 %collective-permute-start.13 = (bf16[32,1024]{1,0:T(8,128)(2,1)S(1)}, bf16[32,1024]{1,0:T(8,128)(2,1)S(1)}, u32[]{:S(2)}, u32[]{:S(2)}) collective-permute-start(bf16[32,1024]{1,0:T(8,128)(2,1)S(1)} %group_spectra.1.refs_1_), channel_id=1, source_target_pairs={{0,64},{4,68},{8,72},{12,76},{16,80},{20,84},{24,88},{28,92},{32,9... | collective-permute-start | bytes 196616 | tf_op jit(solution)/shard_map/ppermute | solution.py:181
  21.1 20.6 %collective-permute-start.6 = (bf16[32,1024]{1,0:T(8,128)(2,1)S(1)}, bf16[32,1024]{1,0:T(8,128)(2,1)S(1)}, u32[]{:S(2)}, u32[]{:S(2)}) collective-permute-start(bf16[32,1024]{1,0:T(8,128)(2,1)S(1)} %get-tuple-element.8), channel_id=1, source_target_pairs={{0,16},{4,20},{8,24},{12,28},{16,0},{20,4},{24,8},{28,12},{32,48},... | collective-permute-start | bytes 196616 | tf_op jit(solution)/shard_map/ppermute | solution.py:181
  28.2 13.5 %collective-permute-start.5 = (bf16[32,1024]{1,0:T(8,128)(2,1)S(1)}, bf16[32,1024]{1,0:T(8,128)(2,1)S(1)}, u32[]{:S(2)}, u32[]{:S(2)}) collective-permute-start(bf16[32,1024]{1,0:T(8,128)(2,1)S(1)} %collective-permute-done.3), channel_id=1, source_target_pairs={{0,16},{4,20},{8,24},{12,28},{16,0},{20,4},{24,8},{28,12},{32,48},... | collective-permute-start | bytes 196616 | tf_op jit(solution)/shard_map/ppermute | solution.py:181
  31.5 6.3 %collective-permute-start.12 = (bf16[32,1024]{1,0:T(8,128)(2,1)S(1)}, bf16[32,1024]{1,0:T(8,128)(2,1)S(1)}, u32[]{:S(2)}, u32[]{:S(2)}) collective-permute-start(bf16[32,1024]{1,0:T(8,128)(2,1)S(1)} %collective-permute-done.11), channel_id=1, source_target_pairs={{0,16},{4,20},{8,24},{12,28},{16,0},{20,4},{24,8},{28,12},{32,48},... | collective-permute-start | bytes 196616 | tf_op jit(solution)/shard_map/ppermute | solution.py:181
  33.8 5.8 %collective-permute-start.14 = (bf16[32,1024]{1,0:T(8,128)(2,1)S(1)}, bf16[32,1024]{1,0:T(8,128)(2,1)S(1)}, u32[]{:S(2)}, u32[]{:S(2)}) collective-permute-start(bf16[32,1024]{1,0:T(8,128)(2,1)S(1)} %collective-permute-done.13), channel_id=1, source_target_pairs={{0,16},{4,20},{8,24},{12,28},{16,0},{20,4},{24,8},{28,12},{32,48},... | collective-permute-start | bytes 196616 | tf_op jit(solution)/shard_map/ppermute | solution.py:181
  39.6 9.3 %collective-permute-start.15 = (bf16[4,32,1024]{2,1,0:T(8,128)(2,1)S(1)}, bf16[4,32,1024]{2,1,0:T(8,128)(2,1)S(1)}, u32[]{:S(2)}, u32[]{:S(2)}) collective-permute-start(bf16[4,32,1024]{2,1,0:T(8,128)(2,1)S(1)} %pad_maximum_fusion.1), channel_id=1, source_target_pairs={{0,4},{4,8},{8,12},{12,0},{16,20},{20,24},{24,28},{28,16},{32,36},... | collective-permute-start | bytes 786440 | tf_op jit(solution)/shard_map/ppermute | solution.py:181
  40.2 10.5 %collective-permute-start.16 = (bf16[4,32,1024]{2,1,0:T(8,128)(2,1)S(1)}, bf16[4,32,1024]{2,1,0:T(8,128)(2,1)S(1)}, u32[]{:S(2)}, u32[]{:S(2)}) collective-permute-start(bf16[4,32,1024]{2,1,0:T(8,128)(2,1)S(1)} %pad_maximum_fusion.1), channel_id=1, source_target_pairs={{0,12},{4,0},{8,4},{12,8},{16,28},{20,16},{24,20},{28,24},{32,44},... | collective-permute-start | bytes 786440 | tf_op jit(solution)/shard_map/ppermute | solution.py:181
  41.7 13.2 %collective-permute-start.8 = (bf16[4,32,1024]{2,1,0:T(8,128)(2,1)S(1)}, bf16[4,32,1024]{2,1,0:T(8,128)(2,1)S(1)}, u32[]{:S(2)}, u32[]{:S(2)}) collective-permute-start(bf16[4,32,1024]{2,1,0:T(8,128)(2,1)S(1)} %pad_maximum_fusion), channel_id=1, source_target_pairs={{0,12},{4,0},{8,4},{12,8},{16,28},{20,16},{24,20},{28,24},{32,44},... | collective-permute-start | bytes 786440 | tf_op jit(solution)/shard_map/ppermute | solution.py:181
  42.7 13.8 %collective-permute-start.7 = (bf16[5,32,1024]{2,1,0:T(8,128)(2,1)S(1)}, bf16[5,32,1024]{2,1,0:T(8,128)(2,1)S(1)}, u32[]{:S(2)}, u32[]{:S(2)}) collective-permute-start(bf16[5,32,1024]{2,1,0:T(8,128)(2,1)S(1)} %bitcast_dynamic-update-slice_fusion), channel_id=1, source_target_pairs={{0,4},{4,8},{8,12},{12,0},{16,20},{20,24},{24,28},{28,16},{32,36},... | collective-permute-start | bytes 983048 | tf_op jit(solution)/shard_map/ppermute | solution.py:181
  48.9 12.7 %collective-permute-start.17 = (bf16[2,32,1024]{2,1,0:T(8,128)(2,1)S(1)}, bf16[2,32,1024]{2,1,0:T(8,128)(2,1)S(1)}, u32[]{:S(2)}, u32[]{:S(2)}) collective-permute-start(bf16[2,32,1024]{2,1,0:T(8,128)(2,1)S(1)} %slice.18), channel_id=1, source_target_pairs={{0,4},{4,8},{8,12},{12,0},{16,20},{20,24},{24,28},{28,16},{32,36},... | collective-permute-start | bytes 393224 | tf_op jit(solution)/shard_map/ppermute | solution.py:181
  50.6 11.1 %collective-permute-start.18 = (bf16[2,32,1024]{2,1,0:T(8,128)(2,1)S(1)}, bf16[2,32,1024]{2,1,0:T(8,128)(2,1)S(1)}, u32[]{:S(2)}, u32[]{:S(2)}) collective-permute-start(bf16[2,32,1024]{2,1,0:T(8,128)(2,1)S(1)} %slice.19), channel_id=1, source_target_pairs={{0,12},{4,0},{8,4},{12,8},{16,28},{20,16},{24,20},{28,24},{32,44},... | collective-permute-start | bytes 393224 | tf_op jit(solution)/shard_map/ppermute | solution.py:181
  55.0 10.6 %collective-permute-start.10 = (bf16[2,32,1024]{2,1,0:T(8,128)(2,1)S(1)}, bf16[2,32,1024]{2,1,0:T(8,128)(2,1)S(1)}, u32[]{:S(2)}, u32[]{:S(2)}) collective-permute-start(bf16[2,32,1024]{2,1,0:T(8,128)(2,1)S(1)} %slice.17), channel_id=1, source_target_pairs={{0,12},{4,0},{8,4},{12,8},{16,28},{20,16},{24,20},{28,24},{32,44},... | collective-permute-start | bytes 393224 | tf_op jit(solution)/shard_map/ppermute | solution.py:181
  56.5 9.1 %collective-permute-start.9 = (bf16[2,32,1024]{2,1,0:T(8,128)(2,1)S(1)}, bf16[2,32,1024]{2,1,0:T(8,128)(2,1)S(1)}, u32[]{:S(2)}, u32[]{:S(2)}) collective-permute-start(bf16[2,32,1024]{2,1,0:T(8,128)(2,1)S(1)} %slice.16), channel_id=1, source_target_pairs={{0,4},{4,8},{8,12},{12,0},{16,20},{20,24},{24,28},{28,16},{32,36},... | collective-permute-start | bytes 393224 | tf_op jit(solution)/shard_map/ppermute | solution.py:181

commit v2 on v1

v2 whole, which is shorter than its diff:
```python
import functools
import math

import jax
import jax.numpy as jnp
import numpy as np
from jax import lax
from jax.experimental import pallas as pl
from jax.experimental.pallas import tpu as pltpu
from jax.sharding import PartitionSpec as P

NFFT = 8192
TAPS = 16
CH_WIN = 1024
N_Z, N_Y, N_X = 8, 2, 4
MIB = 1 << 20
UNROLL = 8
SMEM = pltpu.MemorySpace.SMEM
VMEM = pltpu.MemorySpace.VMEM
HBM = pltpu.MemorySpace.HBM


def filter_taps():
    pos = np.arange(TAPS * NFFT, dtype=np.float64)
    shifted = (pos + 0.5) / NFFT - TAPS / 2.0
    window = 0.5 - 0.5 * np.cos(2.0 * math.pi * (pos + 0.5) / (TAPS * NFFT))
    taps = (np.sinc(shifted) * window).reshape(TAPS, 64, 1, 128)
    return np.broadcast_to(taps, (TAPS, 64, 2, 128)).reshape(TAPS, 128, 128).astype(np.float32)


def transform_tables():
    k1 = np.arange(64)
    angle = 2.0 * math.pi * (np.outer(k1, k1) % 64) / 64
    cos, sin = np.cos(angle), np.sin(angle)
    first = np.zeros((2, 64, 64, 2))
    first[0, :, :, 0], first[0, :, :, 1] = cos, sin
    first[1, :, :, 0], first[1, :, :, 1] = -sin, cos
    n2 = np.arange(128)
    turn = 2.0 * math.pi * np.outer(k1, n2) / NFFT
    k2 = np.arange(64)
    angle = 2.0 * math.pi * (np.outer(k2, n2) % 128) / 128
    cos = (np.cos(angle) / math.sqrt(NFFT)).reshape(32, 2, 128).transpose(1, 0, 2)
    sin = (np.sin(angle) / math.sqrt(NFFT)).reshape(32, 2, 128).transpose(1, 0, 2)
    second = np.zeros((2, 2, 32, 2, 128))
    second[:, 0, :, 0], second[:, 0, :, 1] = cos, sin
    second[:, 1, :, 0], second[:, 1, :, 1] = -sin, cos
    return (
        first.reshape(128, 128).astype(np.float32),
        np.stack([np.cos(turn), np.sin(turn)]).astype(np.float32),
        second.reshape(128, 256).astype(np.float32),
    )


def spectra_kernel(*refs):
    chan_ref, outs, held, sems, rows_ref = refs[5], refs[6:10], refs[10:15], refs[15], refs[16]
    copies = [pltpu.make_async_copy(refs[n], held[n], sems.at[n]) for n in range(5)]
    for copy in copies:
        copy.start()
    for copy in copies:
        copy.wait()
    x_ref, taps_ref, first_ref, turn_ref, second_ref = held
    turned = []
    for i in range(2):
        for f in range(2):
            total = taps_ref[0] * x_ref[i, f].astype(jnp.float32)
            for tap in range(1, TAPS):
                total = total + taps_ref[tap] * x_ref[i, f + tap].astype(jnp.float32)
            y = jnp.dot(
                first_ref[...], total, precision=lax.Precision.HIGHEST, preferred_element_type=jnp.float32
            )
            re, im = y[:64], y[64:]
            cos, sin = turn_ref[0], turn_ref[1]
            turned.append(jnp.concatenate([re * cos + im * sin, im * cos - re * sin], axis=1))
    z = jnp.concatenate(turned, axis=0)
    o = lax.dot_general(
        second_ref[...], z, (((1,), (1,)), ((), ())),
        precision=lax.Precision.HIGHEST, preferred_element_type=jnp.float32,
    )
    for p in range(2):
        for i in range(2):
            for f in range(2):
                at = (i * 2 + f) * 64
                even = o[p * 32 : p * 32 + 32, at : at + 64]
                odd = o[64 + p * 32 : 64 + p * 32 + 32, at : at + 64]
                s = jnp.concatenate([even, odd], axis=1)
                row = (p * 2 + f) * 2 + i
                for k in range(32):
                    lane = (k % 8) * 128
                    rows_ref[k // 8, row : row + 1, lane : lane + 128] = s[k : k + 1]
    for d in range(4):
        outs[d][...] = rows_ref[lax.rem(chan_ref[0] + d, 4)].astype(jnp.bfloat16)


def spectra(samples, chan):
    x = samples.reshape(2, 17, 2, 64, 128).transpose(0, 1, 3, 2, 4).reshape(2, 17, 128, 128)
    first, turn, second = transform_tables()
    return pl.pallas_call(
        spectra_kernel,
        out_shape=[jax.ShapeDtypeStruct((8, CH_WIN), jnp.bfloat16)] * 4,
        in_specs=[pl.BlockSpec(memory_space=HBM)] * 5 + [pl.BlockSpec(memory_space=SMEM)],
        out_specs=[pl.BlockSpec(memory_space=VMEM)] * 4,
        scratch_shapes=[
            pltpu.VMEM((2, 17, 128, 128), jnp.bfloat16),
            pltpu.VMEM((TAPS, 128, 128), jnp.float32),
            pltpu.VMEM((128, 128), jnp.float32),
            pltpu.VMEM((2, 64, 128), jnp.float32),
            pltpu.VMEM((128, 256), jnp.float32),
            pltpu.SemaphoreType.DMA((5,)),
            pltpu.VMEM((4, 8, CH_WIN), jnp.float32),
        ],
        compiler_params=pltpu.CompilerParams(vmem_limit_bytes=56 * MIB),
        name="spectra",
    )(x, jnp.asarray(filter_taps()), jnp.asarray(first), jnp.asarray(turn), jnp.asarray(second), chan)


def group_kernel(chan_ref, *refs):
    pieces, out_ref, wide_ref, rows_ref = refs[:4], refs[4], refs[5], refs[6]
    for d in range(4):
        wide_ref[d] = pieces[d][...].astype(jnp.float32)
    for source in range(4):
        piece = wide_ref[lax.rem(chan_ref[0] + 4 - source, 4)]
        for t in range(4):
            rows_ref[t, source * 2 : source * 2 + 2, :] = piece[t * 2 : t * 2 + 2]
    out_ref[...] = rows_ref[...].reshape(32, CH_WIN).astype(jnp.bfloat16)


def group_spectra(pieces, chan):
    return pl.pallas_call(
        group_kernel,
        out_shape=jax.ShapeDtypeStruct((32, CH_WIN), jnp.bfloat16),
        in_specs=[pl.BlockSpec(memory_space=SMEM)] + [pl.BlockSpec(memory_space=VMEM)] * 4,
        out_specs=pl.BlockSpec(memory_space=VMEM),
        scratch_shapes=[pltpu.VMEM((4, 8, CH_WIN), jnp.float32)] * 2,
        compiler_params=pltpu.CompilerParams(vmem_limit_bytes=8 * MIB),
        name="group_spectra",
    )(chan, *pieces)


def tiles_kernel(base, counts, aliased, *refs):
    slots_ref, own_ref = refs[:2]
    blocks = refs[2 : 2 + len(counts)]
    out_ref, wide_ref, tile_ref, sems = refs[2 + len(counts) + (1 if aliased else 0) :]
    own = own_ref[...].astype(jnp.float32) * 0.5
    for t in range(4):
        for i in range(8):
            wide_ref[i, t] = jnp.broadcast_to(own[t * 8 + i : t * 8 + i + 1], (8, CH_WIN))

    def copy_of(n):
        return pltpu.make_async_copy(tile_ref.at[n], out_ref.at[:, :, slots_ref[0, base + n]], sems.at[n])

    first = 0
    for block_ref, count in zip(blocks, counts, strict=True):

        @pl.loop(0, count)
        def _(index, block_ref=block_ref, first=first):
            n = first + index
            keep = slots_ref[1, base + n].astype(jnp.float32)

            @pl.loop(0, CH_WIN // 128, unroll=UNROLL)
            def _(step):
                lanes = pl.ds(pl.multiple_of(step * 128, 128), 128)
                other = block_ref[index, :, lanes].astype(jnp.float32) * keep
                r0, r1, i0, i1 = (other[t * 8 : t * 8 + 8] for t in range(4))
                for i in range(8):
                    a0, a1, b0, b1 = (wide_ref[i, t, :, lanes] for t in range(4))
                    tile_ref[n, i, 0, :, lanes] = ((a0 * r0 + a1 * r1) + (b0 * i0 + b1 * i1)).astype(jnp.bfloat16)
                    tile_ref[n, i, 1, :, lanes] = ((b0 * r0 + b1 * r1) - (a0 * i0 + a1 * i1)).astype(jnp.bfloat16)

            copy_of(n).start()

        first += count

    @pl.loop(0, first)
    def _(n):
        copy_of(n).wait()


def tiles(slots, base, own, blocks, result, n_slots):
    counts = [block.shape[0] for block in blocks]
    n = sum(counts)
    aliased = result is not None
    operands = [slots, own, *blocks] + ([result] if aliased else [])
    specs = [pl.BlockSpec(memory_space=SMEM)] + [pl.BlockSpec(memory_space=VMEM)] * (1 + len(blocks))
    specs += [pl.BlockSpec(memory_space=pl.ANY)] if aliased else []
    return pl.pallas_call(
        functools.partial(tiles_kernel, base, counts, aliased),
        out_shape=jax.ShapeDtypeStruct((8, 2, n_slots, 8, CH_WIN), jnp.bfloat16),
        in_specs=specs,
        out_specs=pl.BlockSpec(memory_space=pl.ANY),
        input_output_aliases={len(operands) - 1: 0} if aliased else {},
        scratch_shapes=[
            pltpu.VMEM((8, 4, 8, CH_WIN), jnp.float32),
            pltpu.VMEM((n, 8, 2, 8, CH_WIN), jnp.bfloat16),
            pltpu.SemaphoreType.DMA((n,)),
        ],
        compiler_params=pltpu.CompilerParams(vmem_limit_bytes=16 * MIB),
        cost_estimate=pl.CostEstimate(flops=n * 5 * 10**7, bytes_accessed=n * 300_000, transcendentals=0),
        name="tiles",
    )(*operands)


def move(array, target):
    places = [(z, y, x) for z in range(N_Z) for y in range(N_Y) for x in range(N_X)]

    def number(z, y, x):
        return (z % N_Z * N_Y + y % N_Y) * N_X + x % N_X

    return lax.ppermute(array, "stn", [(number(*p), number(*target(*p))) for p in places])


def along_z(array, step):
    return move(array, lambda z, y, x: (z + step, y, x))


def across_y(array):
    return move(array, lambda z, y, x: (z, 1 - y, x))


def swap_x(array, mask):
    return move(array, lambda z, y, x: (z, y, x ^ mask))


def per_device(samples, keeper):
    group = lax.axis_index("stn")
    chan = lax.axis_index("chan")
    z, y, x = group // (N_Y * N_X), group // N_X % N_Y, group % N_X
    n_slots = 33

    chan_scalar = chan.astype(jnp.int32).reshape(1)
    pieces = [
        part if d == 0 else lax.ppermute(part, "chan", [(c, (c + d) % 4) for c in range(4)])
        for d, part in enumerate(spectra(samples, chan_scalar))
    ]
    own = group_spectra(pieces, chan_scalar)

    z4, z3, z2, z1 = (along_z(own, step) for step in (4, 3, 2, 1))
    za = jnp.stack([z1, z2])

    def where_from(back, other, mask):
        ry = 1 - y if other else y
        rx = x ^ mask
        if back is None:
            back = jnp.where(ry * N_X + rx < y * N_X + x, 0, 4)
        return ((z - back) % N_Z) * (N_Y * N_X) + ry * N_X + rx

    def froms_a(mask):
        return [(1, 0, mask), (2, 0, mask), (1, 1, mask), (2, 1, mask)]

    froms = [
        [(0, 0, 0)],
        froms_a(0),
        [(3, 0, 0), (4, 0, 0), (3, 1, 0), (None, 1, 0)],
        froms_a(1) + froms_a(3),
        froms_a(2)
        + [(3, 1, 1), (None, 1, 1), (3, 0, 1), (None, 0, 1), (3, 0, 3), (None, 0, 3), (3, 1, 3), (None, 1, 3)],
        [(3, 0, 2), (None, 0, 2), (3, 1, 2), (None, 1, 2)],
    ]
    origin = jnp.stack([where_from(*o) for some in froms for o in some]).astype(jnp.int32)
    keep_row = lax.dynamic_index_in_dim(keeper, group, 0, keepdims=False)
    columns = jnp.arange(keeper.shape[1], dtype=jnp.int32)[None, :]
    rank = jnp.sum(jnp.where(columns < origin[:, None], keep_row[None, :], 0), axis=1)
    kept = jnp.sum(jnp.where(columns == origin[:, None], keep_row[None, :], 0), axis=1)
    slots = jnp.stack([jnp.where(kept == 1, rank, n_slots - 1), kept]).astype(jnp.int32)

    bases = [sum(map(len, froms[:n])) for n in range(len(froms))]

    def add(call, blocks, result):
        return tiles(slots, bases[call], own, blocks, result, n_slots)

    result = add(0, [own[None]], None)
    za, result = lax.optimization_barrier((za, result))
    ya = across_y(za)
    a = jnp.concatenate([za, ya])
    a1, a3 = swap_x(a, 1), swap_x(a, 3)
    result = add(1, [za, ya], result)
    s1, s3, sy = (jnp.where(here, own, z4) for here in (x % 2 == 0, x < 2, y == 0))
    yb = across_y(jnp.stack([z3, sy]))
    yb, result = lax.optimization_barrier((yb, result))
    b1 = swap_x(jnp.concatenate([yb, jnp.stack([z3, s1])]), 1)
    b3 = swap_x(jnp.concatenate([jnp.stack([z3, s3]), yb]), 3)
    result = add(2, [z3[None], z4[None], yb], result)
    a1, a3, result = lax.optimization_barrier((a1, a3, result))
    ar1, ar3 = swap_x(a3[:2], 1), swap_x(a1[2:], 3)
    result = add(3, [a1, a3], result)
    b1, b3, result = lax.optimization_barrier((b1, b3, result))
    br1, br3 = swap_x(b3[:2], 1), swap_x(b1[:2], 3)
    result = add(4, [ar1, ar3, b1, b3], result)
    result = add(5, [br1, br3], result)
    return result.reshape(8, 2, n_slots * 8, CH_WIN).swapaxes(2, 3)


def solution(mesh):
    return jax.shard_map(
        per_device,
        mesh=mesh,
        in_specs=(P(("stn", "chan"), None, None, None), P()),
        out_specs=P("stn", None, "chan", None),
        check_vma=False,
    )
```

time: 70 us -> 59.1 us (0.84)
  the two profiles are of different devices: /device:TPU:6 before, /device:TPU:8 now
where the time goes in v2:
time: 59.1 us; the launch traced here: 59 us
  starting transfers between devices  27.4 us (46%)
  Pallas kernels  16.8 us (28%)
  waiting for transfers between devices  13.2 us (22%)
  local copies, waits for them, and re-layouts  0.91 us (2%)
    ppermute x14, starting transfers between devices, move(): lax.ppermute(array, 'stn', [(number(*p), number(*target(*p))) for p in pl...  23.7 us
    pallas_call x6, Pallas kernels, tiles(): pl.pallas_call(functools.partial(tiles_kernel, base, counts, aliased), ou...  13.4 us
    ppermute x14, waiting for transfers between devices, move(): lax.ppermute(array, 'stn', [(number(*p), number(*target(*p))) for p in pl...  11.9 us
    ppermute x3, starting transfers between devices, per_device(): lax.ppermute(part, 'chan', [(c, (c + d) % 4) for c in range(4)])  3.72 us
    pallas_call x1, Pallas kernels, spectra(): pl.pallas_call(spectra_kernel, out_shape=[jax.ShapeDtypeStruct((8, CH_WIN...  3.38 us
    ppermute x3, waiting for transfers between devices, per_device(): lax.ppermute(part, 'chan', [(c, (c + d) % 4) for c in range(4)])  1.29 us
  transfers between devices with their start and end apart: 17, of which 7 were waited for; matrix products, arithmetic and copies ran while one was open for 1% of the time, Pallas kernels for 19%

profile of v2, /device:TPU:8, one launch (start us, length us, event | category | flops | bytes accessed | tf_op | source)
XLA Modules:
  0.0 59.0 jit_solution(11530777859556931400)
XLA Ops:
  0.0 3.4 %spectra.1 = (bf16[8,1024]{1,0:T(8,128)(2,1)}, bf16[8,1024]{1,0:T(8,128)(2,1)}, bf16[8,1024]{1,0:T(8,128)(2,1)}, bf16[8,1024]{1,0:T(8,128)(2,1)}) custom-call(bf16[2,17,128,128]{3,2,1,0:T(8,128)(2,1)} %bitcast.64, f32[16,128,128]{2,1,0:T(8,128)} %constant.177.clone.refs_1_, f32[128,128]{1,0:T(8,128)} %constant.178.clone.refs_2_, ...), custom_call_target="tpu_custom_call" | custom-call | tf_op jit(solution)/shard_map/spectra/pallas_call | solution.py:97
  3.5 2.3 %collective-permute-start.1 = (bf16[8,1024]{1,0:T(8,128)(2,1)}, bf16[8,1024]{1,0:T(8,128)(2,1)S(1)}, u32[]{:S(2)}, u32[]{:S(2)}) collective-permute-start(bf16[8,1024]{1,0:T(8,128)(2,1)} %get-tuple-element.21), channel_id=1, source_target_pairs={{0,2},{1,3},{2,0},{3,1},{4,6},{5,7},{6,4},{7,5},{8,10},{9,11},{10,... | collective-permute-start | bytes 49160 | tf_op jit(solution)/shard_map/ppermute | solution.py:231
  5.8 1.4 %collective-permute-start.2 = (bf16[8,1024]{1,0:T(8,128)(2,1)}, bf16[8,1024]{1,0:T(8,128)(2,1)S(1)}, u32[]{:S(2)}, u32[]{:S(2)}) collective-permute-start(bf16[8,1024]{1,0:T(8,128)(2,1)} %get-tuple-element.22), channel_id=1, source_target_pairs={{0,3},{1,0},{2,1},{3,2},{4,7},{5,4},{6,5},{7,6},{8,11},{9,8},{10,9... | collective-permute-start | bytes 49160 | tf_op jit(solution)/shard_map/ppermute | solution.py:231
  7.1 0.1 stack.166
  7.3 0.2 select_reduce_fusion
  7.5 0.2 collective-permute-done.1.refs_2_
  7.7 1.1 %collective-permute-done.2.refs_3_ = bf16[8,1024]{1,0:T(8,128)(2,1)S(1)} collective-permute-done((bf16[8,1024]{1,0:T(8,128)(2,1)}, bf16[8,1024]{1,0:T(8,128)(2,1)S(1)}, u32[]{:S(2)}, u32[]{:S(2)}) %collective-permute-start.2) | collective-permute-done | bytes 16416 | tf_op jit(solution)/shard_map/ppermute | solution.py:231
  8.8 0.7 %copy-done.1 = bf16[8,1024]{1,0:T(8,128)(2,1)S(1)} copy-done((bf16[8,1024]{1,0:T(8,128)(2,1)S(1)}, bf16[8,1024]{1,0:T(8,128)(2,1)}, u32[]{:S(2)}) %copy-start.1) | copy-done | bytes 16408
  9.6 0.7 %collective-permute-start.6 = (bf16[32,1024]{1,0:T(8,128)(2,1)S(1)}, bf16[32,1024]{1,0:T(8,128)(2,1)S(1)}, u32[]{:S(2)}, u32[]{:S(2)}) collective-permute-start(bf16[32,1024]{1,0:T(8,128)(2,1)S(1)} %group_spectra.1.refs_1_), channel_id=1, source_target_pairs={{0,32},{4,36},{8,40},{12,44},{16,48},{20,52},{24,56},{28,60},{32,6... | collective-permute-start | bytes 196616 | tf_op jit(solution)/shard_map/ppermute | solution.py:208
  10.3 3.3 %collective-permute-start.7 = (bf16[32,1024]{1,0:T(8,128)(2,1)S(1)}, bf16[32,1024]{1,0:T(8,128)(2,1)S(1)}, u32[]{:S(2)}, u32[]{:S(2)}) collective-permute-start(bf16[32,1024]{1,0:T(8,128)(2,1)S(1)} %group_spectra.1.refs_1_), channel_id=1, source_target_pairs={{0,64},{4,68},{8,72},{12,76},{16,80},{20,84},{24,88},{28,92},{32,9... | collective-permute-start | bytes 196616 | tf_op jit(solution)/shard_map/ppermute | solution.py:208
  13.6 4.5 %collective-permute-start.4 = (bf16[32,1024]{1,0:T(8,128)(2,1)S(1)}, bf16[32,1024]{1,0:T(8,128)(2,1)S(1)}, u32[]{:S(2)}, u32[]{:S(2)}) collective-permute-start(bf16[32,1024]{1,0:T(8,128)(2,1)S(1)} %group_spectra.1.refs_1_), channel_id=1, source_target_pairs={{0,128},{4,132},{8,136},{12,140},{16,144},{20,148},{24,152},{28,15... | collective-permute-start | bytes 196616 | tf_op jit(solution)/shard_map/ppermute | solution.py:208
  18.2 1.4 %tiles.6.refs_4_ = bf16[8,2,33,8,1024]{4,3,2,1,0:T(8,128)(2,1)} custom-call(s32[2,33]{1,0:T(2,128)S(1)} %pad_add_fusion.refs_0_, bf16[32,1024]{1,0:T(8,128)(2,1)S(1)} %group_spectra.1.refs_1_, bf16[1,32,1024]{2,1,0:T(8,128)(2,1)S(1)} %bitcast.59), custom_call_target="tpu_custom_call" | custom-call | flops 50000000 | bytes 300000 | tf_op jit(solution)/shard_map/tiles/pallas_call | solution.py:185
  19.6 0.8 %collective-permute-done.7 = bf16[32,1024]{1,0:T(8,128)(2,1)S(1)} collective-permute-done((bf16[32,1024]{1,0:T(8,128)(2,1)S(1)}, bf16[32,1024]{1,0:T(8,128)(2,1)S(1)}, u32[]{:S(2)}, u32[]{:S(2)}) %collective-permute-start.7) | collective-permute-done | bytes 65568 | tf_op jit(solution)/shard_map/ppermute | solution.py:208
  20.4 2.4 %collective-permute-start.8 = (bf16[2,32,1024]{2,1,0:T(8,128)(2,1)S(1)}, bf16[2,32,1024]{2,1,0:T(8,128)(2,1)S(1)}, u32[]{:S(2)}, u32[]{:S(2)}) collective-permute-start(bf16[2,32,1024]{2,1,0:T(8,128)(2,1)S(1)} %pad_maximum_fusion.3.refs_2_), channel_id=1, source_target_pairs={{0,16},{4,20},{8,24},{12,28},{16,0},{20,4},{24,8},{28,12},{32,48},... | collective-permute-start | bytes 393224 | tf_op jit(solution)/shard_map/ppermute | solution.py:208
  22.8 1.0 %collective-permute-done.4 = bf16[32,1024]{1,0:T(8,128)(2,1)S(1)} collective-permute-done((bf16[32,1024]{1,0:T(8,128)(2,1)S(1)}, bf16[32,1024]{1,0:T(8,128)(2,1)S(1)}, u32[]{:S(2)}, u32[]{:S(2)}) %collective-permute-start.4) | collective-permute-done | bytes 65568 | tf_op jit(solution)/shard_map/ppermute | solution.py:208
  23.8 5.7 %collective-permute-done.3 = bf16[32,1024]{1,0:T(8,128)(2,1)S(1)} collective-permute-done((bf16[32,1024]{1,0:T(8,128)(2,1)S(1)}, bf16[32,1024]{1,0:T(8,128)(2,1)S(1)}, u32[]{:S(2)}, u32[]{:S(2)}) %collective-permute-start.3) | collective-permute-done | bytes 65568 | tf_op jit(solution)/shard_map/ppermute | solution.py:208
  29.5 2.4 %collective-permute-start.5 = (bf16[2,32,1024]{2,1,0:T(8,128)(2,1)S(1)}, bf16[2,32,1024]{2,1,0:T(8,128)(2,1)S(1)}, u32[]{:S(2)}, u32[]{:S(2)}) collective-permute-start(bf16[2,32,1024]{2,1,0:T(8,128)(2,1)S(1)} %pad_maximum_fusion.2), channel_id=1, source_target_pairs={{0,16},{4,20},{8,24},{12,28},{16,0},{20,4},{24,8},{28,12},{32,48},... | collective-permute-start | bytes 393224 | tf_op jit(solution)/shard_map/ppermute | solution.py:208
  31.9 1.6 %collective-permute-start.11 = (bf16[4,32,1024]{2,1,0:T(8,128)(2,1)S(1)}, bf16[4,32,1024]{2,1,0:T(8,128)(2,1)S(1)}, u32[]{:S(2)}, u32[]{:S(2)}) collective-permute-start(bf16[4,32,1024]{2,1,0:T(8,128)(2,1)S(1)} %constant_dynamic-update-slice_fusion), channel_id=1, source_target_pairs={{0,4},{4,0},{8,12},{12,8},{16,20},{20,16},{24,28},{28,24},{32,36},... | collective-permute-start | bytes 786440 | tf_op jit(solution)/shard_map/ppermute | solution.py:208
  33.5 2.0 %collective-permute-start.12 = (bf16[4,32,1024]{2,1,0:T(8,128)(2,1)S(1)}, bf16[4,32,1024]{2,1,0:T(8,128)(2,1)S(1)}, u32[]{:S(2)}, u32[]{:S(2)}) collective-permute-start(bf16[4,32,1024]{2,1,0:T(8,128)(2,1)S(1)} %constant_dynamic-update-slice_fusion), channel_id=1, source_target_pairs={{0,12},{4,8},{8,4},{12,0},{16,28},{20,24},{24,20},{28,16},{32,44},... | collective-permute-start | bytes 786440 | tf_op jit(solution)/shard_map/ppermute | solution.py:208
  35.5 2.0 %tiles.7.refs_5_ = bf16[8,2,33,8,1024]{4,3,2,1,0:T(8,128)(2,1)} custom-call(s32[2,33]{1,0:T(2,128)S(1)} %pad_add_fusion.refs_0_, bf16[32,1024]{1,0:T(8,128)(2,1)S(1)} %group_spectra.1.refs_1_, bf16[2,32,1024]{2,1,0:T(8,128)(2,1)S(1)} %pad_maximum_fusion.3.refs_2_, ...), custom_call_target="tpu_custom_call", output_to_operand_aliasing={{}: (4, {})} | custom-call | flops 200000000 | bytes 1200000 | tf_op jit(solution)/shard_map/tiles/pallas_call | solution.py:185
  37.6 1.4 %collective-permute-start.10 = (bf16[4,32,1024]{2,1,0:T(8,128)(2,1)S(1)}, bf16[4,32,1024]{2,1,0:T(8,128)(2,1)S(1)}, u32[]{:S(2)}, u32[]{:S(2)}) collective-permute-start(bf16[4,32,1024]{2,1,0:T(8,128)(2,1)S(1)} %get-tuple-element.35), channel_id=1, source_target_pairs={{0,12},{4,8},{8,4},{12,0},{16,28},{20,24},{24,20},{28,16},{32,44},... | collective-permute-start | bytes 786440 | tf_op jit(solution)/shard_map/ppermute | solution.py:208
  38.9 0.2 collective-permute-start.9
  39.2 2.0 %tiles.8.refs_4_ = bf16[8,2,33,8,1024]{4,3,2,1,0:T(8,128)(2,1)} custom-call(s32[2,33]{1,0:T(2,128)S(1)} %pad_add_fusion.refs_0_, bf16[32,1024]{1,0:T(8,128)(2,1)S(1)} %group_spectra.1.refs_1_, bf16[1,32,1024]{2,1,0:T(8,128)(2,1)S(1)} %bitcast.62, bf16[1,32,1024]{2,1,0:T(8,128)(2,1)S(1)} %bitcast.63, ...), custom_call_target="tpu_custom_call", output_to_operand_aliasing={{}: (5, {})} | custom-call | flops 200000000 | bytes 1200000 | tf_op jit(solution)/shard_map/tiles/pallas_call | solution.py:185
  41.1 2.4 %collective-permute-done.12.refs_3_ = bf16[4,32,1024]{2,1,0:T(8,128)(2,1)S(1)} collective-permute-done((bf16[4,32,1024]{2,1,0:T(8,128)(2,1)S(1)}, bf16[4,32,1024]{2,1,0:T(8,128)(2,1)S(1)}, u32[]{:S(2)}, u32[]{:S(2)}) %collective-permute-start.12) | collective-permute-done | bytes 262176 | tf_op jit(solution)/shard_map/ppermute | solution.py:208
  43.5 0.1 collective-permute-start.15
  43.6 2.8 %collective-permute-start.16 = (bf16[2,32,1024]{2,1,0:T(8,128)(2,1)S(1)}, bf16[2,32,1024]{2,1,0:T(8,128)(2,1)S(1)}, u32[]{:S(2)}, u32[]{:S(2)}) collective-permute-start(bf16[2,32,1024]{2,1,0:T(8,128)(2,1)S(1)} %slice.15), channel_id=1, source_target_pairs={{0,12},{4,8},{8,4},{12,0},{16,28},{20,24},{24,20},{28,16},{32,44},... | collective-permute-start | bytes 393224 | tf_op jit(solution)/shard_map/ppermute | solution.py:208
  46.4 2.7 %tiles.9.refs_6_ = bf16[8,2,33,8,1024]{4,3,2,1,0:T(8,128)(2,1)} custom-call(s32[2,33]{1,0:T(2,128)S(1)} %pad_add_fusion.refs_0_, bf16[32,1024]{1,0:T(8,128)(2,1)S(1)} %group_spectra.1.refs_1_, bf16[4,32,1024]{2,1,0:T(8,128)(2,1)S(1)} %collective-permute-done.11.refs_2_, ...), custom_call_target="tpu_custom_call", output_to_operand_aliasing={{}: (4, {})} | custom-call | flops 400000000 | bytes 2400000 | tf_op jit(solution)/shard_map/tiles/pallas_call | solution.py:185
  49.1 1.4 %collective-permute-start.13 = (bf16[2,32,1024]{2,1,0:T(8,128)(2,1)S(1)}, bf16[2,32,1024]{2,1,0:T(8,128)(2,1)S(1)}, u32[]{:S(2)}, u32[]{:S(2)}) collective-permute-start(bf16[2,32,1024]{2,1,0:T(8,128)(2,1)S(1)} %slice.12), channel_id=1, source_target_pairs={{0,4},{4,0},{8,12},{12,8},{16,20},{20,16},{24,28},{28,24},{32,36},... | collective-permute-start | bytes 393224 | tf_op jit(solution)/shard_map/ppermute | solution.py:208
  50.6 0.9 %collective-permute-start.14 = (bf16[2,32,1024]{2,1,0:T(8,128)(2,1)S(1)}, bf16[2,32,1024]{2,1,0:T(8,128)(2,1)S(1)}, u32[]{:S(2)}, u32[]{:S(2)}) collective-permute-start(bf16[2,32,1024]{2,1,0:T(8,128)(2,1)S(1)} %slice.13), channel_id=1, source_target_pairs={{0,12},{4,8},{8,4},{12,0},{16,28},{20,24},{24,20},{28,16},{32,44},... | collective-permute-start | bytes 393224 | tf_op jit(solution)/shard_map/ppermute | solution.py:208
  51.4 3.3 %tiles.10.refs_4_ = bf16[8,2,33,8,1024]{4,3,2,1,0:T(8,128)(2,1)} custom-call(s32[2,33]{1,0:T(2,128)S(1)} %pad_add_fusion.refs_0_, bf16[32,1024]{1,0:T(8,128)(2,1)S(1)} %group_spectra.1.refs_1_, bf16[2,32,1024]{2,1,0:T(8,128)(2,1)S(1)} %collective-permute-done.15.refs_2_, ...), custom_call_target="tpu_custom_call", output_to_operand_aliasing={{}: (6, {})} | custom-call | flops 600000000 | bytes 3600000 | tf_op jit(solution)/shard_map/tiles/pallas_call | solution.py:185
  54.8 2.1 %collective-permute-done.14.refs_3_ = bf16[2,32,1024]{2,1,0:T(8,128)(2,1)S(1)} collective-permute-done((bf16[2,32,1024]{2,1,0:T(8,128)(2,1)S(1)}, bf16[2,32,1024]{2,1,0:T(8,128)(2,1)S(1)}, u32[]{:S(2)}, u32[]{:S(2)}) %collective-permute-start.14) | collective-permute-done | bytes 131104 | tf_op jit(solution)/shard_map/ppermute | solution.py:208
  56.8 2.0 %tiles.11 = bf16[8,2,33,8,1024]{4,3,2,1,0:T(8,128)(2,1)} custom-call(s32[2,33]{1,0:T(2,128)S(1)} %pad_add_fusion.refs_0_, bf16[32,1024]{1,0:T(8,128)(2,1)S(1)} %group_spectra.1.refs_1_, bf16[2,32,1024]{2,1,0:T(8,128)(2,1)S(1)} %collective-permute-done.13.refs_2_, ...), custom_call_target="tpu_custom_call", output_to_operand_aliasing={{}: (4, {})} | custom-call | flops 200000000 | bytes 1200000 | tf_op jit(solution)/shard_map/tiles/pallas_call | solution.py:185
  (29 shorter events, 0.4 us)
Async XLA Ops:
  0.0 7.1 %copy-start = (s32[64,64]{1,0:T(8,128)S(1)}, s32[64,64]{1,0:T(8,128)}, u32[]{:S(2)}) copy-start(s32[64,64]{1,0:T(8,128)} %param.7) | copy-start | bytes 49156
  3.4 4.1 %collective-permute-start = (bf16[8,1024]{1,0:T(8,128)(2,1)}, bf16[8,1024]{1,0:T(8,128)(2,1)S(1)}, u32[]{:S(2)}, u32[]{:S(2)}) collective-permute-start(bf16[8,1024]{1,0:T(8,128)(2,1)} %get-tuple-element.20), channel_id=1, source_target_pairs={{0,1},{1,2},{2,3},{3,0},{4,5},{5,6},{6,7},{7,4},{8,9},{9,10},{10,1... | collective-permute-start | bytes 49160 | tf_op jit(solution)/shard_map/ppermute | solution.py:231
  3.5 4.2 %collective-permute-start.1 = (bf16[8,1024]{1,0:T(8,128)(2,1)}, bf16[8,1024]{1,0:T(8,128)(2,1)S(1)}, u32[]{:S(2)}, u32[]{:S(2)}) collective-permute-start(bf16[8,1024]{1,0:T(8,128)(2,1)} %get-tuple-element.21), channel_id=1, source_target_pairs={{0,2},{1,3},{2,0},{3,1},{4,6},{5,7},{6,4},{7,5},{8,10},{9,11},{10,... | collective-permute-start | bytes 49160 | tf_op jit(solution)/shard_map/ppermute | solution.py:231
  5.8 3.0 %collective-permute-start.2 = (bf16[8,1024]{1,0:T(8,128)(2,1)}, bf16[8,1024]{1,0:T(8,128)(2,1)S(1)}, u32[]{:S(2)}, u32[]{:S(2)}) collective-permute-start(bf16[8,1024]{1,0:T(8,128)(2,1)} %get-tuple-element.22), channel_id=1, source_target_pairs={{0,3},{1,0},{2,1},{3,2},{4,7},{5,4},{6,5},{7,6},{8,11},{9,8},{10,9... | collective-permute-start | bytes 49160 | tf_op jit(solution)/shard_map/ppermute | solution.py:231
  8.8 0.7 %copy-start.1 = (bf16[8,1024]{1,0:T(8,128)(2,1)S(1)}, bf16[8,1024]{1,0:T(8,128)(2,1)}, u32[]{:S(2)}) copy-start(bf16[8,1024]{1,0:T(8,128)(2,1)} %get-tuple-element.19.refs_0_) | copy-start | bytes 49156
  9.6 10.1 %collective-permute-start.6 = (bf16[32,1024]{1,0:T(8,128)(2,1)S(1)}, bf16[32,1024]{1,0:T(8,128)(2,1)S(1)}, u32[]{:S(2)}, u32[]{:S(2)}) collective-permute-start(bf16[32,1024]{1,0:T(8,128)(2,1)S(1)} %group_spectra.1.refs_1_), channel_id=1, source_target_pairs={{0,32},{4,36},{8,40},{12,44},{16,48},{20,52},{24,56},{28,60},{32,6... | collective-permute-start | bytes 196616 | tf_op jit(solution)/shard_map/ppermute | solution.py:208
  10.3 10.1 %collective-permute-start.7 = (bf16[32,1024]{1,0:T(8,128)(2,1)S(1)}, bf16[32,1024]{1,0:T(8,128)(2,1)S(1)}, u32[]{:S(2)}, u32[]{:S(2)}) collective-permute-start(bf16[32,1024]{1,0:T(8,128)(2,1)S(1)} %group_spectra.1.refs_1_), channel_id=1, source_target_pairs={{0,64},{4,68},{8,72},{12,76},{16,80},{20,84},{24,88},{28,92},{32,9... | collective-permute-start | bytes 196616 | tf_op jit(solution)/shard_map/ppermute | solution.py:208
  13.6 10.2 %collective-permute-start.4 = (bf16[32,1024]{1,0:T(8,128)(2,1)S(1)}, bf16[32,1024]{1,0:T(8,128)(2,1)S(1)}, u32[]{:S(2)}, u32[]{:S(2)}) collective-permute-start(bf16[32,1024]{1,0:T(8,128)(2,1)S(1)} %group_spectra.1.refs_1_), channel_id=1, source_target_pairs={{0,128},{4,132},{8,136},{12,140},{16,144},{20,148},{24,152},{28,15... | collective-permute-start | bytes 196616 | tf_op jit(solution)/shard_map/ppermute | solution.py:208
  18.1 11.4 %collective-permute-start.3 = (bf16[32,1024]{1,0:T(8,128)(2,1)S(1)}, bf16[32,1024]{1,0:T(8,128)(2,1)S(1)}, u32[]{:S(2)}, u32[]{:S(2)}) collective-permute-start(bf16[32,1024]{1,0:T(8,128)(2,1)S(1)} %group_spectra.1.refs_1_), channel_id=1, source_target_pairs={{0,96},{4,100},{8,104},{12,108},{16,112},{20,116},{24,120},{28,124... | collective-permute-start | bytes 196616 | tf_op jit(solution)/shard_map/ppermute | solution.py:208
  20.4 11.5 %collective-permute-start.8 = (bf16[2,32,1024]{2,1,0:T(8,128)(2,1)S(1)}, bf16[2,32,1024]{2,1,0:T(8,128)(2,1)S(1)}, u32[]{:S(2)}, u32[]{:S(2)}) collective-permute-start(bf16[2,32,1024]{2,1,0:T(8,128)(2,1)S(1)} %pad_maximum_fusion.3.refs_2_), channel_id=1, source_target_pairs={{0,16},{4,20},{8,24},{12,28},{16,0},{20,4},{24,8},{28,12},{32,48},... | collective-permute-start | bytes 393224 | tf_op jit(solution)/shard_map/ppermute | solution.py:208
  29.5 8.0 %collective-permute-start.5 = (bf16[2,32,1024]{2,1,0:T(8,128)(2,1)S(1)}, bf16[2,32,1024]{2,1,0:T(8,128)(2,1)S(1)}, u32[]{:S(2)}, u32[]{:S(2)}) collective-permute-start(bf16[2,32,1024]{2,1,0:T(8,128)(2,1)S(1)} %pad_maximum_fusion.2), channel_id=1, source_target_pairs={{0,16},{4,20},{8,24},{12,28},{16,0},{20,4},{24,8},{28,12},{32,48},... | collective-permute-start | bytes 393224 | tf_op jit(solution)/shard_map/ppermute | solution.py:208
  31.9 9.2 %collective-permute-start.11 = (bf16[4,32,1024]{2,1,0:T(8,128)(2,1)S(1)}, bf16[4,32,1024]{2,1,0:T(8,128)(2,1)S(1)}, u32[]{:S(2)}, u32[]{:S(2)}) collective-permute-start(bf16[4,32,1024]{2,1,0:T(8,128)(2,1)S(1)} %constant_dynamic-update-slice_fusion), channel_id=1, source_target_pairs={{0,4},{4,0},{8,12},{12,8},{16,20},{20,16},{24,28},{28,24},{32,36},... | collective-permute-start | bytes 786440 | tf_op jit(solution)/shard_map/ppermute | solution.py:208
  33.5 10.0 %collective-permute-start.12 = (bf16[4,32,1024]{2,1,0:T(8,128)(2,1)S(1)}, bf16[4,32,1024]{2,1,0:T(8,128)(2,1)S(1)}, u32[]{:S(2)}, u32[]{:S(2)}) collective-permute-start(bf16[4,32,1024]{2,1,0:T(8,128)(2,1)S(1)} %constant_dynamic-update-slice_fusion), channel_id=1, source_target_pairs={{0,12},{4,8},{8,4},{12,0},{16,28},{20,24},{24,20},{28,16},{32,44},... | collective-permute-start | bytes 786440 | tf_op jit(solution)/shard_map/ppermute | solution.py:208
  37.6 11.5 %collective-permute-start.10 = (bf16[4,32,1024]{2,1,0:T(8,128)(2,1)S(1)}, bf16[4,32,1024]{2,1,0:T(8,128)(2,1)S(1)}, u32[]{:S(2)}, u32[]{:S(2)}) collective-permute-start(bf16[4,32,1024]{2,1,0:T(8,128)(2,1)S(1)} %get-tuple-element.35), channel_id=1, source_target_pairs={{0,12},{4,8},{8,4},{12,0},{16,28},{20,24},{24,20},{28,16},{32,44},... | collective-permute-start | bytes 786440 | tf_op jit(solution)/shard_map/ppermute | solution.py:208
  38.9 10.1 %collective-permute-start.9 = (bf16[4,32,1024]{2,1,0:T(8,128)(2,1)S(1)}, bf16[4,32,1024]{2,1,0:T(8,128)(2,1)S(1)}, u32[]{:S(2)}, u32[]{:S(2)}) collective-permute-start(bf16[4,32,1024]{2,1,0:T(8,128)(2,1)S(1)} %get-tuple-element.36), channel_id=1, source_target_pairs={{0,4},{4,0},{8,12},{12,8},{16,20},{20,16},{24,28},{28,24},{32,36},... | collective-permute-start | bytes 786440 | tf_op jit(solution)/shard_map/ppermute | solution.py:208
  43.5 7.9 %collective-permute-start.15 = (bf16[2,32,1024]{2,1,0:T(8,128)(2,1)S(1)}, bf16[2,32,1024]{2,1,0:T(8,128)(2,1)S(1)}, u32[]{:S(2)}, u32[]{:S(2)}) collective-permute-start(bf16[2,32,1024]{2,1,0:T(8,128)(2,1)S(1)} %slice.14), channel_id=1, source_target_pairs={{0,4},{4,0},{8,12},{12,8},{16,20},{20,16},{24,28},{28,24},{32,36},... | collective-permute-start | bytes 393224 | tf_op jit(solution)/shard_map/ppermute | solution.py:208
  43.6 7.8 %collective-permute-start.16 = (bf16[2,32,1024]{2,1,0:T(8,128)(2,1)S(1)}, bf16[2,32,1024]{2,1,0:T(8,128)(2,1)S(1)}, u32[]{:S(2)}, u32[]{:S(2)}) collective-permute-start(bf16[2,32,1024]{2,1,0:T(8,128)(2,1)S(1)} %slice.15), channel_id=1, source_target_pairs={{0,12},{4,8},{8,4},{12,0},{16,28},{20,24},{24,20},{28,16},{32,44},... | collective-permute-start | bytes 393224 | tf_op jit(solution)/shard_map/ppermute | solution.py:208
  49.1 5.7 %collective-permute-start.13 = (bf16[2,32,1024]{2,1,0:T(8,128)(2,1)S(1)}, bf16[2,32,1024]{2,1,0:T(8,128)(2,1)S(1)}, u32[]{:S(2)}, u32[]{:S(2)}) collective-permute-start(bf16[2,32,1024]{2,1,0:T(8,128)(2,1)S(1)} %slice.12), channel_id=1, source_target_pairs={{0,4},{4,0},{8,12},{12,8},{16,20},{20,16},{24,28},{28,24},{32,36},... | collective-permute-start | bytes 393224 | tf_op jit(solution)/shard_map/ppermute | solution.py:208
  50.6 6.3 %collective-permute-start.14 = (bf16[2,32,1024]{2,1,0:T(8,128)(2,1)S(1)}, bf16[2,32,1024]{2,1,0:T(8,128)(2,1)S(1)}, u32[]{:S(2)}, u32[]{:S(2)}) collective-permute-start(bf16[2,32,1024]{2,1,0:T(8,128)(2,1)S(1)} %slice.13), channel_id=1, source_target_pairs={{0,12},{4,8},{8,4},{12,0},{16,28},{20,24},{24,20},{28,16},{32,44},... | collective-permute-start | bytes 393224 | tf_op jit(solution)/shard_map/ppermute | solution.py:208

commit v3 on v2

--- a/solution.py
+++ b/solution.py
@@ -194,7 +194,7 @@
             pltpu.SemaphoreType.DMA((n,)),
         ],
         compiler_params=pltpu.CompilerParams(vmem_limit_bytes=16 * MIB),
-        cost_estimate=pl.CostEstimate(flops=n * 5 * 10**7, bytes_accessed=n * 300_000, transcendentals=0),
+        cost_estimate=pl.CostEstimate(flops=n * 10**5, bytes_accessed=n, transcendentals=0),
         name="tiles",
     )(*operands)
 
@@ -231,9 +231,11 @@
         part if d == 0 else lax.ppermute(part, "chan", [(c, (c + d) % 4) for c in range(4)])
         for d, part in enumerate(spectra(samples, chan_scalar))
     ]
+    pieces[0] = jnp.where(chan < 4, pieces[0], jnp.zeros((), jnp.bfloat16))
     own = group_spectra(pieces, chan_scalar)
 
-    z4, z3, z2, z1 = (along_z(own, step) for step in (4, 3, 2, 1))
+    z3, z2, z1 = (along_z(own, step) for step in (3, 2, 1))
+    z4 = along_z(along_z(own, -2), -2)
     za = jnp.stack([z1, z2])
 
     def where_from(back, other, mask):
@@ -247,9 +249,7 @@
         return [(1, 0, mask), (2, 0, mask), (1, 1, mask), (2, 1, mask)]
 
     froms = [
-        [(0, 0, 0)],
-        froms_a(0),
-        [(3, 0, 0), (4, 0, 0), (3, 1, 0), (None, 1, 0)],
+        [(0, 0, 0)] + froms_a(0) + [(3, 0, 0), (4, 0, 0), (3, 1, 0), (None, 1, 0)],
         froms_a(1) + froms_a(3),
         froms_a(2)
         + [(3, 1, 1), (None, 1, 1), (3, 0, 1), (None, 0, 1), (3, 0, 3), (None, 0, 3), (3, 1, 3), (None, 1, 3)],
@@ -267,25 +267,21 @@
     def add(call, blocks, result):
         return tiles(slots, bases[call], own, blocks, result, n_slots)
 
-    result = add(0, [own[None]], None)
-    za, result = lax.optimization_barrier((za, result))
     ya = across_y(za)
     a = jnp.concatenate([za, ya])
     a1, a3 = swap_x(a, 1), swap_x(a, 3)
-    result = add(1, [za, ya], result)
     s1, s3, sy = (jnp.where(here, own, z4) for here in (x % 2 == 0, x < 2, y == 0))
     yb = across_y(jnp.stack([z3, sy]))
-    yb, result = lax.optimization_barrier((yb, result))
     b1 = swap_x(jnp.concatenate([yb, jnp.stack([z3, s1])]), 1)
     b3 = swap_x(jnp.concatenate([jnp.stack([z3, s3]), yb]), 3)
-    result = add(2, [z3[None], z4[None], yb], result)
+    result = add(0, [own[None], za, ya, z3[None], z4[None], yb], None)
     a1, a3, result = lax.optimization_barrier((a1, a3, result))
     ar1, ar3 = swap_x(a3[:2], 1), swap_x(a1[2:], 3)
-    result = add(3, [a1, a3], result)
+    result = add(1, [a1, a3], result)
     b1, b3, result = lax.optimization_barrier((b1, b3, result))
     br1, br3 = swap_x(b3[:2], 1), swap_x(b1[:2], 3)
-    result = add(4, [ar1, ar3, b1, b3], result)
-    result = add(5, [br1, br3], result)
+    result = add(2, [ar1, ar3, b1, b3], result)
+    result = add(3, [br1, br3], result)
     return result.reshape(8, 2, n_slots * 8, CH_WIN).swapaxes(2, 3)
 
 

time: 59.1 us -> 60.7 us (1.027)
  the two profiles are of different devices: /device:TPU:8 before, /device:TPU:16 now
where the time goes in v3:
time: 60.7 us; the launch traced here: 60.6 us
  starting transfers between devices  31.3 us (52%)
  Pallas kernels  14.2 us (23%)
  waiting for transfers between devices  13.5 us (22%)
  other arithmetic  1.03 us (2%)
    ppermute x15, starting transfers between devices, move(): lax.ppermute(array, 'stn', [(number(*p), number(*target(*p))) for p in pl...  28.5 us
    ppermute x15, waiting for transfers between devices, move(): lax.ppermute(array, 'stn', [(number(*p), number(*target(*p))) for p in pl...  12.7 us
    pallas_call x4, Pallas kernels, tiles(): pl.pallas_call(functools.partial(tiles_kernel, base, counts, aliased), ou...  10.8 us
    pallas_call x1, Pallas kernels, spectra(): pl.pallas_call(spectra_kernel, out_shape=[jax.ShapeDtypeStruct((8, CH_WIN...  3.38 us
    ppermute x3, starting transfers between devices, per_device(): lax.ppermute(part, 'chan', [(c, (c + d) % 4) for c in range(4)])  2.82 us
  transfers between devices with their start and end apart: 18, of which 8 were waited for; matrix products, arithmetic and copies ran while one was open for 2% of the time, Pallas kernels for 14%

profile of v3, /device:TPU:16, one launch (start us, length us, event | category | flops | bytes accessed | tf_op | source)
XLA Modules:
  0.0 60.6 jit_solution(16080381061920469665)
XLA Ops:
  0.0 3.4 %spectra.1 = (bf16[8,1024]{1,0:T(8,128)(2,1)}, bf16[8,1024]{1,0:T(8,128)(2,1)}, bf16[8,1024]{1,0:T(8,128)(2,1)}, bf16[8,1024]{1,0:T(8,128)(2,1)}) custom-call(bf16[2,17,128,128]{3,2,1,0:T(8,128)(2,1)} %bitcast.64, f32[16,128,128]{2,1,0:T(8,128)} %constant.179.clone.refs_1_, f32[128,128]{1,0:T(8,128)} %constant.180.clone.refs_2_, ...), custom_call_target="tpu_custom_call" | custom-call | tf_op jit(solution)/shard_map/spectra/pallas_call | solution.py:97
  3.5 1.4 %collective-permute-start.1 = (bf16[8,1024]{1,0:T(8,128)(2,1)}, bf16[8,1024]{1,0:T(8,128)(2,1)S(1)}, u32[]{:S(2)}, u32[]{:S(2)}) collective-permute-start(bf16[8,1024]{1,0:T(8,128)(2,1)} %get-tuple-element.17), channel_id=1, source_target_pairs={{0,2},{1,3},{2,0},{3,1},{4,6},{5,7},{6,4},{7,5},{8,10},{9,11},{10,... | collective-permute-start | bytes 49160 | tf_op jit(solution)/shard_map/ppermute | solution.py:231
  4.9 1.4 %collective-permute-start.2 = (bf16[8,1024]{1,0:T(8,128)(2,1)}, bf16[8,1024]{1,0:T(8,128)(2,1)S(1)}, u32[]{:S(2)}, u32[]{:S(2)}) collective-permute-start(bf16[8,1024]{1,0:T(8,128)(2,1)} %get-tuple-element.18), channel_id=1, source_target_pairs={{0,3},{1,0},{2,1},{3,2},{4,7},{5,4},{6,5},{7,6},{8,11},{9,8},{10,9... | collective-permute-start | bytes 49160 | tf_op jit(solution)/shard_map/ppermute | solution.py:231
  6.2 0.7 %broadcast_select_fusion.refs_0_ = bf16[8,1024]{1,0:T(8,128)(2,1)S(1)} fusion(bf16[8,1024]{1,0:T(8,128)(2,1)} %get-tuple-element.15, pred[]{:T(512)S(6)} %lt.164), kind=kLoop, calls=%fused_computation.12 | loop fusion | flops 8192 | bytes 32769 | tf_op jit(solution)/shard_map/jit(_where)/select_n | solution.py:234
  6.9 0.1 stack.166
  7.1 0.4 collective-permute-done.1.refs_2_
  7.5 0.4 collective-permute-done.2.refs_3_
  7.9 6.4 %collective-permute-start.4 = (bf16[32,1024]{1,0:T(8,128)(2,1)S(1)}, bf16[32,1024]{1,0:T(8,128)(2,1)S(1)}, u32[]{:S(2)}, u32[]{:S(2)}) collective-permute-start(bf16[32,1024]{1,0:T(8,128)(2,1)S(1)} %group_spectra.1.refs_1_), channel_id=1, source_target_pairs={{0,192},{4,196},{8,200},{12,204},{16,208},{20,212},{24,216},{28,22... | collective-permute-start | bytes 196616 | tf_op jit(solution)/shard_map/ppermute | solution.py:208
  14.3 1.0 %collective-permute-start.9 = (bf16[32,1024]{1,0:T(8,128)(2,1)S(1)}, bf16[32,1024]{1,0:T(8,128)(2,1)S(1)}, u32[]{:S(2)}, u32[]{:S(2)}) collective-permute-start(bf16[32,1024]{1,0:T(8,128)(2,1)S(1)} %group_spectra.1.refs_1_), channel_id=1, source_target_pairs={{0,32},{4,36},{8,40},{12,44},{16,48},{20,52},{24,56},{28,60},{32,6... | collective-permute-start | bytes 196616 | tf_op jit(solution)/shard_map/ppermute | solution.py:208
  15.3 3.4 %collective-permute-start.3 = (bf16[32,1024]{1,0:T(8,128)(2,1)S(1)}, bf16[32,1024]{1,0:T(8,128)(2,1)S(1)}, u32[]{:S(2)}, u32[]{:S(2)}) collective-permute-start(bf16[32,1024]{1,0:T(8,128)(2,1)S(1)} %group_spectra.1.refs_1_), channel_id=1, source_target_pairs={{0,96},{4,100},{8,104},{12,108},{16,112},{20,116},{24,120},{28,124... | collective-permute-start | bytes 196616 | tf_op jit(solution)/shard_map/ppermute | solution.py:208
  18.8 3.9 %collective-permute-start.5 = (bf16[32,1024]{1,0:T(8,128)(2,1)S(1)}, bf16[32,1024]{1,0:T(8,128)(2,1)S(1)}, u32[]{:S(2)}, u32[]{:S(2)}) collective-permute-start(bf16[32,1024]{1,0:T(8,128)(2,1)S(1)} %collective-permute-done.4), channel_id=1, source_target_pairs={{0,192},{4,196},{8,200},{12,204},{16,208},{20,212},{24,216},{28,22... | collective-permute-start | bytes 196616 | tf_op jit(solution)/shard_map/ppermute | solution.py:208
  22.7 3.1 %collective-permute-done.10 = bf16[32,1024]{1,0:T(8,128)(2,1)S(1)} collective-permute-done((bf16[32,1024]{1,0:T(8,128)(2,1)S(1)}, bf16[32,1024]{1,0:T(8,128)(2,1)S(1)}, u32[]{:S(2)}, u32[]{:S(2)}) %collective-permute-start.10) | collective-permute-done | bytes 65568 | tf_op jit(solution)/shard_map/ppermute | solution.py:208
  25.8 0.8 %collective-permute-start.11 = (bf16[2,32,1024]{2,1,0:T(8,128)(2,1)S(1)}, bf16[2,32,1024]{2,1,0:T(8,128)(2,1)S(1)}, u32[]{:S(2)}, u32[]{:S(2)}) collective-permute-start(bf16[2,32,1024]{2,1,0:T(8,128)(2,1)S(1)} %pad_maximum_fusion.4.refs_3_), channel_id=1, source_target_pairs={{0,16},{4,20},{8,24},{12,28},{16,0},{20,4},{24,8},{28,12},{32,48},... | collective-permute-start | bytes 393224 | tf_op jit(solution)/shard_map/ppermute | solution.py:208
  26.6 0.5 collective-permute-done.3
  27.1 2.5 %collective-permute-start.6 = (bf16[2,32,1024]{2,1,0:T(8,128)(2,1)S(1)}, bf16[2,32,1024]{2,1,0:T(8,128)(2,1)S(1)}, u32[]{:S(2)}, u32[]{:S(2)}) collective-permute-start(bf16[2,32,1024]{2,1,0:T(8,128)(2,1)S(1)} %pad_maximum_fusion.3), channel_id=1, source_target_pairs={{0,16},{4,20},{8,24},{12,28},{16,0},{20,4},{24,8},{28,12},{32,48},... | collective-permute-start | bytes 393224 | tf_op jit(solution)/shard_map/ppermute | solution.py:208
  29.6 0.2 select_reduce_fusion
  29.7 3.7 %collective-permute-done.11.refs_4_ = bf16[2,32,1024]{2,1,0:T(8,128)(2,1)S(1)} collective-permute-done((bf16[2,32,1024]{2,1,0:T(8,128)(2,1)S(1)}, bf16[2,32,1024]{2,1,0:T(8,128)(2,1)S(1)}, u32[]{:S(2)}, u32[]{:S(2)}) %collective-permute-start.11) | collective-permute-done | bytes 131104 | tf_op jit(solution)/shard_map/ppermute | solution.py:208
  33.5 1.6 %collective-permute-start.12 = (bf16[4,32,1024]{2,1,0:T(8,128)(2,1)S(1)}, bf16[4,32,1024]{2,1,0:T(8,128)(2,1)S(1)}, u32[]{:S(2)}, u32[]{:S(2)}) collective-permute-start(bf16[4,32,1024]{2,1,0:T(8,128)(2,1)S(1)} %pad_maximum_fusion.2), channel_id=1, source_target_pairs={{0,4},{4,0},{8,12},{12,8},{16,20},{20,16},{24,28},{28,24},{32,36},... | collective-permute-start | bytes 786440 | tf_op jit(solution)/shard_map/ppermute | solution.py:208
  35.0 2.2 %collective-permute-start.13 = (bf16[4,32,1024]{2,1,0:T(8,128)(2,1)S(1)}, bf16[4,32,1024]{2,1,0:T(8,128)(2,1)S(1)}, u32[]{:S(2)}, u32[]{:S(2)}) collective-permute-start(bf16[4,32,1024]{2,1,0:T(8,128)(2,1)S(1)} %pad_maximum_fusion.2), channel_id=1, source_target_pairs={{0,12},{4,8},{8,4},{12,0},{16,28},{20,24},{24,20},{28,16},{32,44},... | collective-permute-start | bytes 786440 | tf_op jit(solution)/shard_map/ppermute | solution.py:208
  37.3 0.6 collective-permute-start.7
  37.9 1.0 %collective-permute-start.8 = (bf16[4,32,1024]{2,1,0:T(8,128)(2,1)S(1)}, bf16[4,32,1024]{2,1,0:T(8,128)(2,1)S(1)}, u32[]{:S(2)}, u32[]{:S(2)}) collective-permute-start(bf16[4,32,1024]{2,1,0:T(8,128)(2,1)S(1)} %get-tuple-element.27), channel_id=1, source_target_pairs={{0,12},{4,8},{8,4},{12,0},{16,28},{20,24},{24,20},{28,16},{32,44},... | collective-permute-start | bytes 786440 | tf_op jit(solution)/shard_map/ppermute | solution.py:208
  38.9 2.8 %tiles.4.refs_4_ = bf16[8,2,33,8,1024]{4,3,2,1,0:T(8,128)(2,1)} custom-call(s32[2,33]{1,0:T(2,128)S(1)} %pad_add_fusion.refs_0_, bf16[32,1024]{1,0:T(8,128)(2,1)S(1)} %group_spectra.1.refs_1_, bf16[1,32,1024]{2,1,0:T(8,128)(2,1)S(1)} %bitcast.59, bf16[2,32,1024]{2,1,0:T(8,128)(2,1)S(1)} %pad_maximum_fusion.4.refs_3_, ...), custom_call_target="tpu_custom_call" | custom-call | flops 900000 | bytes 9 | tf_op jit(solution)/shard_map/tiles/pallas_call | solution.py:185
  41.7 0.9 %collective-permute-done.12.refs_2_ = bf16[4,32,1024]{2,1,0:T(8,128)(2,1)S(1)} collective-permute-done((bf16[4,32,1024]{2,1,0:T(8,128)(2,1)S(1)}, bf16[4,32,1024]{2,1,0:T(8,128)(2,1)S(1)}, u32[]{:S(2)}, u32[]{:S(2)}) %collective-permute-start.12) | collective-permute-done | bytes 262176 | tf_op jit(solution)/shard_map/ppermute | solution.py:208
  42.6 2.6 %collective-permute-done.13.refs_3_ = bf16[4,32,1024]{2,1,0:T(8,128)(2,1)S(1)} collective-permute-done((bf16[4,32,1024]{2,1,0:T(8,128)(2,1)S(1)}, bf16[4,32,1024]{2,1,0:T(8,128)(2,1)S(1)}, u32[]{:S(2)}, u32[]{:S(2)}) %collective-permute-start.13) | collective-permute-done | bytes 262176 | tf_op jit(solution)/shard_map/ppermute | solution.py:208
  45.2 0.3 collective-permute-start.16
  45.5 2.5 %collective-permute-start.17 = (bf16[2,32,1024]{2,1,0:T(8,128)(2,1)S(1)}, bf16[2,32,1024]{2,1,0:T(8,128)(2,1)S(1)}, u32[]{:S(2)}, u32[]{:S(2)}) collective-permute-start(bf16[2,32,1024]{2,1,0:T(8,128)(2,1)S(1)} %slice.15), channel_id=1, source_target_pairs={{0,12},{4,8},{8,4},{12,0},{16,28},{20,24},{24,20},{28,16},{32,44},... | collective-permute-start | bytes 393224 | tf_op jit(solution)/shard_map/ppermute | solution.py:208
  48.0 2.7 %tiles.5.refs_6_ = bf16[8,2,33,8,1024]{4,3,2,1,0:T(8,128)(2,1)} custom-call(s32[2,33]{1,0:T(2,128)S(1)} %pad_add_fusion.refs_0_, bf16[32,1024]{1,0:T(8,128)(2,1)S(1)} %group_spectra.1.refs_1_, bf16[4,32,1024]{2,1,0:T(8,128)(2,1)S(1)} %collective-permute-done.12.refs_2_, ...), custom_call_target="tpu_custom_call", output_to_operand_aliasing={{}: (4, {})} | custom-call | flops 800000 | bytes 8 | tf_op jit(solution)/shard_map/tiles/pallas_call | solution.py:185
  50.7 1.5 %collective-permute-start.14 = (bf16[2,32,1024]{2,1,0:T(8,128)(2,1)S(1)}, bf16[2,32,1024]{2,1,0:T(8,128)(2,1)S(1)}, u32[]{:S(2)}, u32[]{:S(2)}) collective-permute-start(bf16[2,32,1024]{2,1,0:T(8,128)(2,1)S(1)} %slice.12), channel_id=1, source_target_pairs={{0,4},{4,0},{8,12},{12,8},{16,20},{20,16},{24,28},{28,24},{32,36},... | collective-permute-start | bytes 393224 | tf_op jit(solution)/shard_map/ppermute | solution.py:208
  52.2 1.0 %collective-permute-start.15 = (bf16[2,32,1024]{2,1,0:T(8,128)(2,1)S(1)}, bf16[2,32,1024]{2,1,0:T(8,128)(2,1)S(1)}, u32[]{:S(2)}, u32[]{:S(2)}) collective-permute-start(bf16[2,32,1024]{2,1,0:T(8,128)(2,1)S(1)} %slice.13), channel_id=1, source_target_pairs={{0,12},{4,8},{8,4},{12,0},{16,28},{20,24},{24,20},{28,16},{32,44},... | collective-permute-start | bytes 393224 | tf_op jit(solution)/shard_map/ppermute | solution.py:208
  53.1 3.3 %tiles.6.refs_4_ = bf16[8,2,33,8,1024]{4,3,2,1,0:T(8,128)(2,1)} custom-call(s32[2,33]{1,0:T(2,128)S(1)} %pad_add_fusion.refs_0_, bf16[32,1024]{1,0:T(8,128)(2,1)S(1)} %group_spectra.1.refs_1_, bf16[2,32,1024]{2,1,0:T(8,128)(2,1)S(1)} %collective-permute-done.16.refs_2_, ...), custom_call_target="tpu_custom_call", output_to_operand_aliasing={{}: (6, {})} | custom-call | flops 1200000 | bytes 12 | tf_op jit(solution)/shard_map/tiles/pallas_call | solution.py:185
  56.5 2.0 %collective-permute-done.15.refs_3_ = bf16[2,32,1024]{2,1,0:T(8,128)(2,1)S(1)} collective-permute-done((bf16[2,32,1024]{2,1,0:T(8,128)(2,1)S(1)}, bf16[2,32,1024]{2,1,0:T(8,128)(2,1)S(1)}, u32[]{:S(2)}, u32[]{:S(2)}) %collective-permute-start.15) | collective-permute-done | bytes 131104 | tf_op jit(solution)/shard_map/ppermute | solution.py:208
  58.4 2.0 %tiles.7 = bf16[8,2,33,8,1024]{4,3,2,1,0:T(8,128)(2,1)} custom-call(s32[2,33]{1,0:T(2,128)S(1)} %pad_add_fusion.refs_0_, bf16[32,1024]{1,0:T(8,128)(2,1)S(1)} %group_spectra.1.refs_1_, bf16[2,32,1024]{2,1,0:T(8,128)(2,1)S(1)} %collective-permute-done.14.refs_2_, ...), custom_call_target="tpu_custom_call", output_to_operand_aliasing={{}: (4, {})} | custom-call | flops 400000 | bytes 4 | tf_op jit(solution)/shard_map/tiles/pallas_call | solution.py:185
  (27 shorter events, 0.4 us)
Async XLA Ops:
  0.0 15.3 %copy-start = (s32[64,64]{1,0:T(8,128)S(1)}, s32[64,64]{1,0:T(8,128)}, u32[]{:S(2)}) copy-start(s32[64,64]{1,0:T(8,128)} %param.7) | copy-start | bytes 49156
  3.4 3.7 %collective-permute-start = (bf16[8,1024]{1,0:T(8,128)(2,1)}, bf16[8,1024]{1,0:T(8,128)(2,1)S(1)}, u32[]{:S(2)}, u32[]{:S(2)}) collective-permute-start(bf16[8,1024]{1,0:T(8,128)(2,1)} %get-tuple-element.16), channel_id=1, source_target_pairs={{0,1},{1,2},{2,3},{3,0},{4,5},{5,6},{6,7},{7,4},{8,9},{9,10},{10,1... | collective-permute-start | bytes 49160 | tf_op jit(solution)/shard_map/ppermute | solution.py:231
  3.5 4.0 %collective-permute-start.1 = (bf16[8,1024]{1,0:T(8,128)(2,1)}, bf16[8,1024]{1,0:T(8,128)(2,1)S(1)}, u32[]{:S(2)}, u32[]{:S(2)}) collective-permute-start(bf16[8,1024]{1,0:T(8,128)(2,1)} %get-tuple-element.17), channel_id=1, source_target_pairs={{0,2},{1,3},{2,0},{3,1},{4,6},{5,7},{6,4},{7,5},{8,10},{9,11},{10,... | collective-permute-start | bytes 49160 | tf_op jit(solution)/shard_map/ppermute | solution.py:231
  4.9 3.0 %collective-permute-start.2 = (bf16[8,1024]{1,0:T(8,128)(2,1)}, bf16[8,1024]{1,0:T(8,128)(2,1)S(1)}, u32[]{:S(2)}, u32[]{:S(2)}) collective-permute-start(bf16[8,1024]{1,0:T(8,128)(2,1)} %get-tuple-element.18), channel_id=1, source_target_pairs={{0,3},{1,0},{2,1},{3,2},{4,7},{5,4},{6,5},{7,6},{8,11},{9,8},{10,9... | collective-permute-start | bytes 49160 | tf_op jit(solution)/shard_map/ppermute | solution.py:231
  7.9 10.8 %collective-permute-start.4 = (bf16[32,1024]{1,0:T(8,128)(2,1)S(1)}, bf16[32,1024]{1,0:T(8,128)(2,1)S(1)}, u32[]{:S(2)}, u32[]{:S(2)}) collective-permute-start(bf16[32,1024]{1,0:T(8,128)(2,1)S(1)} %group_spectra.1.refs_1_), channel_id=1, source_target_pairs={{0,192},{4,196},{8,200},{12,204},{16,208},{20,212},{24,216},{28,22... | collective-permute-start | bytes 196616 | tf_op jit(solution)/shard_map/ppermute | solution.py:208
  14.3 8.3 %collective-permute-start.9 = (bf16[32,1024]{1,0:T(8,128)(2,1)S(1)}, bf16[32,1024]{1,0:T(8,128)(2,1)S(1)}, u32[]{:S(2)}, u32[]{:S(2)}) collective-permute-start(bf16[32,1024]{1,0:T(8,128)(2,1)S(1)} %group_spectra.1.refs_1_), channel_id=1, source_target_pairs={{0,32},{4,36},{8,40},{12,44},{16,48},{20,52},{24,56},{28,60},{32,6... | collective-permute-start | bytes 196616 | tf_op jit(solution)/shard_map/ppermute | solution.py:208
  15.3 10.5 %collective-permute-start.10 = (bf16[32,1024]{1,0:T(8,128)(2,1)S(1)}, bf16[32,1024]{1,0:T(8,128)(2,1)S(1)}, u32[]{:S(2)}, u32[]{:S(2)}) collective-permute-start(bf16[32,1024]{1,0:T(8,128)(2,1)S(1)} %group_spectra.1.refs_1_), channel_id=1, source_target_pairs={{0,64},{4,68},{8,72},{12,76},{16,80},{20,84},{24,88},{28,92},{32,9... | collective-permute-start | bytes 196616 | tf_op jit(solution)/shard_map/ppermute | solution.py:208
  15.3 11.7 %collective-permute-start.3 = (bf16[32,1024]{1,0:T(8,128)(2,1)S(1)}, bf16[32,1024]{1,0:T(8,128)(2,1)S(1)}, u32[]{:S(2)}, u32[]{:S(2)}) collective-permute-start(bf16[32,1024]{1,0:T(8,128)(2,1)S(1)} %group_spectra.1.refs_1_), channel_id=1, source_target_pairs={{0,96},{4,100},{8,104},{12,108},{16,112},{20,116},{24,120},{28,124... | collective-permute-start | bytes 196616 | tf_op jit(solution)/shard_map/ppermute | solution.py:208
  18.8 7.8 %collective-permute-start.5 = (bf16[32,1024]{1,0:T(8,128)(2,1)S(1)}, bf16[32,1024]{1,0:T(8,128)(2,1)S(1)}, u32[]{:S(2)}, u32[]{:S(2)}) collective-permute-start(bf16[32,1024]{1,0:T(8,128)(2,1)S(1)} %collective-permute-done.4), channel_id=1, source_target_pairs={{0,192},{4,196},{8,200},{12,204},{16,208},{20,212},{24,216},{28,22... | collective-permute-start | bytes 196616 | tf_op jit(solution)/shard_map/ppermute | solution.py:208
  25.8 7.6 %collective-permute-start.11 = (bf16[2,32,1024]{2,1,0:T(8,128)(2,1)S(1)}, bf16[2,32,1024]{2,1,0:T(8,128)(2,1)S(1)}, u32[]{:S(2)}, u32[]{:S(2)}) collective-permute-start(bf16[2,32,1024]{2,1,0:T(8,128)(2,1)S(1)} %pad_maximum_fusion.4.refs_3_), channel_id=1, source_target_pairs={{0,16},{4,20},{8,24},{12,28},{16,0},{20,4},{24,8},{28,12},{32,48},... | collective-permute-start | bytes 393224 | tf_op jit(solution)/shard_map/ppermute | solution.py:208
  27.1 10.2 %collective-permute-start.6 = (bf16[2,32,1024]{2,1,0:T(8,128)(2,1)S(1)}, bf16[2,32,1024]{2,1,0:T(8,128)(2,1)S(1)}, u32[]{:S(2)}, u32[]{:S(2)}) collective-permute-start(bf16[2,32,1024]{2,1,0:T(8,128)(2,1)S(1)} %pad_maximum_fusion.3), channel_id=1, source_target_pairs={{0,16},{4,20},{8,24},{12,28},{16,0},{20,4},{24,8},{28,12},{32,48},... | collective-permute-start | bytes 393224 | tf_op jit(solution)/shard_map/ppermute | solution.py:208
  33.5 9.1 %collective-permute-start.12 = (bf16[4,32,1024]{2,1,0:T(8,128)(2,1)S(1)}, bf16[4,32,1024]{2,1,0:T(8,128)(2,1)S(1)}, u32[]{:S(2)}, u32[]{:S(2)}) collective-permute-start(bf16[4,32,1024]{2,1,0:T(8,128)(2,1)S(1)} %pad_maximum_fusion.2), channel_id=1, source_target_pairs={{0,4},{4,0},{8,12},{12,8},{16,20},{20,16},{24,28},{28,24},{32,36},... | collective-permute-start | bytes 786440 | tf_op jit(solution)/shard_map/ppermute | solution.py:208
  35.0 10.1 %collective-permute-start.13 = (bf16[4,32,1024]{2,1,0:T(8,128)(2,1)S(1)}, bf16[4,32,1024]{2,1,0:T(8,128)(2,1)S(1)}, u32[]{:S(2)}, u32[]{:S(2)}) collective-permute-start(bf16[4,32,1024]{2,1,0:T(8,128)(2,1)S(1)} %pad_maximum_fusion.2), channel_id=1, source_target_pairs={{0,12},{4,8},{8,4},{12,0},{16,28},{20,24},{24,20},{28,16},{32,44},... | collective-permute-start | bytes 786440 | tf_op jit(solution)/shard_map/ppermute | solution.py:208
  37.3 13.3 %collective-permute-start.7 = (bf16[4,32,1024]{2,1,0:T(8,128)(2,1)S(1)}, bf16[4,32,1024]{2,1,0:T(8,128)(2,1)S(1)}, u32[]{:S(2)}, u32[]{:S(2)}) collective-permute-start(bf16[4,32,1024]{2,1,0:T(8,128)(2,1)S(1)} %get-tuple-element.28), channel_id=1, source_target_pairs={{0,4},{4,0},{8,12},{12,8},{16,20},{20,16},{24,28},{28,24},{32,36},... | collective-permute-start | bytes 786440 | tf_op jit(solution)/shard_map/ppermute | solution.py:208
  37.9 12.8 %collective-permute-start.8 = (bf16[4,32,1024]{2,1,0:T(8,128)(2,1)S(1)}, bf16[4,32,1024]{2,1,0:T(8,128)(2,1)S(1)}, u32[]{:S(2)}, u32[]{:S(2)}) collective-permute-start(bf16[4,32,1024]{2,1,0:T(8,128)(2,1)S(1)} %get-tuple-element.27), channel_id=1, source_target_pairs={{0,12},{4,8},{8,4},{12,0},{16,28},{20,24},{24,20},{28,16},{32,44},... | collective-permute-start | bytes 786440 | tf_op jit(solution)/shard_map/ppermute | solution.py:208
  45.2 7.9 %collective-permute-start.16 = (bf16[2,32,1024]{2,1,0:T(8,128)(2,1)S(1)}, bf16[2,32,1024]{2,1,0:T(8,128)(2,1)S(1)}, u32[]{:S(2)}, u32[]{:S(2)}) collective-permute-start(bf16[2,32,1024]{2,1,0:T(8,128)(2,1)S(1)} %slice.14), channel_id=1, source_target_pairs={{0,4},{4,0},{8,12},{12,8},{16,20},{20,16},{24,28},{28,24},{32,36},... | collective-permute-start | bytes 393224 | tf_op jit(solution)/shard_map/ppermute | solution.py:208
  45.5 7.6 %collective-permute-start.17 = (bf16[2,32,1024]{2,1,0:T(8,128)(2,1)S(1)}, bf16[2,32,1024]{2,1,0:T(8,128)(2,1)S(1)}, u32[]{:S(2)}, u32[]{:S(2)}) collective-permute-start(bf16[2,32,1024]{2,1,0:T(8,128)(2,1)S(1)} %slice.15), channel_id=1, source_target_pairs={{0,12},{4,8},{8,4},{12,0},{16,28},{20,24},{24,20},{28,16},{32,44},... | collective-permute-start | bytes 393224 | tf_op jit(solution)/shard_map/ppermute | solution.py:208
  50.7 5.8 %collective-permute-start.14 = (bf16[2,32,1024]{2,1,0:T(8,128)(2,1)S(1)}, bf16[2,32,1024]{2,1,0:T(8,128)(2,1)S(1)}, u32[]{:S(2)}, u32[]{:S(2)}) collective-permute-start(bf16[2,32,1024]{2,1,0:T(8,128)(2,1)S(1)} %slice.12), channel_id=1, source_target_pairs={{0,4},{4,0},{8,12},{12,8},{16,20},{20,16},{24,28},{28,24},{32,36},... | collective-permute-start | bytes 393224 | tf_op jit(solution)/shard_map/ppermute | solution.py:208
  52.2 6.3 %collective-permute-start.15 = (bf16[2,32,1024]{2,1,0:T(8,128)(2,1)S(1)}, bf16[2,32,1024]{2,1,0:T(8,128)(2,1)S(1)}, u32[]{:S(2)}, u32[]{:S(2)}) collective-permute-start(bf16[2,32,1024]{2,1,0:T(8,128)(2,1)S(1)} %slice.13), channel_id=1, source_target_pairs={{0,12},{4,8},{8,4},{12,0},{16,28},{20,24},{24,20},{28,16},{32,44},... | collective-permute-start | bytes 393224 | tf_op jit(solution)/shard_map/ppermute | solution.py:208

commit v4 on v3

--- a/solution.py
+++ b/solution.py
@@ -15,6 +15,7 @@
 N_Z, N_Y, N_X = 8, 2, 4
 MIB = 1 << 20
 UNROLL = 8
+FRAME_CUTS = ((0, 5), (5, 9), (9, 13), (13, 17))
 SMEM = pltpu.MemorySpace.SMEM
 VMEM = pltpu.MemorySpace.VMEM
 HBM = pltpu.MemorySpace.HBM
@@ -52,19 +53,35 @@
 
 
 def spectra_kernel(*refs):
-    chan_ref, outs, held, sems, rows_ref = refs[5], refs[6:10], refs[10:15], refs[15], refs[16]
-    copies = [pltpu.make_async_copy(refs[n], held[n], sems.at[n]) for n in range(5)]
+    sources, chan_ref, outs, held, sems, total_ref, rows_ref = refs[:5], refs[5], refs[6:10], refs[10:15], *refs[15:]
+    x_ref, taps_ref, first_ref, turn_ref, second_ref = held
+    copies = []
+    for n, (low, high) in enumerate(FRAME_CUTS):
+        frames, taps = pl.ds(low, high - low), pl.ds(low, min(high, TAPS) - low)
+        copies.append(pltpu.make_async_copy(sources[0].at[:, frames], x_ref.at[:, frames], sems.at[2 * n]))
+        copies.append(pltpu.make_async_copy(sources[1].at[taps], taps_ref.at[taps], sems.at[2 * n + 1]))
+    cut = len(copies)
+    copies += [pltpu.make_async_copy(sources[n], held[n], sems.at[cut + n - 2]) for n in range(2, 5)]
     for copy in copies:
         copy.start()
-    for copy in copies:
+    for n, (low, high) in enumerate(FRAME_CUTS):
+        copies[2 * n].wait()
+        copies[2 * n + 1].wait()
+        for i in range(2):
+            for f in range(2):
+                terms = [
+                    taps_ref[frame - f] * x_ref[i, frame].astype(jnp.float32)
+                    for frame in range(low, high)
+                    if 0 <= frame - f < TAPS
+                ]
+                total = functools.reduce(jnp.add, terms)
+                total_ref[i * 2 + f] = total if n == 0 else total_ref[i * 2 + f] + total
+    for copy in copies[cut:]:
         copy.wait()
-    x_ref, taps_ref, first_ref, turn_ref, second_ref = held
     turned = []
     for i in range(2):
         for f in range(2):
-            total = taps_ref[0] * x_ref[i, f].astype(jnp.float32)
-            for tap in range(1, TAPS):
-                total = total + taps_ref[tap] * x_ref[i, f + tap].astype(jnp.float32)
+            total = total_ref[i * 2 + f]
             y = jnp.dot(
                 first_ref[...], total, precision=lax.Precision.HIGHEST, preferred_element_type=jnp.float32
             )
@@ -88,7 +105,7 @@
                     lane = (k % 8) * 128
                     rows_ref[k // 8, row : row + 1, lane : lane + 128] = s[k : k + 1]
     for d in range(4):
-        outs[d][...] = rows_ref[lax.rem(chan_ref[0] + d, 4)].astype(jnp.bfloat16)
+        outs[d][...] = rows_ref[lax.bitwise_xor(chan_ref[0], d)].astype(jnp.bfloat16)
 
 
 def spectra(samples, chan):
@@ -105,7 +122,8 @@
             pltpu.VMEM((128, 128), jnp.float32),
             pltpu.VMEM((2, 64, 128), jnp.float32),
             pltpu.VMEM((128, 256), jnp.float32),
-            pltpu.SemaphoreType.DMA((5,)),
+            pltpu.SemaphoreType.DMA((2 * len(FRAME_CUTS) + 3,)),
+            pltpu.VMEM((4, 128, 128), jnp.float32),
             pltpu.VMEM((4, 8, CH_WIN), jnp.float32),
         ],
         compiler_params=pltpu.CompilerParams(vmem_limit_bytes=56 * MIB),
@@ -118,7 +136,7 @@
     for d in range(4):
         wide_ref[d] = pieces[d][...].astype(jnp.float32)
     for source in range(4):
-        piece = wide_ref[lax.rem(chan_ref[0] + 4 - source, 4)]
+        piece = wide_ref[lax.bitwise_xor(chan_ref[0], source)]
         for t in range(4):
             rows_ref[t, source * 2 : source * 2 + 2, :] = piece[t * 2 : t * 2 + 2]
     out_ref[...] = rows_ref[...].reshape(32, CH_WIN).astype(jnp.bfloat16)
@@ -228,7 +246,7 @@
 
     chan_scalar = chan.astype(jnp.int32).reshape(1)
     pieces = [
-        part if d == 0 else lax.ppermute(part, "chan", [(c, (c + d) % 4) for c in range(4)])
+        part if d == 0 else lax.ppermute(part, "chan", [(c, c ^ d) for c in range(4)])
         for d, part in enumerate(spectra(samples, chan_scalar))
     ]
     pieces[0] = jnp.where(chan < 4, pieces[0], jnp.zeros((), jnp.bfloat16))

time: 60.7 us -> 58.5 us (0.964)
  starting transfers between devices: 31.3 us -> 29.9 us
    ppermute x15, waiting for transfers between devices: 12.7 us -> 10.9 us  [move(): lax.ppermute(array, 'stn', [(number(*p), number(*target(*p))) for p in pl...]
    ppermute x3, waiting for transfers between devices: 0.81 us -> 2.03 us  [per_device(): lax.ppermute(part, 'chan', [(c, c ^ d) for c in range(4)])]
    ppermute x3, starting transfers between devices: 2.82 us -> 1.96 us  [per_device(): lax.ppermute(part, 'chan', [(c, c ^ d) for c in range(4)])]
  transfers between devices with their start and end apart: 18 -> 18, of which waited for: 8 -> 6; matrix products, arithmetic and copies ran while one was open for 2% -> 2% of each run, Pallas kernels for 14% -> 15%
where the time goes in v4:
time: 58.5 us; the launch traced here: 58.3 us
  starting transfers between devices  29.9 us (51%)
  Pallas kernels  14 us (24%)
  waiting for transfers between devices  12.9 us (22%)
  other arithmetic  1.04 us (2%)
    ppermute x15, starting transfers between devices, move(): lax.ppermute(array, 'stn', [(number(*p), number(*target(*p))) for p in pl...  27.9 us
    ppermute x15, waiting for transfers between devices, move(): lax.ppermute(array, 'stn', [(number(*p), number(*target(*p))) for p in pl...  10.9 us
    pallas_call x4, Pallas kernels, tiles(): pl.pallas_call(functools.partial(tiles_kernel, base, counts, aliased), ou...  10.8 us
    pallas_call x1, Pallas kernels, spectra(): pl.pallas_call(spectra_kernel, out_shape=[jax.ShapeDtypeStruct((8, CH_WIN...  3.18 us
    ppermute x3, waiting for transfers between devices, per_device(): lax.ppermute(part, 'chan', [(c, c ^ d) for c in range(4)])  2.03 us
    ppermute x3, starting transfers between devices, per_device(): lax.ppermute(part, 'chan', [(c, c ^ d) for c in range(4)])  1.96 us
  transfers between devices with their start and end apart: 18, of which 6 were waited for; matrix products, arithmetic and copies ran while one was open for 2% of the time, Pallas kernels for 15%

profile of v4, /device:TPU:16, one launch (start us, length us, event | category | flops | bytes accessed | tf_op | source)
XLA Modules:
  0.0 58.3 jit_solution(10572751017121166905)
XLA Ops:
  0.0 3.2 %spectra.1 = (bf16[8,1024]{1,0:T(8,128)(2,1)}, bf16[8,1024]{1,0:T(8,128)(2,1)}, bf16[8,1024]{1,0:T(8,128)(2,1)}, bf16[8,1024]{1,0:T(8,128)(2,1)}) custom-call(bf16[2,17,128,128]{3,2,1,0:T(8,128)(2,1)} %bitcast.64, f32[16,128,128]{2,1,0:T(8,128)} %constant.179.clone.refs_1_, f32[128,128]{1,0:T(8,128)} %constant.180.clone.refs_2_, ...), custom_call_target="tpu_custom_call" | custom-call | tf_op jit(solution)/shard_map/spectra/pallas_call | solution.py:114
  3.2 0.1 collective-permute-start
  3.3 1.4 %collective-permute-start.1 = (bf16[8,1024]{1,0:T(8,128)(2,1)}, bf16[8,1024]{1,0:T(8,128)(2,1)S(1)}, u32[]{:S(2)}, u32[]{:S(2)}) collective-permute-start(bf16[8,1024]{1,0:T(8,128)(2,1)} %get-tuple-element.17), channel_id=1, source_target_pairs={{0,2},{1,3},{2,0},{3,1},{4,6},{5,7},{6,4},{7,5},{8,10},{9,11},{10,... | collective-permute-start | bytes 49160 | tf_op jit(solution)/shard_map/ppermute | solution.py:249
  4.7 0.5 collective-permute-start.2
  5.2 0.7 %broadcast_select_fusion.refs_0_ = bf16[8,1024]{1,0:T(8,128)(2,1)S(1)} fusion(bf16[8,1024]{1,0:T(8,128)(2,1)} %get-tuple-element.15, pred[]{:T(512)S(6)} %lt.164), kind=kLoop, calls=%fused_computation.12 | loop fusion | flops 8192 | bytes 32769 | tf_op jit(solution)/shard_map/jit(_where)/select_n | solution.py:252
  5.9 0.1 stack.166
  6.0 1.3 %collective-permute-done.1.refs_2_ = bf16[8,1024]{1,0:T(8,128)(2,1)S(1)} collective-permute-done((bf16[8,1024]{1,0:T(8,128)(2,1)}, bf16[8,1024]{1,0:T(8,128)(2,1)S(1)}, u32[]{:S(2)}, u32[]{:S(2)}) %collective-permute-start.1) | collective-permute-done | bytes 16416 | tf_op jit(solution)/shard_map/ppermute | solution.py:249
  7.3 0.7 %collective-permute-done.2.refs_3_ = bf16[8,1024]{1,0:T(8,128)(2,1)S(1)} collective-permute-done((bf16[8,1024]{1,0:T(8,128)(2,1)}, bf16[8,1024]{1,0:T(8,128)(2,1)S(1)}, u32[]{:S(2)}, u32[]{:S(2)}) %collective-permute-start.2) | collective-permute-done | bytes 16416 | tf_op jit(solution)/shard_map/ppermute | solution.py:249
  8.0 0.1 group_spectra.1.refs_1_
  8.1 6.4 %collective-permute-start.4 = (bf16[32,1024]{1,0:T(8,128)(2,1)S(1)}, bf16[32,1024]{1,0:T(8,128)(2,1)S(1)}, u32[]{:S(2)}, u32[]{:S(2)}) collective-permute-start(bf16[32,1024]{1,0:T(8,128)(2,1)S(1)} %group_spectra.1.refs_1_), channel_id=1, source_target_pairs={{0,192},{4,196},{8,200},{12,204},{16,208},{20,212},{24,216},{28,22... | collective-permute-start | bytes 196616 | tf_op jit(solution)/shard_map/ppermute | solution.py:226
  14.5 1.0 %collective-permute-start.9 = (bf16[32,1024]{1,0:T(8,128)(2,1)S(1)}, bf16[32,1024]{1,0:T(8,128)(2,1)S(1)}, u32[]{:S(2)}, u32[]{:S(2)}) collective-permute-start(bf16[32,1024]{1,0:T(8,128)(2,1)S(1)} %group_spectra.1.refs_1_), channel_id=1, source_target_pairs={{0,32},{4,36},{8,40},{12,44},{16,48},{20,52},{24,56},{28,60},{32,6... | collective-permute-start | bytes 196616 | tf_op jit(solution)/shard_map/ppermute | solution.py:226
  15.5 3.4 %collective-permute-start.3 = (bf16[32,1024]{1,0:T(8,128)(2,1)S(1)}, bf16[32,1024]{1,0:T(8,128)(2,1)S(1)}, u32[]{:S(2)}, u32[]{:S(2)}) collective-permute-start(bf16[32,1024]{1,0:T(8,128)(2,1)S(1)} %group_spectra.1.refs_1_), channel_id=1, source_target_pairs={{0,96},{4,100},{8,104},{12,108},{16,112},{20,116},{24,120},{28,124... | collective-permute-start | bytes 196616 | tf_op jit(solution)/shard_map/ppermute | solution.py:226
  18.9 3.2 %collective-permute-start.5 = (bf16[32,1024]{1,0:T(8,128)(2,1)S(1)}, bf16[32,1024]{1,0:T(8,128)(2,1)S(1)}, u32[]{:S(2)}, u32[]{:S(2)}) collective-permute-start(bf16[32,1024]{1,0:T(8,128)(2,1)S(1)} %collective-permute-done.4), channel_id=1, source_target_pairs={{0,192},{4,196},{8,200},{12,204},{16,208},{20,212},{24,216},{28,22... | collective-permute-start | bytes 196616 | tf_op jit(solution)/shard_map/ppermute | solution.py:226
  22.1 4.0 %collective-permute-done.10 = bf16[32,1024]{1,0:T(8,128)(2,1)S(1)} collective-permute-done((bf16[32,1024]{1,0:T(8,128)(2,1)S(1)}, bf16[32,1024]{1,0:T(8,128)(2,1)S(1)}, u32[]{:S(2)}, u32[]{:S(2)}) %collective-permute-start.10) | collective-permute-done | bytes 65568 | tf_op jit(solution)/shard_map/ppermute | solution.py:226
  26.1 0.7 %collective-permute-start.11 = (bf16[2,32,1024]{2,1,0:T(8,128)(2,1)S(1)}, bf16[2,32,1024]{2,1,0:T(8,128)(2,1)S(1)}, u32[]{:S(2)}, u32[]{:S(2)}) collective-permute-start(bf16[2,32,1024]{2,1,0:T(8,128)(2,1)S(1)} %pad_maximum_fusion.4.refs_3_), channel_id=1, source_target_pairs={{0,16},{4,20},{8,24},{12,28},{16,0},{20,4},{24,8},{28,12},{32,48},... | collective-permute-start | bytes 393224 | tf_op jit(solution)/shard_map/ppermute | solution.py:226
  26.9 3.0 %collective-permute-start.6 = (bf16[2,32,1024]{2,1,0:T(8,128)(2,1)S(1)}, bf16[2,32,1024]{2,1,0:T(8,128)(2,1)S(1)}, u32[]{:S(2)}, u32[]{:S(2)}) collective-permute-start(bf16[2,32,1024]{2,1,0:T(8,128)(2,1)S(1)} %pad_maximum_fusion.3), channel_id=1, source_target_pairs={{0,16},{4,20},{8,24},{12,28},{16,0},{20,4},{24,8},{28,12},{32,48},... | collective-permute-start | bytes 393224 | tf_op jit(solution)/shard_map/ppermute | solution.py:226
  29.9 0.2 select_reduce_fusion
  30.1 2.6 %collective-permute-done.11.refs_4_ = bf16[2,32,1024]{2,1,0:T(8,128)(2,1)S(1)} collective-permute-done((bf16[2,32,1024]{2,1,0:T(8,128)(2,1)S(1)}, bf16[2,32,1024]{2,1,0:T(8,128)(2,1)S(1)}, u32[]{:S(2)}, u32[]{:S(2)}) %collective-permute-start.11) | collective-permute-done | bytes 131104 | tf_op jit(solution)/shard_map/ppermute | solution.py:226
  32.7 1.6 %collective-permute-start.12 = (bf16[4,32,1024]{2,1,0:T(8,128)(2,1)S(1)}, bf16[4,32,1024]{2,1,0:T(8,128)(2,1)S(1)}, u32[]{:S(2)}, u32[]{:S(2)}) collective-permute-start(bf16[4,32,1024]{2,1,0:T(8,128)(2,1)S(1)} %pad_maximum_fusion.2), channel_id=1, source_target_pairs={{0,4},{4,0},{8,12},{12,8},{16,20},{20,16},{24,28},{28,24},{32,36},... | collective-permute-start | bytes 786440 | tf_op jit(solution)/shard_map/ppermute | solution.py:226
  34.3 2.1 %collective-permute-start.13 = (bf16[4,32,1024]{2,1,0:T(8,128)(2,1)S(1)}, bf16[4,32,1024]{2,1,0:T(8,128)(2,1)S(1)}, u32[]{:S(2)}, u32[]{:S(2)}) collective-permute-start(bf16[4,32,1024]{2,1,0:T(8,128)(2,1)S(1)} %pad_maximum_fusion.2), channel_id=1, source_target_pairs={{0,12},{4,8},{8,4},{12,0},{16,28},{20,24},{24,20},{28,16},{32,44},... | collective-permute-start | bytes 786440 | tf_op jit(solution)/shard_map/ppermute | solution.py:226
  36.4 0.7 %collective-permute-start.7 = (bf16[4,32,1024]{2,1,0:T(8,128)(2,1)S(1)}, bf16[4,32,1024]{2,1,0:T(8,128)(2,1)S(1)}, u32[]{:S(2)}, u32[]{:S(2)}) collective-permute-start(bf16[4,32,1024]{2,1,0:T(8,128)(2,1)S(1)} %get-tuple-element.28), channel_id=1, source_target_pairs={{0,4},{4,0},{8,12},{12,8},{16,20},{20,16},{24,28},{28,24},{32,36},... | collective-permute-start | bytes 786440 | tf_op jit(solution)/shard_map/ppermute | solution.py:226
  37.1 0.7 %collective-permute-start.8 = (bf16[4,32,1024]{2,1,0:T(8,128)(2,1)S(1)}, bf16[4,32,1024]{2,1,0:T(8,128)(2,1)S(1)}, u32[]{:S(2)}, u32[]{:S(2)}) collective-permute-start(bf16[4,32,1024]{2,1,0:T(8,128)(2,1)S(1)} %get-tuple-element.27), channel_id=1, source_target_pairs={{0,12},{4,8},{8,4},{12,0},{16,28},{20,24},{24,20},{28,16},{32,44},... | collective-permute-start | bytes 786440 | tf_op jit(solution)/shard_map/ppermute | solution.py:226
  37.8 2.8 %tiles.4.refs_4_ = bf16[8,2,33,8,1024]{4,3,2,1,0:T(8,128)(2,1)} custom-call(s32[2,33]{1,0:T(2,128)S(1)} %pad_add_fusion.refs_0_, bf16[32,1024]{1,0:T(8,128)(2,1)S(1)} %group_spectra.1.refs_1_, bf16[1,32,1024]{2,1,0:T(8,128)(2,1)S(1)} %bitcast.59, bf16[2,32,1024]{2,1,0:T(8,128)(2,1)S(1)} %pad_maximum_fusion.4.refs_3_, ...), custom_call_target="tpu_custom_call" | custom-call | flops 900000 | bytes 9 | tf_op jit(solution)/shard_map/tiles/pallas_call | solution.py:203
  40.6 2.6 %collective-permute-done.13.refs_3_ = bf16[4,32,1024]{2,1,0:T(8,128)(2,1)S(1)} collective-permute-done((bf16[4,32,1024]{2,1,0:T(8,128)(2,1)S(1)}, bf16[4,32,1024]{2,1,0:T(8,128)(2,1)S(1)}, u32[]{:S(2)}, u32[]{:S(2)}) %collective-permute-start.13) | collective-permute-done | bytes 262176 | tf_op jit(solution)/shard_map/ppermute | solution.py:226
  43.3 0.3 collective-permute-start.16
  43.6 2.2 %collective-permute-start.17 = (bf16[2,32,1024]{2,1,0:T(8,128)(2,1)S(1)}, bf16[2,32,1024]{2,1,0:T(8,128)(2,1)S(1)}, u32[]{:S(2)}, u32[]{:S(2)}) collective-permute-start(bf16[2,32,1024]{2,1,0:T(8,128)(2,1)S(1)} %slice.15), channel_id=1, source_target_pairs={{0,12},{4,8},{8,4},{12,0},{16,28},{20,24},{24,20},{28,16},{32,44},... | collective-permute-start | bytes 393224 | tf_op jit(solution)/shard_map/ppermute | solution.py:226
  45.7 2.7 %tiles.5.refs_6_ = bf16[8,2,33,8,1024]{4,3,2,1,0:T(8,128)(2,1)} custom-call(s32[2,33]{1,0:T(2,128)S(1)} %pad_add_fusion.refs_0_, bf16[32,1024]{1,0:T(8,128)(2,1)S(1)} %group_spectra.1.refs_1_, bf16[4,32,1024]{2,1,0:T(8,128)(2,1)S(1)} %collective-permute-done.12.refs_2_, ...), custom_call_target="tpu_custom_call", output_to_operand_aliasing={{}: (4, {})} | custom-call | flops 800000 | bytes 8 | tf_op jit(solution)/shard_map/tiles/pallas_call | solution.py:203
  48.4 1.4 %collective-permute-start.14 = (bf16[2,32,1024]{2,1,0:T(8,128)(2,1)S(1)}, bf16[2,32,1024]{2,1,0:T(8,128)(2,1)S(1)}, u32[]{:S(2)}, u32[]{:S(2)}) collective-permute-start(bf16[2,32,1024]{2,1,0:T(8,128)(2,1)S(1)} %slice.12), channel_id=1, source_target_pairs={{0,4},{4,0},{8,12},{12,8},{16,20},{20,16},{24,28},{28,24},{32,36},... | collective-permute-start | bytes 393224 | tf_op jit(solution)/shard_map/ppermute | solution.py:226
  49.9 1.3 %collective-permute-start.15 = (bf16[2,32,1024]{2,1,0:T(8,128)(2,1)S(1)}, bf16[2,32,1024]{2,1,0:T(8,128)(2,1)S(1)}, u32[]{:S(2)}, u32[]{:S(2)}) collective-permute-start(bf16[2,32,1024]{2,1,0:T(8,128)(2,1)S(1)} %slice.13), channel_id=1, source_target_pairs={{0,12},{4,8},{8,4},{12,0},{16,28},{20,24},{24,20},{28,16},{32,44},... | collective-permute-start | bytes 393224 | tf_op jit(solution)/shard_map/ppermute | solution.py:226
  51.2 3.3 %tiles.6.refs_4_ = bf16[8,2,33,8,1024]{4,3,2,1,0:T(8,128)(2,1)} custom-call(s32[2,33]{1,0:T(2,128)S(1)} %pad_add_fusion.refs_0_, bf16[32,1024]{1,0:T(8,128)(2,1)S(1)} %group_spectra.1.refs_1_, bf16[2,32,1024]{2,1,0:T(8,128)(2,1)S(1)} %collective-permute-done.16.refs_2_, ...), custom_call_target="tpu_custom_call", output_to_operand_aliasing={{}: (6, {})} | custom-call | flops 1200000 | bytes 12 | tf_op jit(solution)/shard_map/tiles/pallas_call | solution.py:203
  54.5 1.6 %collective-permute-done.15.refs_3_ = bf16[2,32,1024]{2,1,0:T(8,128)(2,1)S(1)} collective-permute-done((bf16[2,32,1024]{2,1,0:T(8,128)(2,1)S(1)}, bf16[2,32,1024]{2,1,0:T(8,128)(2,1)S(1)}, u32[]{:S(2)}, u32[]{:S(2)}) %collective-permute-start.15) | collective-permute-done | bytes 131104 | tf_op jit(solution)/shard_map/ppermute | solution.py:226
  56.2 2.0 %tiles.7 = bf16[8,2,33,8,1024]{4,3,2,1,0:T(8,128)(2,1)} custom-call(s32[2,33]{1,0:T(2,128)S(1)} %pad_add_fusion.refs_0_, bf16[32,1024]{1,0:T(8,128)(2,1)S(1)} %group_spectra.1.refs_1_, bf16[2,32,1024]{2,1,0:T(8,128)(2,1)S(1)} %collective-permute-done.14.refs_2_, ...), custom_call_target="tpu_custom_call", output_to_operand_aliasing={{}: (4, {})} | custom-call | flops 400000 | bytes 4 | tf_op jit(solution)/shard_map/tiles/pallas_call | solution.py:203
  (27 shorter events, 0.2 us)
Async XLA Ops:
  0.0 15.5 %copy-start = (s32[64,64]{1,0:T(8,128)S(1)}, s32[64,64]{1,0:T(8,128)}, u32[]{:S(2)}) copy-start(s32[64,64]{1,0:T(8,128)} %param.7) | copy-start | bytes 49156
  3.2 2.8 %collective-permute-start = (bf16[8,1024]{1,0:T(8,128)(2,1)}, bf16[8,1024]{1,0:T(8,128)(2,1)S(1)}, u32[]{:S(2)}, u32[]{:S(2)}) collective-permute-start(bf16[8,1024]{1,0:T(8,128)(2,1)} %get-tuple-element.16), channel_id=1, source_target_pairs={{0,1},{1,0},{2,3},{3,2},{4,5},{5,4},{6,7},{7,6},{8,9},{9,8},{10,11... | collective-permute-start | bytes 49160 | tf_op jit(solution)/shard_map/ppermute | solution.py:249
  3.3 4.0 %collective-permute-start.1 = (bf16[8,1024]{1,0:T(8,128)(2,1)}, bf16[8,1024]{1,0:T(8,128)(2,1)S(1)}, u32[]{:S(2)}, u32[]{:S(2)}) collective-permute-start(bf16[8,1024]{1,0:T(8,128)(2,1)} %get-tuple-element.17), channel_id=1, source_target_pairs={{0,2},{1,3},{2,0},{3,1},{4,6},{5,7},{6,4},{7,5},{8,10},{9,11},{10,... | collective-permute-start | bytes 49160 | tf_op jit(solution)/shard_map/ppermute | solution.py:249
  4.7 3.4 %collective-permute-start.2 = (bf16[8,1024]{1,0:T(8,128)(2,1)}, bf16[8,1024]{1,0:T(8,128)(2,1)S(1)}, u32[]{:S(2)}, u32[]{:S(2)}) collective-permute-start(bf16[8,1024]{1,0:T(8,128)(2,1)} %get-tuple-element.18), channel_id=1, source_target_pairs={{0,3},{1,2},{2,1},{3,0},{4,7},{5,6},{6,5},{7,4},{8,11},{9,10},{10,... | collective-permute-start | bytes 49160 | tf_op jit(solution)/shard_map/ppermute | solution.py:249
  8.1 10.8 %collective-permute-start.4 = (bf16[32,1024]{1,0:T(8,128)(2,1)S(1)}, bf16[32,1024]{1,0:T(8,128)(2,1)S(1)}, u32[]{:S(2)}, u32[]{:S(2)}) collective-permute-start(bf16[32,1024]{1,0:T(8,128)(2,1)S(1)} %group_spectra.1.refs_1_), channel_id=1, source_target_pairs={{0,192},{4,196},{8,200},{12,204},{16,208},{20,212},{24,216},{28,22... | collective-permute-start | bytes 196616 | tf_op jit(solution)/shard_map/ppermute | solution.py:226
  14.5 7.7 %collective-permute-start.9 = (bf16[32,1024]{1,0:T(8,128)(2,1)S(1)}, bf16[32,1024]{1,0:T(8,128)(2,1)S(1)}, u32[]{:S(2)}, u32[]{:S(2)}) collective-permute-start(bf16[32,1024]{1,0:T(8,128)(2,1)S(1)} %group_spectra.1.refs_1_), channel_id=1, source_target_pairs={{0,32},{4,36},{8,40},{12,44},{16,48},{20,52},{24,56},{28,60},{32,6... | collective-permute-start | bytes 196616 | tf_op jit(solution)/shard_map/ppermute | solution.py:226
  15.5 10.6 %collective-permute-start.10 = (bf16[32,1024]{1,0:T(8,128)(2,1)S(1)}, bf16[32,1024]{1,0:T(8,128)(2,1)S(1)}, u32[]{:S(2)}, u32[]{:S(2)}) collective-permute-start(bf16[32,1024]{1,0:T(8,128)(2,1)S(1)} %group_spectra.1.refs_1_), channel_id=1, source_target_pairs={{0,64},{4,68},{8,72},{12,76},{16,80},{20,84},{24,88},{28,92},{32,9... | collective-permute-start | bytes 196616 | tf_op jit(solution)/shard_map/ppermute | solution.py:226
  15.5 11.4 %collective-permute-start.3 = (bf16[32,1024]{1,0:T(8,128)(2,1)S(1)}, bf16[32,1024]{1,0:T(8,128)(2,1)S(1)}, u32[]{:S(2)}, u32[]{:S(2)}) collective-permute-start(bf16[32,1024]{1,0:T(8,128)(2,1)S(1)} %group_spectra.1.refs_1_), channel_id=1, source_target_pairs={{0,96},{4,100},{8,104},{12,108},{16,112},{20,116},{24,120},{28,124... | collective-permute-start | bytes 196616 | tf_op jit(solution)/shard_map/ppermute | solution.py:226
  18.9 7.9 %collective-permute-start.5 = (bf16[32,1024]{1,0:T(8,128)(2,1)S(1)}, bf16[32,1024]{1,0:T(8,128)(2,1)S(1)}, u32[]{:S(2)}, u32[]{:S(2)}) collective-permute-start(bf16[32,1024]{1,0:T(8,128)(2,1)S(1)} %collective-permute-done.4), channel_id=1, source_target_pairs={{0,192},{4,196},{8,200},{12,204},{16,208},{20,212},{24,216},{28,22... | collective-permute-start | bytes 196616 | tf_op jit(solution)/shard_map/ppermute | solution.py:226
  26.1 6.6 %collective-permute-start.11 = (bf16[2,32,1024]{2,1,0:T(8,128)(2,1)S(1)}, bf16[2,32,1024]{2,1,0:T(8,128)(2,1)S(1)}, u32[]{:S(2)}, u32[]{:S(2)}) collective-permute-start(bf16[2,32,1024]{2,1,0:T(8,128)(2,1)S(1)} %pad_maximum_fusion.4.refs_3_), channel_id=1, source_target_pairs={{0,16},{4,20},{8,24},{12,28},{16,0},{20,4},{24,8},{28,12},{32,48},... | collective-permute-start | bytes 393224 | tf_op jit(solution)/shard_map/ppermute | solution.py:226
  26.9 9.5 %collective-permute-start.6 = (bf16[2,32,1024]{2,1,0:T(8,128)(2,1)S(1)}, bf16[2,32,1024]{2,1,0:T(8,128)(2,1)S(1)}, u32[]{:S(2)}, u32[]{:S(2)}) collective-permute-start(bf16[2,32,1024]{2,1,0:T(8,128)(2,1)S(1)} %pad_maximum_fusion.3), channel_id=1, source_target_pairs={{0,16},{4,20},{8,24},{12,28},{16,0},{20,4},{24,8},{28,12},{32,48},... | collective-permute-start | bytes 393224 | tf_op jit(solution)/shard_map/ppermute | solution.py:226
  32.7 7.9 %collective-permute-start.12 = (bf16[4,32,1024]{2,1,0:T(8,128)(2,1)S(1)}, bf16[4,32,1024]{2,1,0:T(8,128)(2,1)S(1)}, u32[]{:S(2)}, u32[]{:S(2)}) collective-permute-start(bf16[4,32,1024]{2,1,0:T(8,128)(2,1)S(1)} %pad_maximum_fusion.2), channel_id=1, source_target_pairs={{0,4},{4,0},{8,12},{12,8},{16,20},{20,16},{24,28},{28,24},{32,36},... | collective-permute-start | bytes 786440 | tf_op jit(solution)/shard_map/ppermute | solution.py:226
  34.3 9.0 %collective-permute-start.13 = (bf16[4,32,1024]{2,1,0:T(8,128)(2,1)S(1)}, bf16[4,32,1024]{2,1,0:T(8,128)(2,1)S(1)}, u32[]{:S(2)}, u32[]{:S(2)}) collective-permute-start(bf16[4,32,1024]{2,1,0:T(8,128)(2,1)S(1)} %pad_maximum_fusion.2), channel_id=1, source_target_pairs={{0,12},{4,8},{8,4},{12,0},{16,28},{20,24},{24,20},{28,16},{32,44},... | collective-permute-start | bytes 786440 | tf_op jit(solution)/shard_map/ppermute | solution.py:226
  36.4 12.0 %collective-permute-start.7 = (bf16[4,32,1024]{2,1,0:T(8,128)(2,1)S(1)}, bf16[4,32,1024]{2,1,0:T(8,128)(2,1)S(1)}, u32[]{:S(2)}, u32[]{:S(2)}) collective-permute-start(bf16[4,32,1024]{2,1,0:T(8,128)(2,1)S(1)} %get-tuple-element.28), channel_id=1, source_target_pairs={{0,4},{4,0},{8,12},{12,8},{16,20},{20,16},{24,28},{28,24},{32,36},... | collective-permute-start | bytes 786440 | tf_op jit(solution)/shard_map/ppermute | solution.py:226
  37.1 11.3 %collective-permute-start.8 = (bf16[4,32,1024]{2,1,0:T(8,128)(2,1)S(1)}, bf16[4,32,1024]{2,1,0:T(8,128)(2,1)S(1)}, u32[]{:S(2)}, u32[]{:S(2)}) collective-permute-start(bf16[4,32,1024]{2,1,0:T(8,128)(2,1)S(1)} %get-tuple-element.27), channel_id=1, source_target_pairs={{0,12},{4,8},{8,4},{12,0},{16,28},{20,24},{24,20},{28,16},{32,44},... | collective-permute-start | bytes 786440 | tf_op jit(solution)/shard_map/ppermute | solution.py:226
  43.3 7.9 %collective-permute-start.16 = (bf16[2,32,1024]{2,1,0:T(8,128)(2,1)S(1)}, bf16[2,32,1024]{2,1,0:T(8,128)(2,1)S(1)}, u32[]{:S(2)}, u32[]{:S(2)}) collective-permute-start(bf16[2,32,1024]{2,1,0:T(8,128)(2,1)S(1)} %slice.14), channel_id=1, source_target_pairs={{0,4},{4,0},{8,12},{12,8},{16,20},{20,16},{24,28},{28,24},{32,36},... | collective-permute-start | bytes 393224 | tf_op jit(solution)/shard_map/ppermute | solution.py:226
  43.6 7.6 %collective-permute-start.17 = (bf16[2,32,1024]{2,1,0:T(8,128)(2,1)S(1)}, bf16[2,32,1024]{2,1,0:T(8,128)(2,1)S(1)}, u32[]{:S(2)}, u32[]{:S(2)}) collective-permute-start(bf16[2,32,1024]{2,1,0:T(8,128)(2,1)S(1)} %slice.15), channel_id=1, source_target_pairs={{0,12},{4,8},{8,4},{12,0},{16,28},{20,24},{24,20},{28,16},{32,44},... | collective-permute-start | bytes 393224 | tf_op jit(solution)/shard_map/ppermute | solution.py:226
  48.4 6.1 %collective-permute-start.14 = (bf16[2,32,1024]{2,1,0:T(8,128)(2,1)S(1)}, bf16[2,32,1024]{2,1,0:T(8,128)(2,1)S(1)}, u32[]{:S(2)}, u32[]{:S(2)}) collective-permute-start(bf16[2,32,1024]{2,1,0:T(8,128)(2,1)S(1)} %slice.12), channel_id=1, source_target_pairs={{0,4},{4,0},{8,12},{12,8},{16,20},{20,16},{24,28},{28,24},{32,36},... | collective-permute-start | bytes 393224 | tf_op jit(solution)/shard_map/ppermute | solution.py:226
  49.9 6.3 %collective-permute-start.15 = (bf16[2,32,1024]{2,1,0:T(8,128)(2,1)S(1)}, bf16[2,32,1024]{2,1,0:T(8,128)(2,1)S(1)}, u32[]{:S(2)}, u32[]{:S(2)}) collective-permute-start(bf16[2,32,1024]{2,1,0:T(8,128)(2,1)S(1)} %slice.13), channel_id=1, source_target_pairs={{0,12},{4,8},{8,4},{12,0},{16,28},{20,24},{24,20},{28,16},{32,44},... | collective-permute-start | bytes 393224 | tf_op jit(solution)/shard_map/ppermute | solution.py:226

commit v5 on v4

--- a/solution.py
+++ b/solution.py
@@ -263,15 +263,13 @@
             back = jnp.where(ry * N_X + rx < y * N_X + x, 0, 4)
         return ((z - back) % N_Z) * (N_Y * N_X) + ry * N_X + rx
 
-    def froms_a(mask):
-        return [(1, 0, mask), (2, 0, mask), (1, 1, mask), (2, 1, mask)]
+    def froms_a(other):
+        return [(back, other, mask) for mask in (0, 1, 3, 2) for back in (1, 2)]
 
     froms = [
         [(0, 0, 0)] + froms_a(0) + [(3, 0, 0), (4, 0, 0), (3, 1, 0), (None, 1, 0)],
-        froms_a(1) + froms_a(3),
-        froms_a(2)
-        + [(3, 1, 1), (None, 1, 1), (3, 0, 1), (None, 0, 1), (3, 0, 3), (None, 0, 3), (3, 1, 3), (None, 1, 3)],
-        [(3, 0, 2), (None, 0, 2), (3, 1, 2), (None, 1, 2)],
+        [(3, 1, 1), (None, 1, 1), (3, 0, 1), (None, 0, 1), (3, 0, 3), (None, 0, 3), (3, 1, 3), (None, 1, 3)],
+        froms_a(1) + [(3, 0, 2), (None, 0, 2), (3, 1, 2), (None, 1, 2)],
     ]
     origin = jnp.stack([where_from(*o) for some in froms for o in some]).astype(jnp.int32)
     keep_row = lax.dynamic_index_in_dim(keeper, group, 0, keepdims=False)
@@ -285,21 +283,19 @@
     def add(call, blocks, result):
         return tiles(slots, bases[call], own, blocks, result, n_slots)
 
-    ya = across_y(za)
-    a = jnp.concatenate([za, ya])
-    a1, a3 = swap_x(a, 1), swap_x(a, 3)
+    a1, a3 = swap_x(za, 1), swap_x(za, 3)
+    ar1, ar3 = swap_x(a3[:1], 1), swap_x(a1[1:], 3)
     s1, s3, sy = (jnp.where(here, own, z4) for here in (x % 2 == 0, x < 2, y == 0))
     yb = across_y(jnp.stack([z3, sy]))
+    row = jnp.concatenate([za, a1, a3, ar1, ar3])
+    ya = across_y(row)
     b1 = swap_x(jnp.concatenate([yb, jnp.stack([z3, s1])]), 1)
     b3 = swap_x(jnp.concatenate([jnp.stack([z3, s3]), yb]), 3)
-    result = add(0, [own[None], za, ya, z3[None], z4[None], yb], None)
-    a1, a3, result = lax.optimization_barrier((a1, a3, result))
-    ar1, ar3 = swap_x(a3[:2], 1), swap_x(a1[2:], 3)
-    result = add(1, [a1, a3], result)
+    result = add(0, [own[None], row, z3[None], z4[None], yb], None)
     b1, b3, result = lax.optimization_barrier((b1, b3, result))
     br1, br3 = swap_x(b3[:2], 1), swap_x(b1[:2], 3)
-    result = add(2, [ar1, ar3, b1, b3], result)
-    result = add(3, [br1, br3], result)
+    result = add(1, [b1, b3], result)
+    result = add(2, [ya, br1, br3], result)
     return result.reshape(8, 2, n_slots * 8, CH_WIN).swapaxes(2, 3)
 
 

time: 58.5 us -> 60.1 us (1.027); the launches traced: 58.3 us -> 58.9 us
  waiting for transfers between devices: 12.9 us -> 15.3 us
  Pallas kernels: 14 us -> 12.7 us
  starting transfers between devices: 29.9 us -> 29.1 us
    ppermute x15, waiting for transfers between devices: 10.9 us -> 13.6 us  [move(): lax.ppermute(array, 'stn', [(number(*p), number(*target(*p))) for p in pl...]
    pallas_call x4 -> x3, Pallas kernels: 10.8 us -> 9.43 us  [tiles(): pl.pallas_call(functools.partial(tiles_kernel, base, counts, aliased), ou...]
    ppermute x15, starting transfers between devices: 27.9 us -> 27.2 us  [move(): lax.ppermute(array, 'stn', [(number(*p), number(*target(*p))) for p in pl...]
  transfers between devices with their start and end apart: 18 -> 18, of which waited for: 6 -> 9; matrix products, arithmetic and copies ran while one was open for 2% -> 2% of each run, Pallas kernels for 15% -> 10%
where the time goes in v5:
time: 60.1 us; the launch traced here: 58.9 us
  starting transfers between devices  29.1 us (48%)
  waiting for transfers between devices  15.3 us (25%)
  Pallas kernels  12.7 us (21%)
  other arithmetic  1.01 us (2%)
  between operations  0.62 us (1%)
    ppermute x15, starting transfers between devices, move(): lax.ppermute(array, 'stn', [(number(*p), number(*target(*p))) for p in pl...  27.2 us
    ppermute x15, waiting for transfers between devices, move(): lax.ppermute(array, 'stn', [(number(*p), number(*target(*p))) for p in pl...  13.6 us
    pallas_call x3, Pallas kernels, tiles(): pl.pallas_call(functools.partial(tiles_kernel, base, counts, aliased), ou...  9.43 us
    pallas_call x1, Pallas kernels, spectra(): pl.pallas_call(spectra_kernel, out_shape=[jax.ShapeDtypeStruct((8, CH_WIN...  3.18 us
    ppermute x3, starting transfers between devices, per_device(): lax.ppermute(part, 'chan', [(c, c ^ d) for c in range(4)])  1.96 us
    ppermute x3, waiting for transfers between devices, per_device(): lax.ppermute(part, 'chan', [(c, c ^ d) for c in range(4)])  1.69 us
  transfers between devices with their start and end apart: 18, of which 9 were waited for; matrix products, arithmetic and copies ran while one was open for 2% of the time, Pallas kernels for 10%

profile of v5, /device:TPU:16, one launch (start us, length us, event | category | flops | bytes accessed | tf_op | source)
XLA Modules:
  0.0 58.9 jit_solution(16110414004926425186)
XLA Ops:
  0.0 3.2 %spectra.1 = (bf16[8,1024]{1,0:T(8,128)(2,1)}, bf16[8,1024]{1,0:T(8,128)(2,1)}, bf16[8,1024]{1,0:T(8,128)(2,1)}, bf16[8,1024]{1,0:T(8,128)(2,1)}) custom-call(bf16[2,17,128,128]{3,2,1,0:T(8,128)(2,1)} %bitcast.66, f32[16,128,128]{2,1,0:T(8,128)} %constant.179.clone.refs_1_, f32[128,128]{1,0:T(8,128)} %constant.180.clone.refs_2_, ...), custom_call_target="tpu_custom_call" | custom-call | tf_op jit(solution)/shard_map/spectra/pallas_call | solution.py:114
  3.2 0.1 collective-permute-start
  3.3 1.4 %collective-permute-start.1 = (bf16[8,1024]{1,0:T(8,128)(2,1)}, bf16[8,1024]{1,0:T(8,128)(2,1)S(1)}, u32[]{:S(2)}, u32[]{:S(2)}) collective-permute-start(bf16[8,1024]{1,0:T(8,128)(2,1)} %get-tuple-element.14), channel_id=1, source_target_pairs={{0,2},{1,3},{2,0},{3,1},{4,6},{5,7},{6,4},{7,5},{8,10},{9,11},{10,... | collective-permute-start | bytes 49160 | tf_op jit(solution)/shard_map/ppermute | solution.py:249
  4.7 0.5 collective-permute-start.2
  5.2 0.7 %broadcast_select_fusion.refs_0_ = bf16[8,1024]{1,0:T(8,128)(2,1)S(1)} fusion(bf16[8,1024]{1,0:T(8,128)(2,1)} %get-tuple-element.12, pred[]{:T(512)S(6)} %lt.164), kind=kLoop, calls=%fused_computation.11 | loop fusion | flops 8192 | bytes 32769 | tf_op jit(solution)/shard_map/jit(_where)/select_n | solution.py:252
  6.2 0.1 stack.166
  6.4 1.0 %collective-permute-done.1.refs_2_ = bf16[8,1024]{1,0:T(8,128)(2,1)S(1)} collective-permute-done((bf16[8,1024]{1,0:T(8,128)(2,1)}, bf16[8,1024]{1,0:T(8,128)(2,1)S(1)}, u32[]{:S(2)}, u32[]{:S(2)}) %collective-permute-start.1) | collective-permute-done | bytes 16416 | tf_op jit(solution)/shard_map/ppermute | solution.py:249
  7.3 0.7 %collective-permute-done.2.refs_3_ = bf16[8,1024]{1,0:T(8,128)(2,1)S(1)} collective-permute-done((bf16[8,1024]{1,0:T(8,128)(2,1)}, bf16[8,1024]{1,0:T(8,128)(2,1)S(1)}, u32[]{:S(2)}, u32[]{:S(2)}) %collective-permute-start.2) | collective-permute-done | bytes 16416 | tf_op jit(solution)/shard_map/ppermute | solution.py:249
  8.1 3.3 %collective-permute-start.4 = (bf16[32,1024]{1,0:T(8,128)(2,1)S(1)}, bf16[32,1024]{1,0:T(8,128)(2,1)S(1)}, u32[]{:S(2)}, u32[]{:S(2)}) collective-permute-start(bf16[32,1024]{1,0:T(8,128)(2,1)S(1)} %group_spectra.1.refs_1_), channel_id=1, source_target_pairs={{0,64},{4,68},{8,72},{12,76},{16,80},{20,84},{24,88},{28,92},{32,9... | collective-permute-start | bytes 196616 | tf_op jit(solution)/shard_map/ppermute | solution.py:226
  11.4 1.9 %collective-permute-start.3 = (bf16[32,1024]{1,0:T(8,128)(2,1)S(1)}, bf16[32,1024]{1,0:T(8,128)(2,1)S(1)}, u32[]{:S(2)}, u32[]{:S(2)}) collective-permute-start(bf16[32,1024]{1,0:T(8,128)(2,1)S(1)} %group_spectra.1.refs_1_), channel_id=1, source_target_pairs={{0,32},{4,36},{8,40},{12,44},{16,48},{20,52},{24,56},{28,60},{32,6... | collective-permute-start | bytes 196616 | tf_op jit(solution)/shard_map/ppermute | solution.py:226
  13.4 0.2 select_reduce_fusion
  13.5 2.3 %collective-permute-start.11 = (bf16[32,1024]{1,0:T(8,128)(2,1)S(1)}, bf16[32,1024]{1,0:T(8,128)(2,1)S(1)}, u32[]{:S(2)}, u32[]{:S(2)}) collective-permute-start(bf16[32,1024]{1,0:T(8,128)(2,1)S(1)} %group_spectra.1.refs_1_), channel_id=1, source_target_pairs={{0,192},{4,196},{8,200},{12,204},{16,208},{20,212},{24,216},{28,22... | collective-permute-start | bytes 196616 | tf_op jit(solution)/shard_map/ppermute | solution.py:226
  15.8 3.3 %collective-permute-start.10 = (bf16[32,1024]{1,0:T(8,128)(2,1)S(1)}, bf16[32,1024]{1,0:T(8,128)(2,1)S(1)}, u32[]{:S(2)}, u32[]{:S(2)}) collective-permute-start(bf16[32,1024]{1,0:T(8,128)(2,1)S(1)} %group_spectra.1.refs_1_), channel_id=1, source_target_pairs={{0,96},{4,100},{8,104},{12,108},{16,112},{20,116},{24,120},{28,124... | collective-permute-start | bytes 196616 | tf_op jit(solution)/shard_map/ppermute | solution.py:226
  19.1 0.1 collective-permute-done.3
  19.3 2.8 %collective-permute-start.6 = (bf16[2,32,1024]{2,1,0:T(8,128)(2,1)S(1)}, bf16[2,32,1024]{2,1,0:T(8,128)(2,1)S(1)}, u32[]{:S(2)}, u32[]{:S(2)}) collective-permute-start(bf16[2,32,1024]{2,1,0:T(8,128)(2,1)S(1)} %pad_maximum_fusion.2), channel_id=1, source_target_pairs={{0,12},{4,8},{8,4},{12,0},{16,28},{20,24},{24,20},{28,16},{32,44},... | collective-permute-start | bytes 393224 | tf_op jit(solution)/shard_map/ppermute | solution.py:226
  22.1 0.2 collective-permute-start.5
  22.3 3.7 %collective-permute-start.12 = (bf16[32,1024]{1,0:T(8,128)(2,1)S(1)}, bf16[32,1024]{1,0:T(8,128)(2,1)S(1)}, u32[]{:S(2)}, u32[]{:S(2)}) collective-permute-start(bf16[32,1024]{1,0:T(8,128)(2,1)S(1)} %collective-permute-done.11), channel_id=1, source_target_pairs={{0,192},{4,196},{8,200},{12,204},{16,208},{20,212},{24,216},{28,22... | collective-permute-start | bytes 196616 | tf_op jit(solution)/shard_map/ppermute | solution.py:226
  26.0 2.0 %collective-permute-done.12 = bf16[32,1024]{1,0:T(8,128)(2,1)S(1)} collective-permute-done((bf16[32,1024]{1,0:T(8,128)(2,1)S(1)}, bf16[32,1024]{1,0:T(8,128)(2,1)S(1)}, u32[]{:S(2)}, u32[]{:S(2)}) %collective-permute-start.12) | collective-permute-done | bytes 65568 | tf_op jit(solution)/shard_map/ppermute | solution.py:226
  28.1 0.7 %collective-permute-start.13 = (bf16[2,32,1024]{2,1,0:T(8,128)(2,1)S(1)}, bf16[2,32,1024]{2,1,0:T(8,128)(2,1)S(1)}, u32[]{:S(2)}, u32[]{:S(2)}) collective-permute-start(bf16[2,32,1024]{2,1,0:T(8,128)(2,1)S(1)} %pad_maximum_fusion.3), channel_id=1, source_target_pairs={{0,16},{4,20},{8,24},{12,28},{16,0},{20,4},{24,8},{28,12},{32,48},... | collective-permute-start | bytes 393224 | tf_op jit(solution)/shard_map/ppermute | solution.py:226
  28.8 1.9 %collective-permute-start.7 = (bf16[1,32,1024]{2,1,0:T(8,128)(2,1)S(1)}, bf16[1,32,1024]{2,1,0:T(8,128)(2,1)S(1)}, u32[]{:S(2)}, u32[]{:S(2)}) collective-permute-start(bf16[1,32,1024]{2,1,0:T(8,128)(2,1)S(1)} %slice.16), channel_id=1, source_target_pairs={{0,4},{4,0},{8,12},{12,8},{16,20},{20,16},{24,28},{28,24},{32,36},... | collective-permute-start | bytes 196616 | tf_op jit(solution)/shard_map/ppermute | solution.py:226
  30.7 0.9 %collective-permute-start.8 = (bf16[1,32,1024]{2,1,0:T(8,128)(2,1)S(1)}, bf16[1,32,1024]{2,1,0:T(8,128)(2,1)S(1)}, u32[]{:S(2)}, u32[]{:S(2)}) collective-permute-start(bf16[1,32,1024]{2,1,0:T(8,128)(2,1)S(1)} %slice.17), channel_id=1, source_target_pairs={{0,12},{4,8},{8,4},{12,0},{16,28},{20,24},{24,20},{28,16},{32,44},... | collective-permute-start | bytes 196616 | tf_op jit(solution)/shard_map/ppermute | solution.py:226
  31.6 1.5 %collective-permute-done.7 = bf16[1,32,1024]{2,1,0:T(8,128)(2,1)S(1)} collective-permute-done((bf16[1,32,1024]{2,1,0:T(8,128)(2,1)S(1)}, bf16[1,32,1024]{2,1,0:T(8,128)(2,1)S(1)}, u32[]{:S(2)}, u32[]{:S(2)}) %collective-permute-start.7) | collective-permute-done | bytes 65568 | tf_op jit(solution)/shard_map/ppermute | solution.py:226
  33.1 3.1 %collective-permute-done.8 = bf16[1,32,1024]{2,1,0:T(8,128)(2,1)S(1)} collective-permute-done((bf16[1,32,1024]{2,1,0:T(8,128)(2,1)S(1)}, bf16[1,32,1024]{2,1,0:T(8,128)(2,1)S(1)}, u32[]{:S(2)}, u32[]{:S(2)}) %collective-permute-start.8) | collective-permute-done | bytes 65568 | tf_op jit(solution)/shard_map/ppermute | solution.py:226
  36.3 2.9 %collective-permute-start.9 = (bf16[8,32,1024]{2,1,0:T(8,128)(2,1)S(1)}, bf16[8,32,1024]{2,1,0:T(8,128)(2,1)S(1)}, u32[]{:S(2)}, u32[]{:S(2)}) collective-permute-start(bf16[8,32,1024]{2,1,0:T(8,128)(2,1)S(1)} %constant_dynamic-update-slice_fusion.refs_3_), channel_id=1, source_target_pairs={{0,16},{4,20},{8,24},{12,28},{16,0},{20,4},{24,8},{28,12},{32,48},... | collective-permute-start | bytes 1572872 | tf_op jit(solution)/shard_map/ppermute | solution.py:226
  39.2 0.8 %collective-permute-start.15 = (bf16[4,32,1024]{2,1,0:T(8,128)(2,1)S(1)}, bf16[4,32,1024]{2,1,0:T(8,128)(2,1)S(1)}, u32[]{:S(2)}, u32[]{:S(2)}) collective-permute-start(bf16[4,32,1024]{2,1,0:T(8,128)(2,1)S(1)} %get-tuple-element.21), channel_id=1, source_target_pairs={{0,12},{4,8},{8,4},{12,0},{16,28},{20,24},{24,20},{28,16},{32,44},... | collective-permute-start | bytes 786440 | tf_op jit(solution)/shard_map/ppermute | solution.py:226
  40.1 3.5 %tiles.3.refs_4_ = bf16[8,2,33,8,1024]{4,3,2,1,0:T(8,128)(2,1)} custom-call(s32[2,33]{1,0:T(2,128)S(1)} %pad_add_fusion.refs_0_, bf16[32,1024]{1,0:T(8,128)(2,1)S(1)} %group_spectra.1.refs_1_, bf16[1,32,1024]{2,1,0:T(8,128)(2,1)S(1)} %bitcast.61, bf16[8,32,1024]{2,1,0:T(8,128)(2,1)S(1)} %constant_dynamic-update-slice_fusion.refs_3_, ...), custom_call_target="tpu_custom_call" | custom-call | flops 1300000 | bytes 13 | tf_op jit(solution)/shard_map/tiles/pallas_call | solution.py:203
  43.6 4.5 %collective-permute-done.15.refs_3_ = bf16[4,32,1024]{2,1,0:T(8,128)(2,1)S(1)} collective-permute-done((bf16[4,32,1024]{2,1,0:T(8,128)(2,1)S(1)}, bf16[4,32,1024]{2,1,0:T(8,128)(2,1)S(1)}, u32[]{:S(2)}, u32[]{:S(2)}) %collective-permute-start.15) | collective-permute-done | bytes 262176 | tf_op jit(solution)/shard_map/ppermute | solution.py:226
  48.1 2.4 %collective-permute-start.17 = (bf16[2,32,1024]{2,1,0:T(8,128)(2,1)S(1)}, bf16[2,32,1024]{2,1,0:T(8,128)(2,1)S(1)}, u32[]{:S(2)}, u32[]{:S(2)}) collective-permute-start(bf16[2,32,1024]{2,1,0:T(8,128)(2,1)S(1)} %slice.15), channel_id=1, source_target_pairs={{0,12},{4,8},{8,4},{12,0},{16,28},{20,24},{24,20},{28,16},{32,44},... | collective-permute-start | bytes 393224 | tf_op jit(solution)/shard_map/ppermute | solution.py:226
  50.4 2.7 %tiles.4.refs_5_ = bf16[8,2,33,8,1024]{4,3,2,1,0:T(8,128)(2,1)} custom-call(s32[2,33]{1,0:T(2,128)S(1)} %pad_add_fusion.refs_0_, bf16[32,1024]{1,0:T(8,128)(2,1)S(1)} %group_spectra.1.refs_1_, bf16[4,32,1024]{2,1,0:T(8,128)(2,1)S(1)} %collective-permute-done.14.refs_2_, ...), custom_call_target="tpu_custom_call", output_to_operand_aliasing={{}: (4, {})} | custom-call | flops 800000 | bytes 8 | tf_op jit(solution)/shard_map/tiles/pallas_call | solution.py:203
  53.1 1.2 %collective-permute-done.17.refs_4_ = bf16[2,32,1024]{2,1,0:T(8,128)(2,1)S(1)} collective-permute-done((bf16[2,32,1024]{2,1,0:T(8,128)(2,1)S(1)}, bf16[2,32,1024]{2,1,0:T(8,128)(2,1)S(1)}, u32[]{:S(2)}, u32[]{:S(2)}) %collective-permute-start.17) | collective-permute-done | bytes 131104 | tf_op jit(solution)/shard_map/ppermute | solution.py:226
  54.3 1.1 %collective-permute-done.16.refs_3_ = bf16[2,32,1024]{2,1,0:T(8,128)(2,1)S(1)} collective-permute-done((bf16[2,32,1024]{2,1,0:T(8,128)(2,1)S(1)}, bf16[2,32,1024]{2,1,0:T(8,128)(2,1)S(1)}, u32[]{:S(2)}, u32[]{:S(2)}) %collective-permute-start.16) | collective-permute-done | bytes 131104 | tf_op jit(solution)/shard_map/ppermute | solution.py:226
  55.4 3.3 %tiles.5 = bf16[8,2,33,8,1024]{4,3,2,1,0:T(8,128)(2,1)} custom-call(s32[2,33]{1,0:T(2,128)S(1)} %pad_add_fusion.refs_0_, bf16[32,1024]{1,0:T(8,128)(2,1)S(1)} %group_spectra.1.refs_1_, bf16[8,32,1024]{2,1,0:T(8,128)(2,1)S(1)} %collective-permute-done.9.refs_2_, ...), custom_call_target="tpu_custom_call", output_to_operand_aliasing={{}: (5, {})} | custom-call | flops 1200000 | bytes 12 | tf_op jit(solution)/shard_map/tiles/pallas_call | solution.py:203
  (31 shorter events, 0.4 us)
Async XLA Ops:
  0.0 5.9 %copy-start = (s32[64,64]{1,0:T(8,128)S(1)}, s32[64,64]{1,0:T(8,128)}, u32[]{:S(2)}) copy-start(s32[64,64]{1,0:T(8,128)} %param.7) | copy-start | bytes 49156
  3.2 3.1 %collective-permute-start = (bf16[8,1024]{1,0:T(8,128)(2,1)}, bf16[8,1024]{1,0:T(8,128)(2,1)S(1)}, u32[]{:S(2)}, u32[]{:S(2)}) collective-permute-start(bf16[8,1024]{1,0:T(8,128)(2,1)} %get-tuple-element.13), channel_id=1, source_target_pairs={{0,1},{1,0},{2,3},{3,2},{4,5},{5,4},{6,7},{7,6},{8,9},{9,8},{10,11... | collective-permute-start | bytes 49160 | tf_op jit(solution)/shard_map/ppermute | solution.py:249
  3.3 4.0 %collective-permute-start.1 = (bf16[8,1024]{1,0:T(8,128)(2,1)}, bf16[8,1024]{1,0:T(8,128)(2,1)S(1)}, u32[]{:S(2)}, u32[]{:S(2)}) collective-permute-start(bf16[8,1024]{1,0:T(8,128)(2,1)} %get-tuple-element.14), channel_id=1, source_target_pairs={{0,2},{1,3},{2,0},{3,1},{4,6},{5,7},{6,4},{7,5},{8,10},{9,11},{10,... | collective-permute-start | bytes 49160 | tf_op jit(solution)/shard_map/ppermute | solution.py:249
  4.7 3.4 %collective-permute-start.2 = (bf16[8,1024]{1,0:T(8,128)(2,1)}, bf16[8,1024]{1,0:T(8,128)(2,1)S(1)}, u32[]{:S(2)}, u32[]{:S(2)}) collective-permute-start(bf16[8,1024]{1,0:T(8,128)(2,1)} %get-tuple-element.15), channel_id=1, source_target_pairs={{0,3},{1,2},{2,1},{3,0},{4,7},{5,6},{6,5},{7,4},{8,11},{9,10},{10,... | collective-permute-start | bytes 49160 | tf_op jit(solution)/shard_map/ppermute | solution.py:249
  8.1 11.0 %collective-permute-start.4 = (bf16[32,1024]{1,0:T(8,128)(2,1)S(1)}, bf16[32,1024]{1,0:T(8,128)(2,1)S(1)}, u32[]{:S(2)}, u32[]{:S(2)}) collective-permute-start(bf16[32,1024]{1,0:T(8,128)(2,1)S(1)} %group_spectra.1.refs_1_), channel_id=1, source_target_pairs={{0,64},{4,68},{8,72},{12,76},{16,80},{20,84},{24,88},{28,92},{32,9... | collective-permute-start | bytes 196616 | tf_op jit(solution)/shard_map/ppermute | solution.py:226
  11.4 7.8 %collective-permute-start.3 = (bf16[32,1024]{1,0:T(8,128)(2,1)S(1)}, bf16[32,1024]{1,0:T(8,128)(2,1)S(1)}, u32[]{:S(2)}, u32[]{:S(2)}) collective-permute-start(bf16[32,1024]{1,0:T(8,128)(2,1)S(1)} %group_spectra.1.refs_1_), channel_id=1, source_target_pairs={{0,32},{4,36},{8,40},{12,44},{16,48},{20,52},{24,56},{28,60},{32,6... | collective-permute-start | bytes 196616 | tf_op jit(solution)/shard_map/ppermute | solution.py:226
  13.5 8.8 %collective-permute-start.11 = (bf16[32,1024]{1,0:T(8,128)(2,1)S(1)}, bf16[32,1024]{1,0:T(8,128)(2,1)S(1)}, u32[]{:S(2)}, u32[]{:S(2)}) collective-permute-start(bf16[32,1024]{1,0:T(8,128)(2,1)S(1)} %group_spectra.1.refs_1_), channel_id=1, source_target_pairs={{0,192},{4,196},{8,200},{12,204},{16,208},{20,212},{24,216},{28,22... | collective-permute-start | bytes 196616 | tf_op jit(solution)/shard_map/ppermute | solution.py:226
  15.8 12.2 %collective-permute-start.10 = (bf16[32,1024]{1,0:T(8,128)(2,1)S(1)}, bf16[32,1024]{1,0:T(8,128)(2,1)S(1)}, u32[]{:S(2)}, u32[]{:S(2)}) collective-permute-start(bf16[32,1024]{1,0:T(8,128)(2,1)S(1)} %group_spectra.1.refs_1_), channel_id=1, source_target_pairs={{0,96},{4,100},{8,104},{12,108},{16,112},{20,116},{24,120},{28,124... | collective-permute-start | bytes 196616 | tf_op jit(solution)/shard_map/ppermute | solution.py:226
  19.3 9.5 %collective-permute-start.6 = (bf16[2,32,1024]{2,1,0:T(8,128)(2,1)S(1)}, bf16[2,32,1024]{2,1,0:T(8,128)(2,1)S(1)}, u32[]{:S(2)}, u32[]{:S(2)}) collective-permute-start(bf16[2,32,1024]{2,1,0:T(8,128)(2,1)S(1)} %pad_maximum_fusion.2), channel_id=1, source_target_pairs={{0,12},{4,8},{8,4},{12,0},{16,28},{20,24},{24,20},{28,16},{32,44},... | collective-permute-start | bytes 393224 | tf_op jit(solution)/shard_map/ppermute | solution.py:226
  22.1 8.6 %collective-permute-start.5 = (bf16[2,32,1024]{2,1,0:T(8,128)(2,1)S(1)}, bf16[2,32,1024]{2,1,0:T(8,128)(2,1)S(1)}, u32[]{:S(2)}, u32[]{:S(2)}) collective-permute-start(bf16[2,32,1024]{2,1,0:T(8,128)(2,1)S(1)} %pad_maximum_fusion.2), channel_id=1, source_target_pairs={{0,4},{4,0},{8,12},{12,8},{16,20},{20,16},{24,28},{28,24},{32,36},... | collective-permute-start | bytes 393224 | tf_op jit(solution)/shard_map/ppermute | solution.py:226
  22.3 5.7 %collective-permute-start.12 = (bf16[32,1024]{1,0:T(8,128)(2,1)S(1)}, bf16[32,1024]{1,0:T(8,128)(2,1)S(1)}, u32[]{:S(2)}, u32[]{:S(2)}) collective-permute-start(bf16[32,1024]{1,0:T(8,128)(2,1)S(1)} %collective-permute-done.11), channel_id=1, source_target_pairs={{0,192},{4,196},{8,200},{12,204},{16,208},{20,212},{24,216},{28,22... | collective-permute-start | bytes 196616 | tf_op jit(solution)/shard_map/ppermute | solution.py:226
  28.1 11.1 %collective-permute-start.13 = (bf16[2,32,1024]{2,1,0:T(8,128)(2,1)S(1)}, bf16[2,32,1024]{2,1,0:T(8,128)(2,1)S(1)}, u32[]{:S(2)}, u32[]{:S(2)}) collective-permute-start(bf16[2,32,1024]{2,1,0:T(8,128)(2,1)S(1)} %pad_maximum_fusion.3), channel_id=1, source_target_pairs={{0,16},{4,20},{8,24},{12,28},{16,0},{20,4},{24,8},{28,12},{32,48},... | collective-permute-start | bytes 393224 | tf_op jit(solution)/shard_map/ppermute | solution.py:226
  28.8 4.4 %collective-permute-start.7 = (bf16[1,32,1024]{2,1,0:T(8,128)(2,1)S(1)}, bf16[1,32,1024]{2,1,0:T(8,128)(2,1)S(1)}, u32[]{:S(2)}, u32[]{:S(2)}) collective-permute-start(bf16[1,32,1024]{2,1,0:T(8,128)(2,1)S(1)} %slice.16), channel_id=1, source_target_pairs={{0,4},{4,0},{8,12},{12,8},{16,20},{20,16},{24,28},{28,24},{32,36},... | collective-permute-start | bytes 196616 | tf_op jit(solution)/shard_map/ppermute | solution.py:226
  30.7 5.6 %collective-permute-start.8 = (bf16[1,32,1024]{2,1,0:T(8,128)(2,1)S(1)}, bf16[1,32,1024]{2,1,0:T(8,128)(2,1)S(1)}, u32[]{:S(2)}, u32[]{:S(2)}) collective-permute-start(bf16[1,32,1024]{2,1,0:T(8,128)(2,1)S(1)} %slice.17), channel_id=1, source_target_pairs={{0,12},{4,8},{8,4},{12,0},{16,28},{20,24},{24,20},{28,16},{32,44},... | collective-permute-start | bytes 196616 | tf_op jit(solution)/shard_map/ppermute | solution.py:226
  36.3 19.1 %collective-permute-start.9 = (bf16[8,32,1024]{2,1,0:T(8,128)(2,1)S(1)}, bf16[8,32,1024]{2,1,0:T(8,128)(2,1)S(1)}, u32[]{:S(2)}, u32[]{:S(2)}) collective-permute-start(bf16[8,32,1024]{2,1,0:T(8,128)(2,1)S(1)} %constant_dynamic-update-slice_fusion.refs_3_), channel_id=1, source_target_pairs={{0,16},{4,20},{8,24},{12,28},{16,0},{20,4},{24,8},{28,12},{32,48},... | collective-permute-start | bytes 1572872 | tf_op jit(solution)/shard_map/ppermute | solution.py:226
  39.2 8.8 %collective-permute-start.15 = (bf16[4,32,1024]{2,1,0:T(8,128)(2,1)S(1)}, bf16[4,32,1024]{2,1,0:T(8,128)(2,1)S(1)}, u32[]{:S(2)}, u32[]{:S(2)}) collective-permute-start(bf16[4,32,1024]{2,1,0:T(8,128)(2,1)S(1)} %get-tuple-element.21), channel_id=1, source_target_pairs={{0,12},{4,8},{8,4},{12,0},{16,28},{20,24},{24,20},{28,16},{32,44},... | collective-permute-start | bytes 786440 | tf_op jit(solution)/shard_map/ppermute | solution.py:226
  40.0 8.0 %collective-permute-start.14 = (bf16[4,32,1024]{2,1,0:T(8,128)(2,1)S(1)}, bf16[4,32,1024]{2,1,0:T(8,128)(2,1)S(1)}, u32[]{:S(2)}, u32[]{:S(2)}) collective-permute-start(bf16[4,32,1024]{2,1,0:T(8,128)(2,1)S(1)} %get-tuple-element.22), channel_id=1, source_target_pairs={{0,4},{4,0},{8,12},{12,8},{16,20},{20,16},{24,28},{28,24},{32,36},... | collective-permute-start | bytes 786440 | tf_op jit(solution)/shard_map/ppermute | solution.py:226
  48.1 6.3 %collective-permute-start.17 = (bf16[2,32,1024]{2,1,0:T(8,128)(2,1)S(1)}, bf16[2,32,1024]{2,1,0:T(8,128)(2,1)S(1)}, u32[]{:S(2)}, u32[]{:S(2)}) collective-permute-start(bf16[2,32,1024]{2,1,0:T(8,128)(2,1)S(1)} %slice.15), channel_id=1, source_target_pairs={{0,12},{4,8},{8,4},{12,0},{16,28},{20,24},{24,20},{28,16},{32,44},... | collective-permute-start | bytes 393224 | tf_op jit(solution)/shard_map/ppermute | solution.py:226
  50.4 5.0 %collective-permute-start.16 = (bf16[2,32,1024]{2,1,0:T(8,128)(2,1)S(1)}, bf16[2,32,1024]{2,1,0:T(8,128)(2,1)S(1)}, u32[]{:S(2)}, u32[]{:S(2)}) collective-permute-start(bf16[2,32,1024]{2,1,0:T(8,128)(2,1)S(1)} %slice.14), channel_id=1, source_target_pairs={{0,4},{4,0},{8,12},{12,8},{16,20},{20,16},{24,28},{28,24},{32,36},... | collective-permute-start | bytes 393224 | tf_op jit(solution)/shard_map/ppermute | solution.py:226

commit v6 on v5

--- a/solution.py
+++ b/solution.py
@@ -285,6 +285,7 @@
 
     a1, a3 = swap_x(za, 1), swap_x(za, 3)
     ar1, ar3 = swap_x(a3[:1], 1), swap_x(a1[1:], 3)
+    z3, z4, a1, a3 = lax.optimization_barrier((z3, z4, a1, a3))
     s1, s3, sy = (jnp.where(here, own, z4) for here in (x % 2 == 0, x < 2, y == 0))
     yb = across_y(jnp.stack([z3, sy]))
     row = jnp.concatenate([za, a1, a3, ar1, ar3])

time: 60.1 us -> 58.2 us (0.968)
  waiting for transfers between devices: 15.3 us -> 14.3 us
    ppermute x15, waiting for transfers between devices: 13.6 us -> 12.6 us  [move(): lax.ppermute(array, 'stn', [(number(*p), number(*target(*p))) for p in pl...]
  transfers between devices with their start and end apart: 18 -> 18, of which waited for: 9 -> 10; matrix products, arithmetic and copies ran while one was open for 2% -> 2% of each run, Pallas kernels for 10% -> 11%
where the time goes in v6:
time: 58.2 us; the launch traced here: 57.5 us
  starting transfers between devices  28.6 us (49%)
  waiting for transfers between devices  14.3 us (25%)
  Pallas kernels  12.7 us (22%)
  other arithmetic  1.01 us (2%)
  between operations  0.63 us (1%)
    ppermute x15, starting transfers between devices, move(): lax.ppermute(array, 'stn', [(number(*p), number(*target(*p))) for p in pl...  26.7 us
    ppermute x15, waiting for transfers between devices, move(): lax.ppermute(array, 'stn', [(number(*p), number(*target(*p))) for p in pl...  12.6 us
    pallas_call x3, Pallas kernels, tiles(): pl.pallas_call(functools.partial(tiles_kernel, base, counts, aliased), ou...  9.43 us
    pallas_call x1, Pallas kernels, spectra(): pl.pallas_call(spectra_kernel, out_shape=[jax.ShapeDtypeStruct((8, CH_WIN...  3.18 us
    ppermute x3, starting transfers between devices, per_device(): lax.ppermute(part, 'chan', [(c, c ^ d) for c in range(4)])  1.96 us
    ppermute x3, waiting for transfers between devices, per_device(): lax.ppermute(part, 'chan', [(c, c ^ d) for c in range(4)])  1.69 us
  transfers between devices with their start and end apart: 18, of which 10 were waited for; matrix products, arithmetic and copies ran while one was open for 2% of the time, Pallas kernels for 11%

profile of v6, /device:TPU:16, one launch (start us, length us, event | category | flops | bytes accessed | tf_op | source)
XLA Modules:
  0.0 57.5 jit_solution(2070559116861196760)
XLA Ops:
  0.0 3.2 %spectra.1 = (bf16[8,1024]{1,0:T(8,128)(2,1)}, bf16[8,1024]{1,0:T(8,128)(2,1)}, bf16[8,1024]{1,0:T(8,128)(2,1)}, bf16[8,1024]{1,0:T(8,128)(2,1)}) custom-call(bf16[2,17,128,128]{3,2,1,0:T(8,128)(2,1)} %bitcast.66, f32[16,128,128]{2,1,0:T(8,128)} %constant.179.clone.refs_1_, f32[128,128]{1,0:T(8,128)} %constant.180.clone.refs_2_, ...), custom_call_target="tpu_custom_call" | custom-call | tf_op jit(solution)/shard_map/spectra/pallas_call | solution.py:114
  3.3 1.4 %collective-permute-start.1 = (bf16[8,1024]{1,0:T(8,128)(2,1)}, bf16[8,1024]{1,0:T(8,128)(2,1)S(1)}, u32[]{:S(2)}, u32[]{:S(2)}) collective-permute-start(bf16[8,1024]{1,0:T(8,128)(2,1)} %get-tuple-element.18), channel_id=1, source_target_pairs={{0,2},{1,3},{2,0},{3,1},{4,6},{5,7},{6,4},{7,5},{8,10},{9,11},{10,... | collective-permute-start | bytes 49160 | tf_op jit(solution)/shard_map/ppermute | solution.py:249
  4.7 0.5 collective-permute-start.2
  5.2 0.7 %broadcast_select_fusion.refs_0_ = bf16[8,1024]{1,0:T(8,128)(2,1)S(1)} fusion(bf16[8,1024]{1,0:T(8,128)(2,1)} %get-tuple-element.16, pred[]{:T(512)S(6)} %lt.164), kind=kLoop, calls=%fused_computation.11 | loop fusion | flops 8192 | bytes 32769 | tf_op jit(solution)/shard_map/jit(_where)/select_n | solution.py:252
  6.2 0.1 stack.166
  6.4 1.0 %collective-permute-done.1.refs_2_ = bf16[8,1024]{1,0:T(8,128)(2,1)S(1)} collective-permute-done((bf16[8,1024]{1,0:T(8,128)(2,1)}, bf16[8,1024]{1,0:T(8,128)(2,1)S(1)}, u32[]{:S(2)}, u32[]{:S(2)}) %collective-permute-start.1) | collective-permute-done | bytes 16416 | tf_op jit(solution)/shard_map/ppermute | solution.py:249
  7.3 0.7 %collective-permute-done.2.refs_3_ = bf16[8,1024]{1,0:T(8,128)(2,1)S(1)} collective-permute-done((bf16[8,1024]{1,0:T(8,128)(2,1)}, bf16[8,1024]{1,0:T(8,128)(2,1)S(1)}, u32[]{:S(2)}, u32[]{:S(2)}) %collective-permute-start.2) | collective-permute-done | bytes 16416 | tf_op jit(solution)/shard_map/ppermute | solution.py:249
  8.1 3.3 %collective-permute-start.4 = (bf16[32,1024]{1,0:T(8,128)(2,1)S(1)}, bf16[32,1024]{1,0:T(8,128)(2,1)S(1)}, u32[]{:S(2)}, u32[]{:S(2)}) collective-permute-start(bf16[32,1024]{1,0:T(8,128)(2,1)S(1)} %group_spectra.1.refs_1_), channel_id=1, source_target_pairs={{0,64},{4,68},{8,72},{12,76},{16,80},{20,84},{24,88},{28,92},{32,9... | collective-permute-start | bytes 196616 | tf_op jit(solution)/shard_map/ppermute | solution.py:226
  11.4 1.9 %collective-permute-start.3 = (bf16[32,1024]{1,0:T(8,128)(2,1)S(1)}, bf16[32,1024]{1,0:T(8,128)(2,1)S(1)}, u32[]{:S(2)}, u32[]{:S(2)}) collective-permute-start(bf16[32,1024]{1,0:T(8,128)(2,1)S(1)} %group_spectra.1.refs_1_), channel_id=1, source_target_pairs={{0,32},{4,36},{8,40},{12,44},{16,48},{20,52},{24,56},{28,60},{32,6... | collective-permute-start | bytes 196616 | tf_op jit(solution)/shard_map/ppermute | solution.py:226
  13.4 0.2 select_reduce_fusion
  13.5 2.3 %collective-permute-start.6 = (bf16[32,1024]{1,0:T(8,128)(2,1)S(1)}, bf16[32,1024]{1,0:T(8,128)(2,1)S(1)}, u32[]{:S(2)}, u32[]{:S(2)}) collective-permute-start(bf16[32,1024]{1,0:T(8,128)(2,1)S(1)} %group_spectra.1.refs_1_), channel_id=1, source_target_pairs={{0,192},{4,196},{8,200},{12,204},{16,208},{20,212},{24,216},{28,22... | collective-permute-start | bytes 196616 | tf_op jit(solution)/shard_map/ppermute | solution.py:226
  15.8 3.3 %collective-permute-start.5 = (bf16[32,1024]{1,0:T(8,128)(2,1)S(1)}, bf16[32,1024]{1,0:T(8,128)(2,1)S(1)}, u32[]{:S(2)}, u32[]{:S(2)}) collective-permute-start(bf16[32,1024]{1,0:T(8,128)(2,1)S(1)} %group_spectra.1.refs_1_), channel_id=1, source_target_pairs={{0,96},{4,100},{8,104},{12,108},{16,112},{20,116},{24,120},{28,124... | collective-permute-start | bytes 196616 | tf_op jit(solution)/shard_map/ppermute | solution.py:226
  19.1 0.1 collective-permute-done.3
  19.3 2.8 %collective-permute-start.9 = (bf16[2,32,1024]{2,1,0:T(8,128)(2,1)S(1)}, bf16[2,32,1024]{2,1,0:T(8,128)(2,1)S(1)}, u32[]{:S(2)}, u32[]{:S(2)}) collective-permute-start(bf16[2,32,1024]{2,1,0:T(8,128)(2,1)S(1)} %pad_maximum_fusion.2), channel_id=1, source_target_pairs={{0,12},{4,8},{8,4},{12,0},{16,28},{20,24},{24,20},{28,16},{32,44},... | collective-permute-start | bytes 393224 | tf_op jit(solution)/shard_map/ppermute | solution.py:226
  22.1 0.2 collective-permute-start.8
  22.3 3.7 %collective-permute-start.7 = (bf16[32,1024]{1,0:T(8,128)(2,1)S(1)}, bf16[32,1024]{1,0:T(8,128)(2,1)S(1)}, u32[]{:S(2)}, u32[]{:S(2)}) collective-permute-start(bf16[32,1024]{1,0:T(8,128)(2,1)S(1)} %collective-permute-done.6), channel_id=1, source_target_pairs={{0,192},{4,196},{8,200},{12,204},{16,208},{20,212},{24,216},{28,22... | collective-permute-start | bytes 196616 | tf_op jit(solution)/shard_map/ppermute | solution.py:226
  26.0 1.9 %collective-permute-start.10 = (bf16[1,32,1024]{2,1,0:T(8,128)(2,1)S(1)}, bf16[1,32,1024]{2,1,0:T(8,128)(2,1)S(1)}, u32[]{:S(2)}, u32[]{:S(2)}) collective-permute-start(bf16[1,32,1024]{2,1,0:T(8,128)(2,1)S(1)} %slice.16), channel_id=1, source_target_pairs={{0,4},{4,0},{8,12},{12,8},{16,20},{20,16},{24,28},{28,24},{32,36},... | collective-permute-start | bytes 196616 | tf_op jit(solution)/shard_map/ppermute | solution.py:226
  28.0 1.8 %collective-permute-start.11 = (bf16[1,32,1024]{2,1,0:T(8,128)(2,1)S(1)}, bf16[1,32,1024]{2,1,0:T(8,128)(2,1)S(1)}, u32[]{:S(2)}, u32[]{:S(2)}) collective-permute-start(bf16[1,32,1024]{2,1,0:T(8,128)(2,1)S(1)} %slice.17), channel_id=1, source_target_pairs={{0,12},{4,8},{8,4},{12,0},{16,28},{20,24},{24,20},{28,16},{32,44},... | collective-permute-start | bytes 196616 | tf_op jit(solution)/shard_map/ppermute | solution.py:226
  29.8 0.7 %collective-permute-start.13 = (bf16[2,32,1024]{2,1,0:T(8,128)(2,1)S(1)}, bf16[2,32,1024]{2,1,0:T(8,128)(2,1)S(1)}, u32[]{:S(2)}, u32[]{:S(2)}) collective-permute-start(bf16[2,32,1024]{2,1,0:T(8,128)(2,1)S(1)} %pad_maximum_fusion.3), channel_id=1, source_target_pairs={{0,16},{4,20},{8,24},{12,28},{16,0},{20,4},{24,8},{28,12},{32,48},... | collective-permute-start | bytes 393224 | tf_op jit(solution)/shard_map/ppermute | solution.py:226
  30.6 3.0 %collective-permute-done.11 = bf16[1,32,1024]{2,1,0:T(8,128)(2,1)S(1)} collective-permute-done((bf16[1,32,1024]{2,1,0:T(8,128)(2,1)S(1)}, bf16[1,32,1024]{2,1,0:T(8,128)(2,1)S(1)}, u32[]{:S(2)}, u32[]{:S(2)}) %collective-permute-start.11) | collective-permute-done | bytes 65568 | tf_op jit(solution)/shard_map/ppermute | solution.py:226
  33.6 0.6 %collective-permute-start.12 = (bf16[8,32,1024]{2,1,0:T(8,128)(2,1)S(1)}, bf16[8,32,1024]{2,1,0:T(8,128)(2,1)S(1)}, u32[]{:S(2)}, u32[]{:S(2)}) collective-permute-start(bf16[8,32,1024]{2,1,0:T(8,128)(2,1)S(1)} %constant_dynamic-update-slice_fusion.refs_3_), channel_id=1, source_target_pairs={{0,16},{4,20},{8,24},{12,28},{16,0},{20,4},{24,8},{28,12},{32,48},... | collective-permute-start | bytes 1572872 | tf_op jit(solution)/shard_map/ppermute | solution.py:226
  34.2 3.5 %collective-permute-done.13.refs_6_ = bf16[2,32,1024]{2,1,0:T(8,128)(2,1)S(1)} collective-permute-done((bf16[2,32,1024]{2,1,0:T(8,128)(2,1)S(1)}, bf16[2,32,1024]{2,1,0:T(8,128)(2,1)S(1)}, u32[]{:S(2)}, u32[]{:S(2)}) %collective-permute-start.13) | collective-permute-done | bytes 131104 | tf_op jit(solution)/shard_map/ppermute | solution.py:226
  37.8 1.6 %collective-permute-start.15 = (bf16[4,32,1024]{2,1,0:T(8,128)(2,1)S(1)}, bf16[4,32,1024]{2,1,0:T(8,128)(2,1)S(1)}, u32[]{:S(2)}, u32[]{:S(2)}) collective-permute-start(bf16[4,32,1024]{2,1,0:T(8,128)(2,1)S(1)} %get-tuple-element.29), channel_id=1, source_target_pairs={{0,12},{4,8},{8,4},{12,0},{16,28},{20,24},{24,20},{28,16},{32,44},... | collective-permute-start | bytes 786440 | tf_op jit(solution)/shard_map/ppermute | solution.py:226
  39.4 0.7 %collective-permute-start.14 = (bf16[4,32,1024]{2,1,0:T(8,128)(2,1)S(1)}, bf16[4,32,1024]{2,1,0:T(8,128)(2,1)S(1)}, u32[]{:S(2)}, u32[]{:S(2)}) collective-permute-start(bf16[4,32,1024]{2,1,0:T(8,128)(2,1)S(1)} %get-tuple-element.30), channel_id=1, source_target_pairs={{0,4},{4,0},{8,12},{12,8},{16,20},{20,16},{24,28},{28,24},{32,36},... | collective-permute-start | bytes 786440 | tf_op jit(solution)/shard_map/ppermute | solution.py:226
  40.1 3.5 %tiles.3.refs_4_ = bf16[8,2,33,8,1024]{4,3,2,1,0:T(8,128)(2,1)} custom-call(s32[2,33]{1,0:T(2,128)S(1)} %pad_add_fusion.refs_0_, bf16[32,1024]{1,0:T(8,128)(2,1)S(1)} %group_spectra.1.refs_1_, bf16[1,32,1024]{2,1,0:T(8,128)(2,1)S(1)} %bitcast.61, bf16[8,32,1024]{2,1,0:T(8,128)(2,1)S(1)} %constant_dynamic-update-slice_fusion.refs_3_, ...), custom_call_target="tpu_custom_call" | custom-call | flops 1300000 | bytes 13 | tf_op jit(solution)/shard_map/tiles/pallas_call | solution.py:203
  43.6 3.3 %collective-permute-done.15.refs_3_ = bf16[4,32,1024]{2,1,0:T(8,128)(2,1)S(1)} collective-permute-done((bf16[4,32,1024]{2,1,0:T(8,128)(2,1)S(1)}, bf16[4,32,1024]{2,1,0:T(8,128)(2,1)S(1)}, u32[]{:S(2)}, u32[]{:S(2)}) %collective-permute-start.15) | collective-permute-done | bytes 262176 | tf_op jit(solution)/shard_map/ppermute | solution.py:226
  46.9 0.3 collective-permute-done.14.refs_2_
  47.2 1.8 %collective-permute-start.17 = (bf16[2,32,1024]{2,1,0:T(8,128)(2,1)S(1)}, bf16[2,32,1024]{2,1,0:T(8,128)(2,1)S(1)}, u32[]{:S(2)}, u32[]{:S(2)}) collective-permute-start(bf16[2,32,1024]{2,1,0:T(8,128)(2,1)S(1)} %slice.15), channel_id=1, source_target_pairs={{0,12},{4,8},{8,4},{12,0},{16,28},{20,24},{24,20},{28,16},{32,44},... | collective-permute-start | bytes 393224 | tf_op jit(solution)/shard_map/ppermute | solution.py:226
  49.0 2.7 %tiles.4.refs_5_ = bf16[8,2,33,8,1024]{4,3,2,1,0:T(8,128)(2,1)} custom-call(s32[2,33]{1,0:T(2,128)S(1)} %pad_add_fusion.refs_0_, bf16[32,1024]{1,0:T(8,128)(2,1)S(1)} %group_spectra.1.refs_1_, bf16[4,32,1024]{2,1,0:T(8,128)(2,1)S(1)} %collective-permute-done.14.refs_2_, ...), custom_call_target="tpu_custom_call", output_to_operand_aliasing={{}: (4, {})} | custom-call | flops 800000 | bytes 8 | tf_op jit(solution)/shard_map/tiles/pallas_call | solution.py:203
  51.7 1.8 %collective-permute-done.17.refs_4_ = bf16[2,32,1024]{2,1,0:T(8,128)(2,1)S(1)} collective-permute-done((bf16[2,32,1024]{2,1,0:T(8,128)(2,1)S(1)}, bf16[2,32,1024]{2,1,0:T(8,128)(2,1)S(1)}, u32[]{:S(2)}, u32[]{:S(2)}) %collective-permute-start.17) | collective-permute-done | bytes 131104 | tf_op jit(solution)/shard_map/ppermute | solution.py:226
  53.5 0.5 collective-permute-done.16.refs_3_
  54.0 3.3 %tiles.5 = bf16[8,2,33,8,1024]{4,3,2,1,0:T(8,128)(2,1)} custom-call(s32[2,33]{1,0:T(2,128)S(1)} %pad_add_fusion.refs_0_, bf16[32,1024]{1,0:T(8,128)(2,1)S(1)} %group_spectra.1.refs_1_, bf16[8,32,1024]{2,1,0:T(8,128)(2,1)S(1)} %collective-permute-done.12.refs_2_, ...), custom_call_target="tpu_custom_call", output_to_operand_aliasing={{}: (5, {})} | custom-call | flops 1200000 | bytes 12 | tf_op jit(solution)/shard_map/tiles/pallas_call | solution.py:203
  (31 shorter events, 0.4 us)
Async XLA Ops:
  0.0 5.9 %copy-start = (s32[64,64]{1,0:T(8,128)S(1)}, s32[64,64]{1,0:T(8,128)}, u32[]{:S(2)}) copy-start(s32[64,64]{1,0:T(8,128)} %param.7) | copy-start | bytes 49156
  3.2 3.1 %collective-permute-start = (bf16[8,1024]{1,0:T(8,128)(2,1)}, bf16[8,1024]{1,0:T(8,128)(2,1)S(1)}, u32[]{:S(2)}, u32[]{:S(2)}) collective-permute-start(bf16[8,1024]{1,0:T(8,128)(2,1)} %get-tuple-element.17), channel_id=1, source_target_pairs={{0,1},{1,0},{2,3},{3,2},{4,5},{5,4},{6,7},{7,6},{8,9},{9,8},{10,11... | collective-permute-start | bytes 49160 | tf_op jit(solution)/shard_map/ppermute | solution.py:249
  3.3 4.0 %collective-permute-start.1 = (bf16[8,1024]{1,0:T(8,128)(2,1)}, bf16[8,1024]{1,0:T(8,128)(2,1)S(1)}, u32[]{:S(2)}, u32[]{:S(2)}) collective-permute-start(bf16[8,1024]{1,0:T(8,128)(2,1)} %get-tuple-element.18), channel_id=1, source_target_pairs={{0,2},{1,3},{2,0},{3,1},{4,6},{5,7},{6,4},{7,5},{8,10},{9,11},{10,... | collective-permute-start | bytes 49160 | tf_op jit(solution)/shard_map/ppermute | solution.py:249
  4.7 3.4 %collective-permute-start.2 = (bf16[8,1024]{1,0:T(8,128)(2,1)}, bf16[8,1024]{1,0:T(8,128)(2,1)S(1)}, u32[]{:S(2)}, u32[]{:S(2)}) collective-permute-start(bf16[8,1024]{1,0:T(8,128)(2,1)} %get-tuple-element.19), channel_id=1, source_target_pairs={{0,3},{1,2},{2,1},{3,0},{4,7},{5,6},{6,5},{7,4},{8,11},{9,10},{10,... | collective-permute-start | bytes 49160 | tf_op jit(solution)/shard_map/ppermute | solution.py:249
  8.1 11.0 %collective-permute-start.4 = (bf16[32,1024]{1,0:T(8,128)(2,1)S(1)}, bf16[32,1024]{1,0:T(8,128)(2,1)S(1)}, u32[]{:S(2)}, u32[]{:S(2)}) collective-permute-start(bf16[32,1024]{1,0:T(8,128)(2,1)S(1)} %group_spectra.1.refs_1_), channel_id=1, source_target_pairs={{0,64},{4,68},{8,72},{12,76},{16,80},{20,84},{24,88},{28,92},{32,9... | collective-permute-start | bytes 196616 | tf_op jit(solution)/shard_map/ppermute | solution.py:226
  11.4 7.8 %collective-permute-start.3 = (bf16[32,1024]{1,0:T(8,128)(2,1)S(1)}, bf16[32,1024]{1,0:T(8,128)(2,1)S(1)}, u32[]{:S(2)}, u32[]{:S(2)}) collective-permute-start(bf16[32,1024]{1,0:T(8,128)(2,1)S(1)} %group_spectra.1.refs_1_), channel_id=1, source_target_pairs={{0,32},{4,36},{8,40},{12,44},{16,48},{20,52},{24,56},{28,60},{32,6... | collective-permute-start | bytes 196616 | tf_op jit(solution)/shard_map/ppermute | solution.py:226
  13.5 8.8 %collective-permute-start.6 = (bf16[32,1024]{1,0:T(8,128)(2,1)S(1)}, bf16[32,1024]{1,0:T(8,128)(2,1)S(1)}, u32[]{:S(2)}, u32[]{:S(2)}) collective-permute-start(bf16[32,1024]{1,0:T(8,128)(2,1)S(1)} %group_spectra.1.refs_1_), channel_id=1, source_target_pairs={{0,192},{4,196},{8,200},{12,204},{16,208},{20,212},{24,216},{28,22... | collective-permute-start | bytes 196616 | tf_op jit(solution)/shard_map/ppermute | solution.py:226
  15.8 12.1 %collective-permute-start.5 = (bf16[32,1024]{1,0:T(8,128)(2,1)S(1)}, bf16[32,1024]{1,0:T(8,128)(2,1)S(1)}, u32[]{:S(2)}, u32[]{:S(2)}) collective-permute-start(bf16[32,1024]{1,0:T(8,128)(2,1)S(1)} %group_spectra.1.refs_1_), channel_id=1, source_target_pairs={{0,96},{4,100},{8,104},{12,108},{16,112},{20,116},{24,120},{28,124... | collective-permute-start | bytes 196616 | tf_op jit(solution)/shard_map/ppermute | solution.py:226
  19.3 6.7 %collective-permute-start.9 = (bf16[2,32,1024]{2,1,0:T(8,128)(2,1)S(1)}, bf16[2,32,1024]{2,1,0:T(8,128)(2,1)S(1)}, u32[]{:S(2)}, u32[]{:S(2)}) collective-permute-start(bf16[2,32,1024]{2,1,0:T(8,128)(2,1)S(1)} %pad_maximum_fusion.2), channel_id=1, source_target_pairs={{0,12},{4,8},{8,4},{12,0},{16,28},{20,24},{24,20},{28,16},{32,44},... | collective-permute-start | bytes 393224 | tf_op jit(solution)/shard_map/ppermute | solution.py:226
  22.1 5.9 %collective-permute-start.8 = (bf16[2,32,1024]{2,1,0:T(8,128)(2,1)S(1)}, bf16[2,32,1024]{2,1,0:T(8,128)(2,1)S(1)}, u32[]{:S(2)}, u32[]{:S(2)}) collective-permute-start(bf16[2,32,1024]{2,1,0:T(8,128)(2,1)S(1)} %pad_maximum_fusion.2), channel_id=1, source_target_pairs={{0,4},{4,0},{8,12},{12,8},{16,20},{20,16},{24,28},{28,24},{32,36},... | collective-permute-start | bytes 393224 | tf_op jit(solution)/shard_map/ppermute | solution.py:226
  22.3 5.7 %collective-permute-start.7 = (bf16[32,1024]{1,0:T(8,128)(2,1)S(1)}, bf16[32,1024]{1,0:T(8,128)(2,1)S(1)}, u32[]{:S(2)}, u32[]{:S(2)}) collective-permute-start(bf16[32,1024]{1,0:T(8,128)(2,1)S(1)} %collective-permute-done.6), channel_id=1, source_target_pairs={{0,192},{4,196},{8,200},{12,204},{16,208},{20,212},{24,216},{28,22... | collective-permute-start | bytes 196616 | tf_op jit(solution)/shard_map/ppermute | solution.py:226
  26.0 4.5 %collective-permute-start.10 = (bf16[1,32,1024]{2,1,0:T(8,128)(2,1)S(1)}, bf16[1,32,1024]{2,1,0:T(8,128)(2,1)S(1)}, u32[]{:S(2)}, u32[]{:S(2)}) collective-permute-start(bf16[1,32,1024]{2,1,0:T(8,128)(2,1)S(1)} %slice.16), channel_id=1, source_target_pairs={{0,4},{4,0},{8,12},{12,8},{16,20},{20,16},{24,28},{28,24},{32,36},... | collective-permute-start | bytes 196616 | tf_op jit(solution)/shard_map/ppermute | solution.py:226
  28.0 5.6 %collective-permute-start.11 = (bf16[1,32,1024]{2,1,0:T(8,128)(2,1)S(1)}, bf16[1,32,1024]{2,1,0:T(8,128)(2,1)S(1)}, u32[]{:S(2)}, u32[]{:S(2)}) collective-permute-start(bf16[1,32,1024]{2,1,0:T(8,128)(2,1)S(1)} %slice.17), channel_id=1, source_target_pairs={{0,12},{4,8},{8,4},{12,0},{16,28},{20,24},{24,20},{28,16},{32,44},... | collective-permute-start | bytes 196616 | tf_op jit(solution)/shard_map/ppermute | solution.py:226
  29.8 7.9 %collective-permute-start.13 = (bf16[2,32,1024]{2,1,0:T(8,128)(2,1)S(1)}, bf16[2,32,1024]{2,1,0:T(8,128)(2,1)S(1)}, u32[]{:S(2)}, u32[]{:S(2)}) collective-permute-start(bf16[2,32,1024]{2,1,0:T(8,128)(2,1)S(1)} %pad_maximum_fusion.3), channel_id=1, source_target_pairs={{0,16},{4,20},{8,24},{12,28},{16,0},{20,4},{24,8},{28,12},{32,48},... | collective-permute-start | bytes 393224 | tf_op jit(solution)/shard_map/ppermute | solution.py:226
  33.6 20.4 %collective-permute-start.12 = (bf16[8,32,1024]{2,1,0:T(8,128)(2,1)S(1)}, bf16[8,32,1024]{2,1,0:T(8,128)(2,1)S(1)}, u32[]{:S(2)}, u32[]{:S(2)}) collective-permute-start(bf16[8,32,1024]{2,1,0:T(8,128)(2,1)S(1)} %constant_dynamic-update-slice_fusion.refs_3_), channel_id=1, source_target_pairs={{0,16},{4,20},{8,24},{12,28},{16,0},{20,4},{24,8},{28,12},{32,48},... | collective-permute-start | bytes 1572872 | tf_op jit(solution)/shard_map/ppermute | solution.py:226
  37.8 9.1 %collective-permute-start.15 = (bf16[4,32,1024]{2,1,0:T(8,128)(2,1)S(1)}, bf16[4,32,1024]{2,1,0:T(8,128)(2,1)S(1)}, u32[]{:S(2)}, u32[]{:S(2)}) collective-permute-start(bf16[4,32,1024]{2,1,0:T(8,128)(2,1)S(1)} %get-tuple-element.29), channel_id=1, source_target_pairs={{0,12},{4,8},{8,4},{12,0},{16,28},{20,24},{24,20},{28,16},{32,44},... | collective-permute-start | bytes 786440 | tf_op jit(solution)/shard_map/ppermute | solution.py:226
  39.4 7.8 %collective-permute-start.14 = (bf16[4,32,1024]{2,1,0:T(8,128)(2,1)S(1)}, bf16[4,32,1024]{2,1,0:T(8,128)(2,1)S(1)}, u32[]{:S(2)}, u32[]{:S(2)}) collective-permute-start(bf16[4,32,1024]{2,1,0:T(8,128)(2,1)S(1)} %get-tuple-element.30), channel_id=1, source_target_pairs={{0,4},{4,0},{8,12},{12,8},{16,20},{20,16},{24,28},{28,24},{32,36},... | collective-permute-start | bytes 786440 | tf_op jit(solution)/shard_map/ppermute | solution.py:226
  47.2 6.3 %collective-permute-start.17 = (bf16[2,32,1024]{2,1,0:T(8,128)(2,1)S(1)}, bf16[2,32,1024]{2,1,0:T(8,128)(2,1)S(1)}, u32[]{:S(2)}, u32[]{:S(2)}) collective-permute-start(bf16[2,32,1024]{2,1,0:T(8,128)(2,1)S(1)} %slice.15), channel_id=1, source_target_pairs={{0,12},{4,8},{8,4},{12,0},{16,28},{20,24},{24,20},{28,16},{32,44},... | collective-permute-start | bytes 393224 | tf_op jit(solution)/shard_map/ppermute | solution.py:226
  49.0 5.0 %collective-permute-start.16 = (bf16[2,32,1024]{2,1,0:T(8,128)(2,1)S(1)}, bf16[2,32,1024]{2,1,0:T(8,128)(2,1)S(1)}, u32[]{:S(2)}, u32[]{:S(2)}) collective-permute-start(bf16[2,32,1024]{2,1,0:T(8,128)(2,1)S(1)} %slice.14), channel_id=1, source_target_pairs={{0,4},{4,0},{8,12},{12,8},{16,20},{20,16},{24,28},{28,24},{32,36},... | collective-permute-start | bytes 393224 | tf_op jit(solution)/shard_map/ppermute | solution.py:226

commit v7 on v6

--- a/solution.py
+++ b/solution.py
@@ -160,8 +160,10 @@
     out_ref, wide_ref, tile_ref, sems = refs[2 + len(counts) + (1 if aliased else 0) :]
     own = own_ref[...].astype(jnp.float32) * 0.5
     for t in range(4):
-        for i in range(8):
-            wide_ref[i, t] = jnp.broadcast_to(own[t * 8 + i : t * 8 + i + 1], (8, CH_WIN))
+        for pair in range(4):
+            at = t * 8 + pair * 2
+            two = [jnp.broadcast_to(own[n : n + 1], (8, CH_WIN)) for n in (at, at + 1)]
+            wide_ref[pair, t] = jnp.concatenate(two, axis=0).astype(jnp.bfloat16)
 
     def copy_of(n):
         return pltpu.make_async_copy(tile_ref.at[n], out_ref.at[:, :, slots_ref[0, base + n]], sems.at[n])
@@ -178,11 +180,16 @@
             def _(step):
                 lanes = pl.ds(pl.multiple_of(step * 128, 128), 128)
                 other = block_ref[index, :, lanes].astype(jnp.float32) * keep
-                r0, r1, i0, i1 = (other[t * 8 : t * 8 + 8] for t in range(4))
-                for i in range(8):
-                    a0, a1, b0, b1 = (wide_ref[i, t, :, lanes] for t in range(4))
-                    tile_ref[n, i, 0, :, lanes] = ((a0 * r0 + a1 * r1) + (b0 * i0 + b1 * i1)).astype(jnp.bfloat16)
-                    tile_ref[n, i, 1, :, lanes] = ((b0 * r0 + b1 * r1) - (a0 * i0 + a1 * i1)).astype(jnp.bfloat16)
+                twice = (other[t * 8 : t * 8 + 8] for t in range(4))
+                r0, r1, i0, i1 = (jnp.concatenate([o, o], axis=0).astype(jnp.bfloat16) for o in twice)
+                for pair in range(4):
+                    a0, a1, b0, b1 = (wide_ref[pair, t, :, lanes] for t in range(4))
+                    real = (a0 * r0 + a1 * r1) + (b0 * i0 + b1 * i1)
+                    imag = (b0 * r0 + b1 * r1) - (a0 * i0 + a1 * i1)
+                    for half in range(2):
+                        rows = slice(half * 8, half * 8 + 8)
+                        tile_ref[n, pair * 2 + half, 0, :, lanes] = real[rows]
+                        tile_ref[n, pair * 2 + half, 1, :, lanes] = imag[rows]
 
             copy_of(n).start()
 
@@ -207,7 +214,7 @@
         out_specs=pl.BlockSpec(memory_space=pl.ANY),
         input_output_aliases={len(operands) - 1: 0} if aliased else {},
         scratch_shapes=[
-            pltpu.VMEM((8, 4, 8, CH_WIN), jnp.float32),
+            pltpu.VMEM((4, 4, 16, CH_WIN), jnp.bfloat16),
             pltpu.VMEM((n, 8, 2, 8, CH_WIN), jnp.bfloat16),
             pltpu.SemaphoreType.DMA((n,)),
         ],

time: 58.2 us -> 58 us (level)
  Pallas kernels: 12.7 us -> 12.1 us
  transfers between devices with their start and end apart: 18 -> 18, of which waited for: 10 -> 10; matrix products, arithmetic and copies ran while one was open for 2% -> 2% of each run, Pallas kernels for 11% -> 10%
where the time goes in v7:
time: 58 us; the launch traced here: 57.3 us
  starting transfers between devices  28.6 us (49%)
  waiting for transfers between devices  14.7 us (25%)
  Pallas kernels  12.1 us (21%)
  other arithmetic  1.01 us (2%)
  between operations  0.63 us (1%)
    ppermute x15, starting transfers between devices, move(): lax.ppermute(array, 'stn', [(number(*p), number(*target(*p))) for p in pl...  26.7 us
    ppermute x15, waiting for transfers between devices, move(): lax.ppermute(array, 'stn', [(number(*p), number(*target(*p))) for p in pl...  13 us
    pallas_call x3, Pallas kernels, tiles(): pl.pallas_call(functools.partial(tiles_kernel, base, counts, aliased), ou...  8.88 us
    pallas_call x1, Pallas kernels, spectra(): pl.pallas_call(spectra_kernel, out_shape=[jax.ShapeDtypeStruct((8, CH_WIN...  3.18 us
    ppermute x3, starting transfers between devices, per_device(): lax.ppermute(part, 'chan', [(c, c ^ d) for c in range(4)])  1.96 us
    ppermute x3, waiting for transfers between devices, per_device(): lax.ppermute(part, 'chan', [(c, c ^ d) for c in range(4)])  1.69 us
  transfers between devices with their start and end apart: 18, of which 10 were waited for; matrix products, arithmetic and copies ran while one was open for 2% of the time, Pallas kernels for 10%

profile of v7, /device:TPU:16, one launch (start us, length us, event | category | flops | bytes accessed | tf_op | source)
XLA Modules:
  0.0 57.3 jit_solution(3144200616341350361)
XLA Ops:
  0.0 3.2 %spectra.1 = (bf16[8,1024]{1,0:T(8,128)(2,1)}, bf16[8,1024]{1,0:T(8,128)(2,1)}, bf16[8,1024]{1,0:T(8,128)(2,1)}, bf16[8,1024]{1,0:T(8,128)(2,1)}) custom-call(bf16[2,17,128,128]{3,2,1,0:T(8,128)(2,1)} %bitcast.66, f32[16,128,128]{2,1,0:T(8,128)} %constant.179.clone.refs_1_, f32[128,128]{1,0:T(8,128)} %constant.180.clone.refs_2_, ...), custom_call_target="tpu_custom_call" | custom-call | tf_op jit(solution)/shard_map/spectra/pallas_call | solution.py:114
  3.3 1.4 %collective-permute-start.1 = (bf16[8,1024]{1,0:T(8,128)(2,1)}, bf16[8,1024]{1,0:T(8,128)(2,1)S(1)}, u32[]{:S(2)}, u32[]{:S(2)}) collective-permute-start(bf16[8,1024]{1,0:T(8,128)(2,1)} %get-tuple-element.18), channel_id=1, source_target_pairs={{0,2},{1,3},{2,0},{3,1},{4,6},{5,7},{6,4},{7,5},{8,10},{9,11},{10,... | collective-permute-start | bytes 49160 | tf_op jit(solution)/shard_map/ppermute | solution.py:256
  4.7 0.5 collective-permute-start.2
  5.2 0.7 %broadcast_select_fusion.refs_0_ = bf16[8,1024]{1,0:T(8,128)(2,1)S(1)} fusion(bf16[8,1024]{1,0:T(8,128)(2,1)} %get-tuple-element.16, pred[]{:T(512)S(6)} %lt.164), kind=kLoop, calls=%fused_computation.11 | loop fusion | flops 8192 | bytes 32769 | tf_op jit(solution)/shard_map/jit(_where)/select_n | solution.py:259
  6.2 0.1 stack.166
  6.4 1.0 %collective-permute-done.1.refs_2_ = bf16[8,1024]{1,0:T(8,128)(2,1)S(1)} collective-permute-done((bf16[8,1024]{1,0:T(8,128)(2,1)}, bf16[8,1024]{1,0:T(8,128)(2,1)S(1)}, u32[]{:S(2)}, u32[]{:S(2)}) %collective-permute-start.1) | collective-permute-done | bytes 16416 | tf_op jit(solution)/shard_map/ppermute | solution.py:256
  7.3 0.7 %collective-permute-done.2.refs_3_ = bf16[8,1024]{1,0:T(8,128)(2,1)S(1)} collective-permute-done((bf16[8,1024]{1,0:T(8,128)(2,1)}, bf16[8,1024]{1,0:T(8,128)(2,1)S(1)}, u32[]{:S(2)}, u32[]{:S(2)}) %collective-permute-start.2) | collective-permute-done | bytes 16416 | tf_op jit(solution)/shard_map/ppermute | solution.py:256
  8.1 3.3 %collective-permute-start.4 = (bf16[32,1024]{1,0:T(8,128)(2,1)S(1)}, bf16[32,1024]{1,0:T(8,128)(2,1)S(1)}, u32[]{:S(2)}, u32[]{:S(2)}) collective-permute-start(bf16[32,1024]{1,0:T(8,128)(2,1)S(1)} %group_spectra.1.refs_1_), channel_id=1, source_target_pairs={{0,64},{4,68},{8,72},{12,76},{16,80},{20,84},{24,88},{28,92},{32,9... | collective-permute-start | bytes 196616 | tf_op jit(solution)/shard_map/ppermute | solution.py:233
  11.4 1.9 %collective-permute-start.3 = (bf16[32,1024]{1,0:T(8,128)(2,1)S(1)}, bf16[32,1024]{1,0:T(8,128)(2,1)S(1)}, u32[]{:S(2)}, u32[]{:S(2)}) collective-permute-start(bf16[32,1024]{1,0:T(8,128)(2,1)S(1)} %group_spectra.1.refs_1_), channel_id=1, source_target_pairs={{0,32},{4,36},{8,40},{12,44},{16,48},{20,52},{24,56},{28,60},{32,6... | collective-permute-start | bytes 196616 | tf_op jit(solution)/shard_map/ppermute | solution.py:233
  13.4 0.2 select_reduce_fusion
  13.5 2.3 %collective-permute-start.6 = (bf16[32,1024]{1,0:T(8,128)(2,1)S(1)}, bf16[32,1024]{1,0:T(8,128)(2,1)S(1)}, u32[]{:S(2)}, u32[]{:S(2)}) collective-permute-start(bf16[32,1024]{1,0:T(8,128)(2,1)S(1)} %group_spectra.1.refs_1_), channel_id=1, source_target_pairs={{0,192},{4,196},{8,200},{12,204},{16,208},{20,212},{24,216},{28,22... | collective-permute-start | bytes 196616 | tf_op jit(solution)/shard_map/ppermute | solution.py:233
  15.8 3.3 %collective-permute-start.5 = (bf16[32,1024]{1,0:T(8,128)(2,1)S(1)}, bf16[32,1024]{1,0:T(8,128)(2,1)S(1)}, u32[]{:S(2)}, u32[]{:S(2)}) collective-permute-start(bf16[32,1024]{1,0:T(8,128)(2,1)S(1)} %group_spectra.1.refs_1_), channel_id=1, source_target_pairs={{0,96},{4,100},{8,104},{12,108},{16,112},{20,116},{24,120},{28,124... | collective-permute-start | bytes 196616 | tf_op jit(solution)/shard_map/ppermute | solution.py:233
  19.1 0.1 collective-permute-done.3
  19.3 2.8 %collective-permute-start.9 = (bf16[2,32,1024]{2,1,0:T(8,128)(2,1)S(1)}, bf16[2,32,1024]{2,1,0:T(8,128)(2,1)S(1)}, u32[]{:S(2)}, u32[]{:S(2)}) collective-permute-start(bf16[2,32,1024]{2,1,0:T(8,128)(2,1)S(1)} %pad_maximum_fusion.2), channel_id=1, source_target_pairs={{0,12},{4,8},{8,4},{12,0},{16,28},{20,24},{24,20},{28,16},{32,44},... | collective-permute-start | bytes 393224 | tf_op jit(solution)/shard_map/ppermute | solution.py:233
  22.1 0.2 collective-permute-start.8
  22.3 3.7 %collective-permute-start.7 = (bf16[32,1024]{1,0:T(8,128)(2,1)S(1)}, bf16[32,1024]{1,0:T(8,128)(2,1)S(1)}, u32[]{:S(2)}, u32[]{:S(2)}) collective-permute-start(bf16[32,1024]{1,0:T(8,128)(2,1)S(1)} %collective-permute-done.6), channel_id=1, source_target_pairs={{0,192},{4,196},{8,200},{12,204},{16,208},{20,212},{24,216},{28,22... | collective-permute-start | bytes 196616 | tf_op jit(solution)/shard_map/ppermute | solution.py:233
  26.0 1.9 %collective-permute-start.10 = (bf16[1,32,1024]{2,1,0:T(8,128)(2,1)S(1)}, bf16[1,32,1024]{2,1,0:T(8,128)(2,1)S(1)}, u32[]{:S(2)}, u32[]{:S(2)}) collective-permute-start(bf16[1,32,1024]{2,1,0:T(8,128)(2,1)S(1)} %slice.16), channel_id=1, source_target_pairs={{0,4},{4,0},{8,12},{12,8},{16,20},{20,16},{24,28},{28,24},{32,36},... | collective-permute-start | bytes 196616 | tf_op jit(solution)/shard_map/ppermute | solution.py:233
  28.0 1.8 %collective-permute-start.11 = (bf16[1,32,1024]{2,1,0:T(8,128)(2,1)S(1)}, bf16[1,32,1024]{2,1,0:T(8,128)(2,1)S(1)}, u32[]{:S(2)}, u32[]{:S(2)}) collective-permute-start(bf16[1,32,1024]{2,1,0:T(8,128)(2,1)S(1)} %slice.17), channel_id=1, source_target_pairs={{0,12},{4,8},{8,4},{12,0},{16,28},{20,24},{24,20},{28,16},{32,44},... | collective-permute-start | bytes 196616 | tf_op jit(solution)/shard_map/ppermute | solution.py:233
  29.8 0.7 %collective-permute-start.13 = (bf16[2,32,1024]{2,1,0:T(8,128)(2,1)S(1)}, bf16[2,32,1024]{2,1,0:T(8,128)(2,1)S(1)}, u32[]{:S(2)}, u32[]{:S(2)}) collective-permute-start(bf16[2,32,1024]{2,1,0:T(8,128)(2,1)S(1)} %pad_maximum_fusion.3), channel_id=1, source_target_pairs={{0,16},{4,20},{8,24},{12,28},{16,0},{20,4},{24,8},{28,12},{32,48},... | collective-permute-start | bytes 393224 | tf_op jit(solution)/shard_map/ppermute | solution.py:233
  30.6 3.0 %collective-permute-done.11 = bf16[1,32,1024]{2,1,0:T(8,128)(2,1)S(1)} collective-permute-done((bf16[1,32,1024]{2,1,0:T(8,128)(2,1)S(1)}, bf16[1,32,1024]{2,1,0:T(8,128)(2,1)S(1)}, u32[]{:S(2)}, u32[]{:S(2)}) %collective-permute-start.11) | collective-permute-done | bytes 65568 | tf_op jit(solution)/shard_map/ppermute | solution.py:233
  33.6 0.6 %collective-permute-start.12 = (bf16[8,32,1024]{2,1,0:T(8,128)(2,1)S(1)}, bf16[8,32,1024]{2,1,0:T(8,128)(2,1)S(1)}, u32[]{:S(2)}, u32[]{:S(2)}) collective-permute-start(bf16[8,32,1024]{2,1,0:T(8,128)(2,1)S(1)} %constant_dynamic-update-slice_fusion.refs_3_), channel_id=1, source_target_pairs={{0,16},{4,20},{8,24},{12,28},{16,0},{20,4},{24,8},{28,12},{32,48},... | collective-permute-start | bytes 1572872 | tf_op jit(solution)/shard_map/ppermute | solution.py:233
  34.2 3.5 %collective-permute-done.13.refs_6_ = bf16[2,32,1024]{2,1,0:T(8,128)(2,1)S(1)} collective-permute-done((bf16[2,32,1024]{2,1,0:T(8,128)(2,1)S(1)}, bf16[2,32,1024]{2,1,0:T(8,128)(2,1)S(1)}, u32[]{:S(2)}, u32[]{:S(2)}) %collective-permute-start.13) | collective-permute-done | bytes 131104 | tf_op jit(solution)/shard_map/ppermute | solution.py:233
  37.8 1.6 %collective-permute-start.15 = (bf16[4,32,1024]{2,1,0:T(8,128)(2,1)S(1)}, bf16[4,32,1024]{2,1,0:T(8,128)(2,1)S(1)}, u32[]{:S(2)}, u32[]{:S(2)}) collective-permute-start(bf16[4,32,1024]{2,1,0:T(8,128)(2,1)S(1)} %get-tuple-element.29), channel_id=1, source_target_pairs={{0,12},{4,8},{8,4},{12,0},{16,28},{20,24},{24,20},{28,16},{32,44},... | collective-permute-start | bytes 786440 | tf_op jit(solution)/shard_map/ppermute | solution.py:233
  39.4 0.7 %collective-permute-start.14 = (bf16[4,32,1024]{2,1,0:T(8,128)(2,1)S(1)}, bf16[4,32,1024]{2,1,0:T(8,128)(2,1)S(1)}, u32[]{:S(2)}, u32[]{:S(2)}) collective-permute-start(bf16[4,32,1024]{2,1,0:T(8,128)(2,1)S(1)} %get-tuple-element.30), channel_id=1, source_target_pairs={{0,4},{4,0},{8,12},{12,8},{16,20},{20,16},{24,28},{28,24},{32,36},... | collective-permute-start | bytes 786440 | tf_op jit(solution)/shard_map/ppermute | solution.py:233
  40.1 3.2 %tiles.3.refs_4_ = bf16[8,2,33,8,1024]{4,3,2,1,0:T(8,128)(2,1)} custom-call(s32[2,33]{1,0:T(2,128)S(1)} %pad_add_fusion.refs_0_, bf16[32,1024]{1,0:T(8,128)(2,1)S(1)} %group_spectra.1.refs_1_, bf16[1,32,1024]{2,1,0:T(8,128)(2,1)S(1)} %bitcast.61, bf16[8,32,1024]{2,1,0:T(8,128)(2,1)S(1)} %constant_dynamic-update-slice_fusion.refs_3_, ...), custom_call_target="tpu_custom_call" | custom-call | flops 1300000 | bytes 13 | tf_op jit(solution)/shard_map/tiles/pallas_call | solution.py:210
  43.4 3.5 %collective-permute-done.15.refs_3_ = bf16[4,32,1024]{2,1,0:T(8,128)(2,1)S(1)} collective-permute-done((bf16[4,32,1024]{2,1,0:T(8,128)(2,1)S(1)}, bf16[4,32,1024]{2,1,0:T(8,128)(2,1)S(1)}, u32[]{:S(2)}, u32[]{:S(2)}) %collective-permute-start.15) | collective-permute-done | bytes 262176 | tf_op jit(solution)/shard_map/ppermute | solution.py:233
  46.9 0.3 collective-permute-done.14.refs_2_
  47.2 1.8 %collective-permute-start.17 = (bf16[2,32,1024]{2,1,0:T(8,128)(2,1)S(1)}, bf16[2,32,1024]{2,1,0:T(8,128)(2,1)S(1)}, u32[]{:S(2)}, u32[]{:S(2)}) collective-permute-start(bf16[2,32,1024]{2,1,0:T(8,128)(2,1)S(1)} %slice.15), channel_id=1, source_target_pairs={{0,12},{4,8},{8,4},{12,0},{16,28},{20,24},{24,20},{28,16},{32,44},... | collective-permute-start | bytes 393224 | tf_op jit(solution)/shard_map/ppermute | solution.py:233
  49.0 2.5 %tiles.4.refs_5_ = bf16[8,2,33,8,1024]{4,3,2,1,0:T(8,128)(2,1)} custom-call(s32[2,33]{1,0:T(2,128)S(1)} %pad_add_fusion.refs_0_, bf16[32,1024]{1,0:T(8,128)(2,1)S(1)} %group_spectra.1.refs_1_, bf16[4,32,1024]{2,1,0:T(8,128)(2,1)S(1)} %collective-permute-done.14.refs_2_, ...), custom_call_target="tpu_custom_call", output_to_operand_aliasing={{}: (4, {})} | custom-call | flops 800000 | bytes 8 | tf_op jit(solution)/shard_map/tiles/pallas_call | solution.py:210
  51.5 2.0 %collective-permute-done.17.refs_4_ = bf16[2,32,1024]{2,1,0:T(8,128)(2,1)S(1)} collective-permute-done((bf16[2,32,1024]{2,1,0:T(8,128)(2,1)S(1)}, bf16[2,32,1024]{2,1,0:T(8,128)(2,1)S(1)}, u32[]{:S(2)}, u32[]{:S(2)}) %collective-permute-start.17) | collective-permute-done | bytes 131104 | tf_op jit(solution)/shard_map/ppermute | solution.py:233
  53.5 0.5 collective-permute-done.16.refs_3_
  54.0 3.1 %tiles.5 = bf16[8,2,33,8,1024]{4,3,2,1,0:T(8,128)(2,1)} custom-call(s32[2,33]{1,0:T(2,128)S(1)} %pad_add_fusion.refs_0_, bf16[32,1024]{1,0:T(8,128)(2,1)S(1)} %group_spectra.1.refs_1_, bf16[8,32,1024]{2,1,0:T(8,128)(2,1)S(1)} %collective-permute-done.12.refs_2_, ...), custom_call_target="tpu_custom_call", output_to_operand_aliasing={{}: (5, {})} | custom-call | flops 1200000 | bytes 12 | tf_op jit(solution)/shard_map/tiles/pallas_call | solution.py:210
  (31 shorter events, 0.4 us)
Async XLA Ops:
  0.0 5.9 %copy-start = (s32[64,64]{1,0:T(8,128)S(1)}, s32[64,64]{1,0:T(8,128)}, u32[]{:S(2)}) copy-start(s32[64,64]{1,0:T(8,128)} %param.7) | copy-start | bytes 49156
  3.2 3.1 %collective-permute-start = (bf16[8,1024]{1,0:T(8,128)(2,1)}, bf16[8,1024]{1,0:T(8,128)(2,1)S(1)}, u32[]{:S(2)}, u32[]{:S(2)}) collective-permute-start(bf16[8,1024]{1,0:T(8,128)(2,1)} %get-tuple-element.17), channel_id=1, source_target_pairs={{0,1},{1,0},{2,3},{3,2},{4,5},{5,4},{6,7},{7,6},{8,9},{9,8},{10,11... | collective-permute-start | bytes 49160 | tf_op jit(solution)/shard_map/ppermute | solution.py:256
  3.3 4.0 %collective-permute-start.1 = (bf16[8,1024]{1,0:T(8,128)(2,1)}, bf16[8,1024]{1,0:T(8,128)(2,1)S(1)}, u32[]{:S(2)}, u32[]{:S(2)}) collective-permute-start(bf16[8,1024]{1,0:T(8,128)(2,1)} %get-tuple-element.18), channel_id=1, source_target_pairs={{0,2},{1,3},{2,0},{3,1},{4,6},{5,7},{6,4},{7,5},{8,10},{9,11},{10,... | collective-permute-start | bytes 49160 | tf_op jit(solution)/shard_map/ppermute | solution.py:256
  4.7 3.4 %collective-permute-start.2 = (bf16[8,1024]{1,0:T(8,128)(2,1)}, bf16[8,1024]{1,0:T(8,128)(2,1)S(1)}, u32[]{:S(2)}, u32[]{:S(2)}) collective-permute-start(bf16[8,1024]{1,0:T(8,128)(2,1)} %get-tuple-element.19), channel_id=1, source_target_pairs={{0,3},{1,2},{2,1},{3,0},{4,7},{5,6},{6,5},{7,4},{8,11},{9,10},{10,... | collective-permute-start | bytes 49160 | tf_op jit(solution)/shard_map/ppermute | solution.py:256
  8.1 11.0 %collective-permute-start.4 = (bf16[32,1024]{1,0:T(8,128)(2,1)S(1)}, bf16[32,1024]{1,0:T(8,128)(2,1)S(1)}, u32[]{:S(2)}, u32[]{:S(2)}) collective-permute-start(bf16[32,1024]{1,0:T(8,128)(2,1)S(1)} %group_spectra.1.refs_1_), channel_id=1, source_target_pairs={{0,64},{4,68},{8,72},{12,76},{16,80},{20,84},{24,88},{28,92},{32,9... | collective-permute-start | bytes 196616 | tf_op jit(solution)/shard_map/ppermute | solution.py:233
  11.4 7.8 %collective-permute-start.3 = (bf16[32,1024]{1,0:T(8,128)(2,1)S(1)}, bf16[32,1024]{1,0:T(8,128)(2,1)S(1)}, u32[]{:S(2)}, u32[]{:S(2)}) collective-permute-start(bf16[32,1024]{1,0:T(8,128)(2,1)S(1)} %group_spectra.1.refs_1_), channel_id=1, source_target_pairs={{0,32},{4,36},{8,40},{12,44},{16,48},{20,52},{24,56},{28,60},{32,6... | collective-permute-start | bytes 196616 | tf_op jit(solution)/shard_map/ppermute | solution.py:233
  13.5 8.8 %collective-permute-start.6 = (bf16[32,1024]{1,0:T(8,128)(2,1)S(1)}, bf16[32,1024]{1,0:T(8,128)(2,1)S(1)}, u32[]{:S(2)}, u32[]{:S(2)}) collective-permute-start(bf16[32,1024]{1,0:T(8,128)(2,1)S(1)} %group_spectra.1.refs_1_), channel_id=1, source_target_pairs={{0,192},{4,196},{8,200},{12,204},{16,208},{20,212},{24,216},{28,22... | collective-permute-start | bytes 196616 | tf_op jit(solution)/shard_map/ppermute | solution.py:233
  15.8 12.1 %collective-permute-start.5 = (bf16[32,1024]{1,0:T(8,128)(2,1)S(1)}, bf16[32,1024]{1,0:T(8,128)(2,1)S(1)}, u32[]{:S(2)}, u32[]{:S(2)}) collective-permute-start(bf16[32,1024]{1,0:T(8,128)(2,1)S(1)} %group_spectra.1.refs_1_), channel_id=1, source_target_pairs={{0,96},{4,100},{8,104},{12,108},{16,112},{20,116},{24,120},{28,124... | collective-permute-start | bytes 196616 | tf_op jit(solution)/shard_map/ppermute | solution.py:233
  19.3 6.7 %collective-permute-start.9 = (bf16[2,32,1024]{2,1,0:T(8,128)(2,1)S(1)}, bf16[2,32,1024]{2,1,0:T(8,128)(2,1)S(1)}, u32[]{:S(2)}, u32[]{:S(2)}) collective-permute-start(bf16[2,32,1024]{2,1,0:T(8,128)(2,1)S(1)} %pad_maximum_fusion.2), channel_id=1, source_target_pairs={{0,12},{4,8},{8,4},{12,0},{16,28},{20,24},{24,20},{28,16},{32,44},... | collective-permute-start | bytes 393224 | tf_op jit(solution)/shard_map/ppermute | solution.py:233
  22.1 5.9 %collective-permute-start.8 = (bf16[2,32,1024]{2,1,0:T(8,128)(2,1)S(1)}, bf16[2,32,1024]{2,1,0:T(8,128)(2,1)S(1)}, u32[]{:S(2)}, u32[]{:S(2)}) collective-permute-start(bf16[2,32,1024]{2,1,0:T(8,128)(2,1)S(1)} %pad_maximum_fusion.2), channel_id=1, source_target_pairs={{0,4},{4,0},{8,12},{12,8},{16,20},{20,16},{24,28},{28,24},{32,36},... | collective-permute-start | bytes 393224 | tf_op jit(solution)/shard_map/ppermute | solution.py:233
  22.3 5.7 %collective-permute-start.7 = (bf16[32,1024]{1,0:T(8,128)(2,1)S(1)}, bf16[32,1024]{1,0:T(8,128)(2,1)S(1)}, u32[]{:S(2)}, u32[]{:S(2)}) collective-permute-start(bf16[32,1024]{1,0:T(8,128)(2,1)S(1)} %collective-permute-done.6), channel_id=1, source_target_pairs={{0,192},{4,196},{8,200},{12,204},{16,208},{20,212},{24,216},{28,22... | collective-permute-start | bytes 196616 | tf_op jit(solution)/shard_map/ppermute | solution.py:233
  26.0 4.5 %collective-permute-start.10 = (bf16[1,32,1024]{2,1,0:T(8,128)(2,1)S(1)}, bf16[1,32,1024]{2,1,0:T(8,128)(2,1)S(1)}, u32[]{:S(2)}, u32[]{:S(2)}) collective-permute-start(bf16[1,32,1024]{2,1,0:T(8,128)(2,1)S(1)} %slice.16), channel_id=1, source_target_pairs={{0,4},{4,0},{8,12},{12,8},{16,20},{20,16},{24,28},{28,24},{32,36},... | collective-permute-start | bytes 196616 | tf_op jit(solution)/shard_map/ppermute | solution.py:233
  28.0 5.6 %collective-permute-start.11 = (bf16[1,32,1024]{2,1,0:T(8,128)(2,1)S(1)}, bf16[1,32,1024]{2,1,0:T(8,128)(2,1)S(1)}, u32[]{:S(2)}, u32[]{:S(2)}) collective-permute-start(bf16[1,32,1024]{2,1,0:T(8,128)(2,1)S(1)} %slice.17), channel_id=1, source_target_pairs={{0,12},{4,8},{8,4},{12,0},{16,28},{20,24},{24,20},{28,16},{32,44},... | collective-permute-start | bytes 196616 | tf_op jit(solution)/shard_map/ppermute | solution.py:233
  29.8 7.9 %collective-permute-start.13 = (bf16[2,32,1024]{2,1,0:T(8,128)(2,1)S(1)}, bf16[2,32,1024]{2,1,0:T(8,128)(2,1)S(1)}, u32[]{:S(2)}, u32[]{:S(2)}) collective-permute-start(bf16[2,32,1024]{2,1,0:T(8,128)(2,1)S(1)} %pad_maximum_fusion.3), channel_id=1, source_target_pairs={{0,16},{4,20},{8,24},{12,28},{16,0},{20,4},{24,8},{28,12},{32,48},... | collective-permute-start | bytes 393224 | tf_op jit(solution)/shard_map/ppermute | solution.py:233
  33.6 20.4 %collective-permute-start.12 = (bf16[8,32,1024]{2,1,0:T(8,128)(2,1)S(1)}, bf16[8,32,1024]{2,1,0:T(8,128)(2,1)S(1)}, u32[]{:S(2)}, u32[]{:S(2)}) collective-permute-start(bf16[8,32,1024]{2,1,0:T(8,128)(2,1)S(1)} %constant_dynamic-update-slice_fusion.refs_3_), channel_id=1, source_target_pairs={{0,16},{4,20},{8,24},{12,28},{16,0},{20,4},{24,8},{28,12},{32,48},... | collective-permute-start | bytes 1572872 | tf_op jit(solution)/shard_map/ppermute | solution.py:233
  37.8 9.1 %collective-permute-start.15 = (bf16[4,32,1024]{2,1,0:T(8,128)(2,1)S(1)}, bf16[4,32,1024]{2,1,0:T(8,128)(2,1)S(1)}, u32[]{:S(2)}, u32[]{:S(2)}) collective-permute-start(bf16[4,32,1024]{2,1,0:T(8,128)(2,1)S(1)} %get-tuple-element.29), channel_id=1, source_target_pairs={{0,12},{4,8},{8,4},{12,0},{16,28},{20,24},{24,20},{28,16},{32,44},... | collective-permute-start | bytes 786440 | tf_op jit(solution)/shard_map/ppermute | solution.py:233
  39.4 7.8 %collective-permute-start.14 = (bf16[4,32,1024]{2,1,0:T(8,128)(2,1)S(1)}, bf16[4,32,1024]{2,1,0:T(8,128)(2,1)S(1)}, u32[]{:S(2)}, u32[]{:S(2)}) collective-permute-start(bf16[4,32,1024]{2,1,0:T(8,128)(2,1)S(1)} %get-tuple-element.30), channel_id=1, source_target_pairs={{0,4},{4,0},{8,12},{12,8},{16,20},{20,16},{24,28},{28,24},{32,36},... | collective-permute-start | bytes 786440 | tf_op jit(solution)/shard_map/ppermute | solution.py:233
  47.2 6.3 %collective-permute-start.17 = (bf16[2,32,1024]{2,1,0:T(8,128)(2,1)S(1)}, bf16[2,32,1024]{2,1,0:T(8,128)(2,1)S(1)}, u32[]{:S(2)}, u32[]{:S(2)}) collective-permute-start(bf16[2,32,1024]{2,1,0:T(8,128)(2,1)S(1)} %slice.15), channel_id=1, source_target_pairs={{0,12},{4,8},{8,4},{12,0},{16,28},{20,24},{24,20},{28,16},{32,44},... | collective-permute-start | bytes 393224 | tf_op jit(solution)/shard_map/ppermute | solution.py:233
  49.0 5.0 %collective-permute-start.16 = (bf16[2,32,1024]{2,1,0:T(8,128)(2,1)S(1)}, bf16[2,32,1024]{2,1,0:T(8,128)(2,1)S(1)}, u32[]{:S(2)}, u32[]{:S(2)}) collective-permute-start(bf16[2,32,1024]{2,1,0:T(8,128)(2,1)S(1)} %slice.14), channel_id=1, source_target_pairs={{0,4},{4,0},{8,12},{12,8},{16,20},{20,16},{24,28},{28,24},{32,36},... | collective-permute-start | bytes 393224 | tf_op jit(solution)/shard_map/ppermute | solution.py:233
